TPU v7x, 32 devices: a whole 2x2x4 slice. The times are simulated.
32 devices in a mesh: ctx: 8 (over z, x), tp: 4 (over y, core).
Axes of the slice: x: 2, y: 2, z: 4, core: 2. Of those that a mesh axis runs over, the one named last changes fastest.
Arguments:
- q_pre: bfloat16 [2, 512, 4096], P(None, 'ctx', 'tp'), may hold values from -8 to 8
- k_pre: bfloat16 [2, 512, 512], P(None, 'ctx', 'tp'), may hold values from -8 to 8
- value_before_filter: bfloat16 [2, 512, 512], P(None, 'ctx', 'tp'), may hold values from -8 to 8
- d_out: bfloat16 [2, 512, 4096], P(None, 'ctx', 'tp'), may hold values from -8 to 8
- filters: float32 [3, 3, 128], replicated, may hold values from 0.5 to 1.5
- doc_lengths: int32 [8], replicated, may hold values from 1 to 512, 1024 in all
Outputs:
- d_q_pre: float32 [2, 512, 4096], P(None, 'ctx', 'tp')
- d_k_pre: float32 [2, 512, 512], P(None, 'ctx', 'tp')
- d_v_pre: float32 [2, 512, 512], P(None, 'ctx', 'tp')
- d_filters: float32 [3, 3, 128], replicated
Inputs may be any that keep to these rules, and one draw needn't show every extreme that they name: `doc_lengths`: the lengths sum to 1024, and the longest document has exactly 512 positions.
All inputs are finite; a program needn't handle non-finite values.
Results may differ from a plain program's by a relative error of at most 0.009.
The roundings to bfloat16 on the way count: a program that leaves them out, or rounds other values in their place, can miss the bound.
Values may be sent and summed in bfloat16 or wider, within the bound.
No kernel may reach another device: no remote copies, remote signals or barrier semaphores. Data moves between devices by JAX's collectives and lax.ppermute only.
A program may use at most 128 MiB of HBM per device.

v0:
```python
import functools

import jax
import jax.numpy as jnp
import numpy as np
from jax import lax
from jax.experimental import pallas as pl
from jax.experimental.pallas import tpu as pltpu
from jax.sharding import PartitionSpec as P

LANES = 128
NT = (((1,), (1,)), ((), ()))
NN = (((1,), (0,)), ((), ()))
TN = (((0,), (0,)), ((), ()))
TAIL = 16
MAX_CHUNK = 640
RIM = 8
MAX_DIRECT = 4
WINDOWS = (2, 4, 6)
MIB = 1 << 20


def loop(count, body, init, unrolled=16):
    if count <= unrolled:
        for step in range(count):
            init = body(step, init)
        return init
    return lax.fori_loop(0, count, body, init)


def aligned(start, multiple):
    return start if isinstance(start, int) else pl.multiple_of(start, multiple)


def doc_starts(lengths_ref):
    starts = [jnp.int32(0)]
    for index in range(lengths_ref.shape[0] - 1):
        starts.append(starts[-1] + lengths_ref[index])
    return starts


def fold_rows(terms):
    rows, lanes = terms.shape
    return jnp.sum(terms.reshape(rows // 8, 8, lanes), axis=0)


def split_bits(values):
    high = values.astype(jnp.bfloat16)
    low = (values - high.astype(jnp.float32)).astype(jnp.bfloat16)
    return high, low


def joined(pair):
    rows = pair.shape[0] // 2
    pair = pair.astype(jnp.float32)
    return pair[:rows] + pair[rows:]


class Slots:
    def __init__(self, refs, me):
        self.refs, self.me = refs, me

    def __getitem__(self, flip):
        if len(self.refs) == 1:
            place = lax.rem(self.me, jnp.int32(self.refs[0].shape[0]))
            return self.refs[0].at[partner(place, flip)]
        return self.refs[flip]


def partner(me, flip):
    return lax.bitwise_xor(me, jnp.int32(flip))


def pack_kernel(k_ref, v_ref, q_ref, out_ref):
    span = k_ref.shape[1]
    kv = jnp.concatenate([k_ref[...], v_ref[...]], axis=2).reshape(2 * span, 2 * LANES)
    tails = []
    for half in range(2):
        last = q_ref[half].astype(jnp.float32)[TAIL - 2 :]
        tails += [last[:, at : at + 2 * LANES] for at in range(0, last.shape[1], 2 * LANES)]
    out_ref[: 2 * span] = kv
    out_ref[2 * span :] = jnp.concatenate(tails, axis=0).astype(jnp.bfloat16)


def prep_kernel(ctx_count, direct, lengths_ref, filters_ref, q_hbm, d_out_hbm, own_ref, *refs):
    near_refs, refs = refs[:-9], refs[-9:]
    same_ref, same_two_ref, q_scr, qc_ref, do_ref, rim_scr, q_ref, d_out_ref, sems = refs
    f32, bf16 = jnp.float32, jnp.bfloat16
    loads = [
        pltpu.make_async_copy(q_hbm, q_ref, sems.at[0]),
        pltpu.make_async_copy(d_out_hbm, d_out_ref, sems.at[1]),
    ]
    for load in loads:
        load.start()
    group = ctx_count // 2
    span = q_ref.shape[1]
    heads = q_ref.shape[2] // LANES
    blocks = 2 * ctx_count
    length = span * blocks
    me = lax.axis_index("ctx")
    near = Slots((None,) + near_refs if direct else near_refs, me)
    starts = doc_starts(lengths_ref)

    def fill(index, carry):
        rows = pl.ds(aligned(8 + index * span, 8), span)
        same_ref[rows] = jnp.ones((span, LANES), f32)
        same_two_ref[rows] = jnp.ones((span, LANES), f32)
        return carry

    loop(blocks, fill, 0)
    zeros = jnp.zeros((8, LANES), f32)
    for rows in (slice(0, 8), slice(8 + length, 16 + length)):
        same_ref[rows] = zeros
        same_two_ref[rows] = zeros
    for start in starts:
        same_ref[pl.ds(8 + start, 1)] = zeros[:1]
        same_two_ref[pl.ds(8 + start, 1)] = zeros[:1]
        same_two_ref[pl.ds(9 + start, 1)] = zeros[:1]

    before, after = jnp.maximum(me - 1, 0), jnp.minimum(me + 1, ctx_count - 1)
    for index in (before, after):
        rim_scr[index] = jnp.zeros(rim_scr.shape[1:], f32)
    rim_scr[me] = own_ref[2 * span :].astype(f32)

    def place_rims(step, carry):
        flip = step + 1
        if not direct or flip & (flip + 1) == 0:
            rim_scr[partner(me, flip)] = near[flip][2 * span :].astype(f32)
        return carry

    loop(group - 1, place_rims, 0, 16 if direct else 1)
    rim_before, rim_after = rim_scr[before], rim_scr[after]
    late_rim = jnp.where(me == ctx_count - 1, rim_after[:RIM], rim_after[RIM:])
    rims = [rim_before[:RIM], late_rim]
    first_place = [me * span, (blocks - 1 - me) * span]
    taps = [filters_ref[0, tap : tap + 1] for tap in range(3)]

    for load in loads:
        load.wait()
    for half in range(2):
        rows = pl.ds(aligned(first_place[half] + 8, 8), span)
        one, two = same_ref[rows], same_two_ref[rows]
        for head in range(heads):
            lanes = slice(head * LANES, (head + 1) * LANES)
            at = 2 * (head // 2)
            q_scr[half, head, 6:8] = rims[half][at : at + 2, (head % 2) * LANES : (head % 2 + 1) * LANES]
            q_scr[half, head, 8:] = q_ref[half, :, lanes].astype(f32)
            total = taps[0] * q_scr[half, head, 8:]
            total = total + one * (taps[1] * q_scr[half, head, 7 : 7 + span])
            total = total + two * (taps[2] * q_scr[half, head, 6 : 6 + span])
            qc_ref[half, head * span : (head + 1) * span] = total.astype(bf16)
            do_ref[half, head * span : (head + 1) * span] = d_out_ref[half, :, lanes]


def grads_kernel(ctx_count, direct, lengths_ref, filters_ref, *refs):
    group = ctx_count // 2
    arrays = group - 1 if direct else 1
    same_scr, same_two_scr, q_in_ref, qc_in_ref, do_scr, own_ref, across_ref = refs[:7]
    refs = refs[7:]
    near_in, far_in, refs = refs[:arrays], refs[arrays : 2 * arrays], refs[2 * arrays :]
    dq_hbm, dq_tail_ref, own_near_ref, own_far_ref = refs[:4]
    arrays = group - 1 if direct else 1
    first_out, late_out, refs = refs[4 : 4 + arrays], refs[4 + arrays : 4 + 2 * arrays], refs[4 + 2 * arrays :]
    kv_scr, conv_scr, dkv_scr, q_scr, qc_scr, dq_scr = refs[:6]
    bias_scr, s_scr, dp_scr, dq_ref, sems = refs[6:]
    f32, bf16 = jnp.float32, jnp.bfloat16
    span = own_ref.shape[0] // 2 - TAIL // 2
    heads = q_in_ref.shape[1]
    half_rows = span * ctx_count
    length = 2 * half_rows
    blocks = 2 * ctx_count
    me = lax.axis_index("ctx")
    near_in = Slots((None,) + near_in if direct else near_in, me)
    far_in = Slots((None,) + far_in if direct else far_in, me)
    first_out = Slots((None,) + first_out if direct else first_out, me)
    late_out = Slots((None,) + late_out if direct else late_out, me)
    scale = LANES**-0.5
    log2_scale = scale * 1.4426950408889634
    starts = doc_starts(lengths_ref)

    def place(index, block):
        for tensor in range(2):
            lanes = slice(tensor * LANES, (tensor + 1) * LANES)
            kv_scr[tensor, pl.ds(aligned(8 + index * span, 8), span)] = block[:, lanes].astype(f32)

    def place_both(message, index):
        place(index, message[:span])
        place(blocks - 1 - index, message[span : 2 * span])

    def place_received(step, carry):
        flip = step + 1
        source = partner(me, flip)
        place_both(near_in[flip], source)
        place_both(far_in[flip], partner(source, group))
        return carry

    zeros = jnp.zeros((8, LANES), f32)
    for tensor in range(2):
        kv_scr[tensor, :8] = zeros
    for block_ref, index in ((own_ref, me), (across_ref, partner(me, group))):
        place_both(block_ref, index)
    loop(group - 1, place_received, 0, 16 if direct else 1)

    def taps(tensor):
        return [filters_ref[tensor, tap : tap + 1] for tap in range(3)]

    def masks(base, ahead):
        one = same_scr[pl.ds(base + 8 + min(ahead, 1), span)]
        return one, same_two_scr[pl.ds(base + 8 + ahead, span)]

    def convolve_kv(index, carry):
        base = index * span
        one, two = masks(base, 0)
        for tensor in range(2):
            zero_tap, one_tap, two_tap = taps(tensor + 1)
            total = zero_tap * kv_scr[tensor, pl.ds(aligned(base + 8, 8), span)]
            total = total + one * (one_tap * kv_scr[tensor, pl.ds(base + 7, span)])
            total = total + two * (two_tap * kv_scr[tensor, pl.ds(base + 6, span)])
            conv_scr[tensor, pl.ds(aligned(base, 16), span)] = total.astype(bf16)
        return carry

    loop(blocks, convolve_kv, 0)

    first_place = [me * span, (blocks - 1 - me) * span]
    middle = me == ctx_count - 1
    q_scr[...] = q_in_ref[...]
    qc_scr[...] = qc_in_ref[...]
    tails = far_in[group - 1][2 * span :].astype(f32)
    tails = [tails[:RIM], tails[RIM:]]
    for half, crossing in ((0, me == group), (1, me == group - 1)):

        @pl.when(crossing)
        def _(half=half):
            rows = pl.ds(aligned(first_place[half] + 8, 8), TAIL)
            one, two = same_scr[rows], same_two_scr[rows]
            zero_tap, one_tap, two_tap = taps(0)
            for head in range(heads):
                at = 2 * (head // 2)
                q_scr[half, head, 6:8] = tails[half][
                    at : at + 2, (head % 2) * LANES : (head % 2 + 1) * LANES
                ]
                total = zero_tap * q_scr[half, head, 8 : 8 + TAIL]
                total = total + one * (one_tap * q_scr[half, head, 7 : 7 + TAIL])
                total = total + two * (two_tap * q_scr[half, head, 6 : 6 + TAIL])
                qc_scr[half, head * span : head * span + TAIL] = total.astype(bf16)

    def attend(half, window, first_key):
        chunks = 1
        while window // chunks > MAX_CHUNK or window % (16 * chunks):
            chunks += 1
        size = window // chunks
        query = first_place[half] + lax.rem(
            lax.broadcasted_iota(jnp.int32, (1, LANES), 1), jnp.int32(span)
        )
        lowest = jnp.zeros((1, LANES), jnp.int32)
        for start in starts[1:]:
            lowest = jnp.where(query >= start, start, lowest)
        wide = 2 * LANES

        def fill_bias(step, carry):
            places = first_key + step * size + lax.broadcasted_iota(jnp.int32, (size, LANES), 0)
            allowed = (places >= lowest) & (places <= query)
            bias_scr[pl.ds(aligned(step * size, 16), size)] = jnp.where(allowed, 0.0, -1e30)
            return carry

        loop(chunks, fill_bias, 0, 1)
        whole_window = pl.ds(aligned(first_key, 16), window)
        keys_t = conv_scr[0, whole_window].T if chunks == 1 else None
        for at in range(heads * span // wide):
            slot = (half * (heads * span // wide) + at) % s_scr.shape[0]
            cols = slice(at * wide, (at + 1) * wide)
            queries = qc_scr[half, cols]
            grads = do_scr[half, cols]

            def key_rows(step):
                return pl.ds(aligned(first_key + step * size, 16), size)

            def score(step, top):
                keys = conv_scr[0, key_rows(step)]
                scores = lax.dot_general(keys, queries, NT, preferred_element_type=f32)
                bias = bias_scr[pl.ds(aligned(step * size, 16), size)]
                scores = scores + jnp.concatenate([bias, bias], axis=1)
                s_scr[slot, pl.ds(aligned(step * size, 16), size)] = scores
                return jnp.maximum(top, jnp.max(scores, axis=0, keepdims=True))

            top = loop(chunks, score, jnp.full((1, wide), -1e30, f32), 1)

            def weigh(step, carry):
                total, weighted = carry
                rows = pl.ds(aligned(step * size, 16), size)
                weights = jnp.exp2((s_scr[slot, rows] - top) * log2_scale)
                values = conv_scr[1, key_rows(step)]
                prob_grads = lax.dot_general(values, grads, NT, preferred_element_type=f32)
                s_scr[slot, rows] = weights
                dp_scr[slot, rows] = prob_grads
                total = total + jnp.sum(weights, axis=0, keepdims=True)
                weighted = weighted + jnp.sum(weights * prob_grads, axis=0, keepdims=True)
                return total, weighted

            zeros = jnp.zeros((1, wide), f32)
            total, weighted = loop(chunks, weigh, (zeros, zeros), 1)
            inverse = 1.0 / total
            mean = weighted * inverse
            slope = inverse * scale

            def accumulate(step, dq):
                rows = pl.ds(aligned(step * size, 16), size)
                weights = s_scr[slot, rows]
                probs = (weights * inverse).astype(bf16)
                score_grads = (weights * slope * (dp_scr[slot, rows] - mean)).astype(bf16)
                dk = lax.dot_general(score_grads, queries, NN, preferred_element_type=f32)
                dv = lax.dot_general(probs, grads, NN, preferred_element_type=f32)
                target = pl.ds(aligned(first_key + step * size, 16), size)
                for tensor, terms in enumerate((dk, dv)):
                    dkv_scr[tensor, target] += terms
                if keys_t is not None:
                    return lax.dot_general(keys_t, score_grads, NN, preferred_element_type=f32)
                keys = conv_scr[0, key_rows(step)]
                return dq + lax.dot_general(keys, score_grads, TN, preferred_element_type=f32)

            dq = loop(chunks, accumulate, jnp.zeros((LANES, wide), f32), 1)
            dq = dq.T
            for part in range(wide // span):
                head = at * (wide // span) + part
                dq_scr[half, head, :span] = dq[part * span : (part + 1) * span]

    def clear(index, carry):
        for tensor in range(2):
            dkv_scr[tensor, pl.ds(aligned(index * span, 8), span)] = jnp.zeros((span, LANES), f32)
        return carry

    loop(blocks, clear, 0)
    for tensor in range(2):
        dkv_scr[tensor, length:] = zeros

    for half in range(2):
        widest = ctx_count + half
        lowest = jnp.int32(0)
        for start in starts[1:]:
            lowest = jnp.where(first_place[half] >= start, start, lowest)
        needed = first_place[half] // span - lowest // span + 1
        below = 0
        for count in [count for count in WINDOWS if direct and count < widest] + [widest]:

            @pl.when((needed > below) & (needed <= count))
            def _(half=half, count=count):
                first_key = jnp.maximum(first_place[half] + span - count * span, 0)
                attend(half, count * span, first_key)

            below = count

    next_rows = jnp.where(middle, dq_scr[1, :, :8], 0.0)
    dq_scr[0, :, span:] = next_rows
    dq_scr[1, :, span:] = jnp.zeros_like(next_rows)
    sums = [jnp.zeros((8, LANES), f32) for _ in range(3)]
    for half in range(2):
        one, two = masks(first_place[half], 0)
        ahead_one = same_scr[pl.ds(first_place[half] + 9, span)]
        ahead_two = same_two_scr[pl.ds(first_place[half] + 10, span)]
        zero_tap, one_tap, two_tap = taps(0)
        for head in range(heads):
            lanes = slice(head * LANES, (head + 1) * LANES)
            grads = dq_scr[half, head, :span]
            out = zero_tap * grads
            out = out + ahead_one * (one_tap * dq_scr[half, head, 1 : 1 + span])
            out = out + ahead_two * (two_tap * dq_scr[half, head, 2 : 2 + span])
            dq_ref[half, :, lanes] = out
            dq_tail_ref[half, :, lanes] = out[span - 8 :]
            sums[0] += fold_rows(grads * q_scr[half, head, 8:])
            sums[1] += fold_rows(grads * one * q_scr[half, head, 7 : 7 + span])
            sums[2] += fold_rows(grads * two * q_scr[half, head, 6 : 6 + span])
    q_sums = [jnp.sum(term, axis=0, keepdims=True) for term in sums]
    store = pltpu.make_async_copy(dq_ref, dq_hbm, sems.at[0])
    store.start()

    def finish_block(index, carry, target, row):
        base = pl.multiple_of(index * span, 8)
        one, two = masks(base, 0)
        ahead_one = same_scr[pl.ds(base + 9, span)]
        ahead_two = same_two_scr[pl.ds(base + 10, span)]
        carry = list(carry)
        for tensor in range(2):
            zero_tap, one_tap, two_tap = taps(tensor + 1)
            own = dkv_scr[tensor, pl.ds(base, span)]
            out = zero_tap * own
            out = out + ahead_one * (one_tap * dkv_scr[tensor, pl.ds(base + 1, span)])
            out = out + ahead_two * (two_tap * dkv_scr[tensor, pl.ds(base + 2, span)])
            lanes = slice(tensor * LANES, (tensor + 1) * LANES)
            target[row : row + span, lanes] = out.astype(target.dtype)
            at = 3 * tensor
            carry[at] += fold_rows(own * kv_scr[tensor, pl.ds(base + 8, span)])
            carry[at + 1] += fold_rows(own * one * kv_scr[tensor, pl.ds(base + 7, span)])
            carry[at + 2] += fold_rows(own * two * kv_scr[tensor, pl.ds(base + 6, span)])
        return tuple(carry)

    low = me < group

    def finish(step, carry):
        flip = step + 1
        owner = partner(me, flip)
        far_owner = partner(me, flip + group)
        near_late = blocks - 1 - owner
        second = jnp.where(low, blocks - 1 - far_owner, owner)
        third = jnp.where(low & (me > owner), owner, near_late)
        carry = finish_block(far_owner, carry, first_out[flip], 0)
        carry = finish_block(second, carry, first_out[flip], span)
        carry = finish_block(third, carry, late_out[flip], 0)
        return carry

    kv_sums = (zeros,) * 6
    for target, index in ((own_far_ref, partner(me, group)), (own_near_ref, me)):
        kv_sums = finish_block(index, kv_sums, target, 0)
        kv_sums = finish_block(blocks - 1 - index, kv_sums, target, span)
    kv_sums = loop(group - 1, finish, kv_sums)
    kv_sums = [jnp.sum(term, axis=0, keepdims=True) for term in kv_sums]

    padding = [jnp.zeros((2, LANES), f32)]
    left = jnp.concatenate(q_sums + kv_sums[:3] + padding, axis=0)
    right = jnp.concatenate([jnp.zeros((3, LANES), f32)] + kv_sums[3:] + padding, axis=0)
    sums_tile = jnp.concatenate([left, right], axis=1)
    sums_pair = jnp.concatenate(split_bits(sums_tile), axis=0)
    own_far_ref[2 * span :] = joined(sums_pair)
    rims = []
    for half in range(2):
        rows = [dq_scr[half, head, :2] for head in range(heads)]
        rows = [jnp.concatenate(rows[at : at + 2], axis=1) for at in range(0, heads, 2)]
        rims.append(jnp.concatenate(rows, axis=0))

    def rim_for(index):
        return jnp.concatenate(split_bits(jnp.where(index < me, rims[0], rims[1])), axis=0)

    def store_rims(step, carry):
        flip = step + 1
        owner = partner(me, flip)
        first_out[flip][2 * span : 2 * span + 16] = sums_pair
        if not direct or flip == group - 1:
            first_out[flip][2 * span + 16 :] = rim_for(partner(owner, group))
        if not direct or flip & (flip + 1) == 0:
            late_out[flip][span:] = rim_for(owner)
        return carry

    loop(group - 1, store_rims, 0, 16 if direct else 1)
    store.wait()


def merge_kernel(ctx_count, direct, own_near_ref, own_far_ref, *refs):
    received_refs, (near_ref, far_ref, half_sums_ref, sums_scr) = refs[:-4], refs[-4:]
    f32, bf16 = jnp.float32, jnp.bfloat16
    group = ctx_count // 2
    me = lax.axis_index("ctx")
    low = me < group
    received = Slots((own_far_ref,) + received_refs if direct else received_refs, me)
    place = lax.rem(me, jnp.int32(group))
    span = own_near_ref.shape[0] // 2
    rows = 2 * span
    sums_scr[place] = own_far_ref[rows:]
    def add(step, carry):
        flip = step + 1
        message = received[flip]
        early, second = [message[at * span : (at + 1) * span].astype(f32) for at in range(2)]
        near_early, far_early, far_late = carry
        sums_scr[partner(place, flip)] = joined(message[rows : rows + 16])
        zero = jnp.zeros_like(second)
        return (
            near_early + jnp.where(low, zero, second),
            far_early + early,
            far_late + jnp.where(low, second, zero),
        )

    init = (own_near_ref[:span], own_far_ref[:span], own_far_ref[span:rows])
    totals = loop(group - 1, add, init, 16 if direct else 1)
    near_ref[:span] = totals[0]
    near_ref[span:] = own_near_ref[span:]
    far_ref[:span] = totals[1].astype(bf16)
    far_ref[span:rows] = totals[2].astype(bf16)
    sums = loop(group, lambda index, carry: carry + sums_scr[index], jnp.zeros((8, 2 * LANES), f32))
    pair = jnp.concatenate(split_bits(sums), axis=0)
    half_sums_ref[...] = joined(pair)
    far_ref[rows : rows + 16] = pair
    far_ref[rows + 16 :] = received[group - 1][rows + 16 :]


def sums_kernel(span, half_sums_ref, far_ref, out_ref):
    sums = half_sums_ref[...] + joined(far_ref[2 * span : 2 * span + 16])
    out_ref[0] = sums[0:3, :LANES]
    out_ref[1] = sums[3:6, :LANES]
    out_ref[2] = sums[3:6, LANES:]


def finish_kernel(
    ctx_count, direct, lengths_ref, filters_ref, dq_in_hbm, tail_ref, near_ref, far_ref, *refs
):
    received_refs, refs = refs[:-8], refs[-8:]
    dq_hbm, dk_hbm, dv_hbm, dq_ref, dk_ref, dv_ref, rim_scr, sems = refs
    f32 = jnp.float32
    group = ctx_count // 2
    span = dk_ref.shape[1]
    me = lax.axis_index("ctx")
    low = me < group
    received = Slots((None,) + received_refs if direct else received_refs, me)
    starts = doc_starts(lengths_ref)
    blocks = 2 * ctx_count
    neighbours = [jnp.minimum(me + 1, ctx_count - 1), jnp.maximum(me - 1, 0)]
    for index in neighbours:
        rim_scr[index] = jnp.zeros(rim_scr.shape[1:], f32)

    def add(step, carry):
        flip = step + 1
        source = partner(me, flip)
        message = received[flip]
        terms = message[:span].astype(f32)
        if not direct or flip & (flip + 1) == 0:
            rim_scr[source] = joined(message[span:])
        to_early = low & (source > me)
        zero = jnp.zeros_like(terms)
        return carry[0] + jnp.where(to_early, terms, zero), carry[1] + jnp.where(to_early, zero, terms)

    total = near_ref[...] + far_ref[: 2 * span].astype(f32)
    total = loop(group - 1, add, (total[:span], total[span:]), 16 if direct else 1)
    for half in range(2):
        dk_ref[half] = total[half][:, :LANES]
        dv_ref[half] = total[half][:, LANES:]
    stores = [
        pltpu.make_async_copy(dk_ref, dk_hbm, sems.at[0]),
        pltpu.make_async_copy(dv_ref, dv_hbm, sems.at[1]),
        pltpu.make_async_copy(dq_ref, dq_hbm.at[:, pl.ds(span - 8, 8)], sems.at[2]),
    ]
    for store in stores[:2]:
        store.start()

    def same(place):
        cut = place >= blocks * span
        for start in starts:
            cut = cut | (place == start)
        return jnp.where(cut, 0.0, 1.0).astype(f32)

    heads = dq_ref.shape[2] // LANES
    taps = [jnp.concatenate([filters_ref[0, tap : tap + 1]] * heads, axis=1) for tap in range(3)]
    row = lax.broadcasted_iota(jnp.int32, dq_ref.shape[1:], 0)
    far_rim = joined(far_ref[2 * span + 16 :])
    crosses = [me == group - 1, me == group]
    first_place = [me * span, (blocks - 1 - me) * span]
    present = [me < ctx_count - 1, me > 0]
    for half in range(2):
        rim = jnp.where(crosses[half], far_rim, rim_scr[neighbours[half]])
        rows = jnp.concatenate([rim[2 * at : 2 * at + 2] for at in range(rim.shape[0] // 2)], axis=1)
        end = first_place[half] + span
        zero, one, two = same(end - 1), same(end), same(end + 1)
        one = jnp.where(present[half], one, 0.0)
        last_but_one = (zero * one) * (taps[2] * rows[0:1])
        last = one * (taps[1] * rows[0:1]) + (one * two) * (taps[2] * rows[1:2])
        extra = jnp.where(row == 6, last_but_one, jnp.where(row == 7, last, 0.0))
        dq_ref[half] = tail_ref[half] + extra
    stores[2].start()
    for store in stores:
        store.wait()


def shards(q_pre, k_pre, value_before_filter, d_out, filters, doc_lengths):
    f32, bf16 = jnp.float32, jnp.bfloat16
    ctx_count = lax.axis_size("ctx")
    span, width = q_pre.shape[1:]
    length = 2 * span * ctx_count
    rim = 4 * width // (2 * LANES)
    vmem = pl.BlockSpec(memory_space=pltpu.VMEM)
    smem = pl.BlockSpec(memory_space=pltpu.SMEM)
    hbm = pl.BlockSpec(memory_space=pltpu.HBM)

    group = ctx_count // 2
    direct = group <= MAX_DIRECT
    halves = [[half * group + at for at in range(group)] for half in range(2)]
    msg_rows = 2 * span + rim

    def whole(shape):
        return pl.BlockSpec(shape, lambda i: (0,) * len(shape))

    def in_hbm(array):
        return pltpu.with_memory_space_constraint(array, pltpu.HBM)

    def flipped(array, flip):
        return lax.ppermute(array, "ctx", [(i, i ^ flip) for i in range(ctx_count)])

    def gathered(array):
        if direct:
            return [flipped(array, flip) for flip in range(1, group)]
        return [lax.all_gather(array, "ctx", axis_index_groups=halves)]

    def delivered(arrays):
        if direct:
            return [flipped(array, step + 1) for step, array in enumerate(arrays)]
        return [lax.all_to_all(arrays[0], "ctx", 0, 0, axis_index_groups=halves, tiled=True)]

    packed = pl.pallas_call(
        pack_kernel,
        grid=(1,),
        out_shape=jax.ShapeDtypeStruct((msg_rows, 2 * LANES), bf16),
        in_specs=[
            whole(k_pre.shape),
            whole(k_pre.shape),
            pl.BlockSpec((2, TAIL, width), lambda i: (0, span // TAIL - 1, 0)),
        ],
        out_specs=whole((msg_rows, 2 * LANES)),
        compiler_params=pltpu.CompilerParams(vmem_limit_bytes=4 * MIB),
        name="pack",
    )(*[in_hbm(array) for array in (k_pre, value_before_filter, q_pre)])
    across = flipped(packed, group)
    near = gathered(packed)
    far = gathered(across)
    received = [packed, across] + near + far

    window = span * ctx_count + span
    if direct:
        flips = range(1, group)
        first_shapes = [(2 * span + (32 if flip == group - 1 else 16), 2 * LANES) for flip in flips]
        late_shapes = [(span + (16 if flip & (flip + 1) == 0 else 0), 2 * LANES) for flip in flips]
    else:
        first_shapes = [(group, 2 * span + 32, 2 * LANES)]
        late_shapes = [(group, span + 16, 2 * LANES)]
    slots = 4 if direct else 1
    heads = width // LANES
    by_head = (2, span * heads, LANES)
    padded = (2, heads, span + 8, LANES)
    prepared = pl.pallas_call(
        functools.partial(prep_kernel, ctx_count, direct),
        out_shape=[
            jax.ShapeDtypeStruct((length + 16, LANES), f32),
            jax.ShapeDtypeStruct((length + 16, LANES), f32),
            jax.ShapeDtypeStruct(padded, f32),
            jax.ShapeDtypeStruct(by_head, bf16),
            jax.ShapeDtypeStruct(by_head, bf16),
        ],
        in_specs=[smem, vmem, hbm, hbm] + [vmem] * (1 + len(near)),
        out_specs=[vmem] * 5,
        scratch_shapes=[
            pltpu.VMEM((ctx_count, rim, 2 * LANES), f32),
            pltpu.VMEM(q_pre.shape, bf16),
            pltpu.VMEM(q_pre.shape, bf16),
            pltpu.SemaphoreType.DMA((2,)),
        ],
        compiler_params=pltpu.CompilerParams(vmem_limit_bytes=(8 if direct else 32) * MIB),
        name="prep",
    )(doc_lengths, filters, in_hbm(q_pre), in_hbm(d_out), packed, *near)
    scratch = [
        pltpu.VMEM((2, length + 16, LANES), f32),
        pltpu.VMEM((2, length, LANES), bf16),
        pltpu.VMEM((2, length + 8, LANES), f32),
        pltpu.VMEM(padded, f32),
        pltpu.VMEM(by_head, bf16),
        pltpu.VMEM(padded, f32),
        pltpu.VMEM((window, LANES), f32),
        pltpu.VMEM((slots, window, 2 * LANES), f32),
        pltpu.VMEM((slots, window, 2 * LANES), f32),
        pltpu.VMEM(q_pre.shape, f32),
        pltpu.SemaphoreType.DMA((1,)),
    ]
    own_shapes = [(2 * span, 2 * LANES), (2 * span + 8, 2 * LANES)]
    d_q_main, d_q_tail, own_near, own_far, *sent = pl.pallas_call(
        functools.partial(grads_kernel, ctx_count, direct),
        out_shape=[jax.ShapeDtypeStruct(q_pre.shape, f32)]
        + [jax.ShapeDtypeStruct(shape, f32) for shape in [(2, 8, width)] + own_shapes]
        + [jax.ShapeDtypeStruct(shape, bf16) for shape in first_shapes + late_shapes],
        in_specs=[smem, vmem] + [vmem] * (len(prepared) + len(received)),
        out_specs=[hbm] + [vmem] * (3 + len(first_shapes + late_shapes)),
        scratch_shapes=scratch,
        compiler_params=pltpu.CompilerParams(vmem_limit_bytes=(20 if direct else 62) * MIB),
        name="grads",
    )(doc_lengths, filters, *prepared, *received)
    half_terms = delivered(sent[: len(first_shapes)])
    merged_shapes = [
        jax.ShapeDtypeStruct((2 * span, 2 * LANES), f32),
        jax.ShapeDtypeStruct((2 * span + 32, 2 * LANES), bf16),
        jax.ShapeDtypeStruct((8, 2 * LANES), f32),
    ]
    near, far, half_sums = pl.pallas_call(
        functools.partial(merge_kernel, ctx_count, direct),
        out_shape=merged_shapes,
        in_specs=[vmem] * (2 + len(half_terms)),
        out_specs=[vmem] * len(merged_shapes),
        scratch_shapes=[pltpu.VMEM((group, 8, 2 * LANES), f32)],
        compiler_params=pltpu.CompilerParams(vmem_limit_bytes=(4 if direct else 40) * MIB),
        name="merge",
    )(own_near, own_far, *half_terms)
    from_half = flipped(far, group)
    late_terms = delivered(sent[len(first_shapes) :])

    sums = pl.pallas_call(
        functools.partial(sums_kernel, span),
        out_shape=jax.ShapeDtypeStruct(filters.shape, f32),
        in_specs=[vmem, vmem],
        out_specs=vmem,
        compiler_params=pltpu.CompilerParams(vmem_limit_bytes=2 * MIB),
        name="sums",
    )(half_sums, from_half)
    count = lax.axis_size("tp")
    all_sums = [sums] + [
        lax.ppermute(sums, "tp", [(i, i ^ flip) for i in range(count)]) for flip in range(1, count)
    ]
    d_q_pre, d_k_pre, d_v_pre = pl.pallas_call(
        functools.partial(finish_kernel, ctx_count, direct),
        out_shape=(
            jax.ShapeDtypeStruct(q_pre.shape, f32),
            jax.ShapeDtypeStruct(k_pre.shape, f32),
            jax.ShapeDtypeStruct(k_pre.shape, f32),
        ),
        in_specs=[smem, vmem, hbm] + [vmem] * (3 + len(late_terms)),
        out_specs=(hbm, hbm, hbm),
        scratch_shapes=[
            pltpu.VMEM((2, 8, width), f32),
            pltpu.VMEM(k_pre.shape, f32),
            pltpu.VMEM(k_pre.shape, f32),
            pltpu.VMEM((ctx_count, rim // 2, 2 * LANES), f32),
            pltpu.SemaphoreType.DMA((3,)),
        ],
        input_output_aliases={2: 0},
        compiler_params=pltpu.CompilerParams(vmem_limit_bytes=(4 if direct else 16) * MIB),
        name="finish",
    )(doc_lengths, filters, d_q_main, d_q_tail, near, from_half, *late_terms)
    while len(all_sums) > 1:
        all_sums = [all_sums[at] + all_sums[at + 1] for at in range(0, len(all_sums), 2)]
    return (d_q_pre, d_k_pre, d_v_pre, all_sums[0])


def solution(mesh):
    split = P(None, "ctx", "tp")
    return jax.shard_map(
        shards,
        mesh=mesh,
        in_specs=(split, split, split, split, P(), P()),
        out_specs=(split, split, split, P()),
        check_vma=False,
    )
```

profile of v0, /device:TPU:0, one launch (start us, length us, event | category | flops | bytes accessed | tf_op | source)
XLA Modules:
  0.0 40.2 jit_solution(16368072047058655138)
XLA Ops:
  0.6 0.0 copy-start.1
  0.6 0.0 copy-start
  0.7 0.9 %pack.1.own_ref.refs_5_ = bf16[144,256]{1,0:T(8,128)(2,1)S(1)} custom-call(bf16[2,64,128]{2,1,0:T(8,128)(2,1)} %k_ref.1, bf16[2,64,128]{2,1,0:T(8,128)(2,1)} %v_ref.1, bf16[2,64,1024]{2,1,0:T(8,128)(2,1)} %q_hbm.1), custom_call_target="tpu_custom_call" | custom-call | tf_op jit(solution)/shard_map/pack/pallas_call | solution.py:593
  1.6 4.1 %collective-permute-start.3 = (bf16[144,256]{1,0:T(8,128)(2,1)S(1)}, bf16[144,256]{1,0:T(8,128)(2,1)S(1)}, u32[]{:S(2)}, u32[]{:S(2)}) collective-permute-start(bf16[144,256]{1,0:T(8,128)(2,1)S(1)} %pack.1.own_ref.refs_5_), channel_id=1, source_target_pairs={{0,16},{4,20},{8,24},{12,28},{16,0},{20,4},{24,8},{28,12},{1,17},{... | collective-permute-start | bytes 221192 | tf_op jit(solution)/shard_map/ppermute | solution.py:581
  5.7 2.5 %collective-permute-start.2 = (bf16[144,256]{1,0:T(8,128)(2,1)S(1)}, bf16[144,256]{1,0:T(8,128)(2,1)S(1)}, u32[]{:S(2)}, u32[]{:S(2)}) collective-permute-start(bf16[144,256]{1,0:T(8,128)(2,1)S(1)} %pack.1.own_ref.refs_5_), channel_id=1, source_target_pairs={{0,12},{4,8},{8,4},{12,0},{16,28},{20,24},{24,20},{28,16},{1,13},{... | collective-permute-start | bytes 221192 | tf_op jit(solution)/shard_map/ppermute | solution.py:581
  8.2 0.4 %collective-permute-start.1 = (bf16[144,256]{1,0:T(8,128)(2,1)S(1)}, bf16[144,256]{1,0:T(8,128)(2,1)S(1)}, u32[]{:S(2)}, u32[]{:S(2)}) collective-permute-start(bf16[144,256]{1,0:T(8,128)(2,1)S(1)} %pack.1.own_ref.refs_5_), channel_id=1, source_target_pairs={{0,8},{4,12},{8,0},{12,4},{16,24},{20,28},{24,16},{28,20},{1,9},{5... | collective-permute-start | bytes 221192 | tf_op jit(solution)/shard_map/ppermute | solution.py:581
  8.6 0.5 %collective-permute-start = (bf16[144,256]{1,0:T(8,128)(2,1)S(1)}, bf16[144,256]{1,0:T(8,128)(2,1)S(1)}, u32[]{:S(2)}, u32[]{:S(2)}) collective-permute-start(bf16[144,256]{1,0:T(8,128)(2,1)S(1)} %pack.1.own_ref.refs_5_), channel_id=1, source_target_pairs={{0,4},{4,0},{8,12},{12,8},{16,20},{20,16},{24,28},{28,24},{1,5},{5... | collective-permute-start | bytes 221192 | tf_op jit(solution)/shard_map/ppermute | solution.py:581
  9.2 0.0 collective-permute-done.3.refs_6_
  9.2 2.5 %collective-permute-start.6 = (bf16[144,256]{1,0:T(8,128)(2,1)S(1)}, bf16[144,256]{1,0:T(8,128)(2,1)S(1)}, u32[]{:S(2)}, u32[]{:S(2)}) collective-permute-start(bf16[144,256]{1,0:T(8,128)(2,1)S(1)} %collective-permute-done.3.refs_6_), channel_id=1, source_target_pairs={{0,12},{4,8},{8,4},{12,0},{16,28},{20,24},{24,20},{28,16},{1,13},{... | collective-permute-start | bytes 221192 | tf_op jit(solution)/shard_map/ppermute | solution.py:581
  11.7 0.7 %collective-permute-start.5 = (bf16[144,256]{1,0:T(8,128)(2,1)S(1)}, bf16[144,256]{1,0:T(8,128)(2,1)S(1)}, u32[]{:S(2)}, u32[]{:S(2)}) collective-permute-start(bf16[144,256]{1,0:T(8,128)(2,1)S(1)} %collective-permute-done.3.refs_6_), channel_id=1, source_target_pairs={{0,8},{4,12},{8,0},{12,4},{16,24},{20,28},{24,16},{28,20},{1,9},{5... | collective-permute-start | bytes 221192 | tf_op jit(solution)/shard_map/ppermute | solution.py:581
  12.4 0.0 collective-permute-done.2.refs_2_.refs_9_
  12.4 0.9 %collective-permute-start.4 = (bf16[144,256]{1,0:T(8,128)(2,1)S(1)}, bf16[144,256]{1,0:T(8,128)(2,1)S(1)}, u32[]{:S(2)}, u32[]{:S(2)}) collective-permute-start(bf16[144,256]{1,0:T(8,128)(2,1)S(1)} %collective-permute-done.3.refs_6_), channel_id=1, source_target_pairs={{0,4},{4,0},{8,12},{12,8},{16,20},{20,16},{24,28},{28,24},{1,5},{5... | collective-permute-start | bytes 221192 | tf_op jit(solution)/shard_map/ppermute | solution.py:581
  13.3 0.1 collective-permute-done.1.refs_1_.refs_8_
  13.4 0.9 %collective-permute-done.refs_0_.refs_7_ = bf16[144,256]{1,0:T(8,128)(2,1)S(1)} collective-permute-done((bf16[144,256]{1,0:T(8,128)(2,1)S(1)}, bf16[144,256]{1,0:T(8,128)(2,1)S(1)}, u32[]{:S(2)}, u32[]{:S(2)}) %collective-permute-start) | collective-permute-done | bytes 73760 | tf_op jit(solution)/shard_map/ppermute | solution.py:581
  14.3 0.0 copy-done.1
  14.3 0.0 copy-done
  14.3 1.8 %prep.1 = (f32[1040,128]{1,0:T(8,128)S(1)}, f32[1040,128]{1,0:T(8,128)S(1)}, f32[2,8,72,128]{3,2,1,0:T(8,128)S(1)}, bf16[2,512,128]{2,1,0:T(8,128)(2,1)S(1)}, bf16[2,512,128]{2,1,0:T(8,128)(2,1)S(1)}) custom-call(s32[8]{0:T(128)S(1)} %copy-done.1, f32[3,3,128]{2,1,0:T(4,128)S(1)} %copy-done, bf16[2,64,1024]{2,1,0:T(8,128)(2,1)} %q_hbm.1, ...), custom_call_target="tpu_custom_call" | custom-call | tf_op jit(solution)/shard_map/prep/pallas_call | solution.py:623
  16.1 0.0 collective-permute-done.6.refs_12_
  16.1 0.0 collective-permute-done.5.refs_11_
  16.1 0.6 %collective-permute-done.4.refs_10_ = bf16[144,256]{1,0:T(8,128)(2,1)S(1)} collective-permute-done((bf16[144,256]{1,0:T(8,128)(2,1)S(1)}, bf16[144,256]{1,0:T(8,128)(2,1)S(1)}, u32[]{:S(2)}, u32[]{:S(2)}) %collective-permute-start.4) | collective-permute-done | bytes 73760 | tf_op jit(solution)/shard_map/ppermute | solution.py:581
  16.7 3.7 %grads.1 = (f32[2,64,1024]{2,1,0:T(8,128)}, f32[2,8,1024]{2,1,0:T(8,128)S(1)}, f32[128,256]{1,0:T(8,128)S(1)}, f32[136,256]{1,0:T(8,128)S(1)}, bf16[144,256]{1,0...) custom-call(s32[8]{0:T(128)S(1)} %copy-done.1, ...), custom_call_target="tpu_custom_call" | custom-call | tf_op jit(solution)/shard_map/grads/pallas_call | solution.py:657
  20.5 1.4 %collective-permute-start.9 = (bf16[160,256]{1,0:T(8,128)(2,1)S(1)}, bf16[160,256]{1,0:T(8,128)(2,1)S(1)}, u32[]{:S(2)}, u32[]{:S(2)}) collective-permute-start(bf16[160,256]{1,0:T(8,128)(2,1)S(1)} %get-tuple-element.36), channel_id=1, source_target_pairs={{0,12},{4,8},{8,4},{12,0},{16,28},{20,24},{24,20},{28,16},{1,13},{... | collective-permute-start | bytes 245768 | tf_op jit(solution)/shard_map/ppermute | solution.py:581
  21.8 1.9 %collective-permute-start.7 = (bf16[144,256]{1,0:T(8,128)(2,1)S(1)}, bf16[144,256]{1,0:T(8,128)(2,1)S(1)}, u32[]{:S(2)}, u32[]{:S(2)}) collective-permute-start(bf16[144,256]{1,0:T(8,128)(2,1)S(1)} %get-tuple-element.34), channel_id=1, source_target_pairs={{0,4},{4,0},{8,12},{12,8},{16,20},{20,16},{24,28},{28,24},{1,5},{5... | collective-permute-start | bytes 221192 | tf_op jit(solution)/shard_map/ppermute | solution.py:581
  23.7 0.3 collective-permute-start.8
  24.0 2.8 %collective-permute-done.7.refs_0_ = bf16[144,256]{1,0:T(8,128)(2,1)S(1)} collective-permute-done((bf16[144,256]{1,0:T(8,128)(2,1)S(1)}, bf16[144,256]{1,0:T(8,128)(2,1)S(1)}, u32[]{:S(2)}, u32[]{:S(2)}) %collective-permute-start.7) | collective-permute-done | bytes 73760 | tf_op jit(solution)/shard_map/ppermute | solution.py:581
  26.8 1.3 %collective-permute-done.8.refs_1_ = bf16[144,256]{1,0:T(8,128)(2,1)S(1)} collective-permute-done((bf16[144,256]{1,0:T(8,128)(2,1)S(1)}, bf16[144,256]{1,0:T(8,128)(2,1)S(1)}, u32[]{:S(2)}, u32[]{:S(2)}) %collective-permute-start.8) | collective-permute-done | bytes 73760 | tf_op jit(solution)/shard_map/ppermute | solution.py:581
  28.1 0.0 collective-permute-done.9.refs_2_
  28.1 0.1 merge.1
  28.2 4.3 %collective-permute-start.10 = (bf16[160,256]{1,0:T(8,128)(2,1)S(1)}, bf16[160,256]{1,0:T(8,128)(2,1)S(1)}, u32[]{:S(2)}, u32[]{:S(2)}) collective-permute-start(bf16[160,256]{1,0:T(8,128)(2,1)S(1)} %get-tuple-element.38), channel_id=1, source_target_pairs={{0,16},{4,20},{8,24},{12,28},{16,0},{20,4},{24,8},{28,12},{1,17},{... | collective-permute-start | bytes 245768 | tf_op jit(solution)/shard_map/ppermute | solution.py:581
  32.4 0.6 %collective-permute-start.11 = (bf16[80,256]{1,0:T(8,128)(2,1)S(1)}, bf16[80,256]{1,0:T(8,128)(2,1)S(1)}, u32[]{:S(2)}, u32[]{:S(2)}) collective-permute-start(bf16[80,256]{1,0:T(8,128)(2,1)S(1)} %get-tuple-element.39), channel_id=1, source_target_pairs={{0,4},{4,0},{8,12},{12,8},{16,20},{20,16},{24,28},{28,24},{1,5},{5... | collective-permute-start | bytes 122888 | tf_op jit(solution)/shard_map/ppermute | solution.py:581
  33.0 0.4 %collective-permute-start.13 = (bf16[80,256]{1,0:T(8,128)(2,1)S(1)}, bf16[80,256]{1,0:T(8,128)(2,1)S(1)}, u32[]{:S(2)}, u32[]{:S(2)}) collective-permute-start(bf16[80,256]{1,0:T(8,128)(2,1)S(1)} %get-tuple-element.41), channel_id=1, source_target_pairs={{0,12},{4,8},{8,4},{12,0},{16,28},{20,24},{24,20},{28,16},{1,13},{... | collective-permute-start | bytes 122888 | tf_op jit(solution)/shard_map/ppermute | solution.py:581
  33.4 2.5 %collective-permute-start.12 = (bf16[64,256]{1,0:T(8,128)(2,1)S(1)}, bf16[64,256]{1,0:T(8,128)(2,1)S(1)}, u32[]{:S(2)}, u32[]{:S(2)}) collective-permute-start(bf16[64,256]{1,0:T(8,128)(2,1)S(1)} %get-tuple-element.40), channel_id=1, source_target_pairs={{0,8},{4,12},{8,0},{12,4},{16,24},{20,28},{24,16},{28,20},{1,9},{5... | collective-permute-start | bytes 98312 | tf_op jit(solution)/shard_map/ppermute | solution.py:581
  35.9 0.0 collective-permute-done.10.far_ref
  35.9 0.0 collective-permute-start.16
  35.9 1.6 %collective-permute-start.15 = (f32[3,3,128]{2,1,0:T(4,128)S(1)}, f32[3,3,128]{2,1,0:T(4,128)S(1)}, u32[]{:S(2)}, u32[]{:S(2)}) collective-permute-start(f32[3,3,128]{2,1,0:T(4,128)S(1)} %sums.1), channel_id=1, source_target_pairs={{0,2},{1,3},{2,0},{3,1},{4,6},{5,7},{6,4},{7,5},{8,10},{9,11},{10,... | collective-permute-start | bytes 13832 | tf_op jit(solution)/shard_map/ppermute | solution.py:696
  37.5 0.7 %collective-permute-done.12.refs_1_ = bf16[64,256]{1,0:T(8,128)(2,1)S(1)} collective-permute-done((bf16[64,256]{1,0:T(8,128)(2,1)S(1)}, bf16[64,256]{1,0:T(8,128)(2,1)S(1)}, u32[]{:S(2)}, u32[]{:S(2)}) %collective-permute-start.12) | collective-permute-done | bytes 32800 | tf_op jit(solution)/shard_map/ppermute | solution.py:581
  38.3 0.0 collective-permute-start.14
  38.3 0.0 collective-permute-done.11.refs_0_
  38.3 0.0 collective-permute-done.13.refs_2_
  38.3 1.3 %finish.1 = (f32[2,64,1024]{2,1,0:T(8,128)}, f32[2,64,128]{2,1,0:T(8,128)}, f32[2,64,128]{2,1,0:T(8,128)}) custom-call(s32[8]{0:T(128)S(1)} %copy-done.1, f32[3,3,128]{2,1,0:T(4,128)S(1)} %copy-done, f32[2,64,1024]{2,1,0:T(8,128)} %get-tuple-element.30.dq_in_hbm, f32[2,8,1024]{2,1,0:T(8,128)S(1)} %get-tuple-element.31.tail_ref, ...), custom_call_target="tpu_custom_call", output_to_operand_aliasing={{0}: (2, {})} | custom-call | tf_op jit(solution)/shard_map/finish/pallas_call | solution.py:698
  39.6 0.0 collective-permute-done.16
  39.6 0.1 collective-permute-done.15
  39.6 0.0 collective-permute-done.14
  39.6 0.6 %add_add_fusion = f32[3,3,128]{2,1,0:T(4,128)} fusion(f32[3,3,128]{2,1,0:T(4,128)S(1)} %collective-permute-done.15, f32[3,3,128]{2,1,0:T(4,128)S(1)} %collective-permute-done.16, f32[3,3,128]{2,1,0:T(4,128)S(1)} %sums.1, f32[3,3,128]{2,1,0:T(4,128)S(1)} %collective-permute-done.14), kind=kLoop, calls=%fused_computation | loop fusion | flops 3456 | bytes 23040 | tf_op jit(solution)/shard_map/add | solution.py:719
  (1 shorter events, 0.0 us)
Async XLA Ops:
  0.6 13.7 %copy-start.1 = (s32[8]{0:T(128)S(1)}, s32[8]{0:T(128)}, u32[]{:S(2)}) copy-start(s32[8]{0:T(128)} %lengths_ref.5) | copy-start | bytes 100
  0.6 13.7 %copy-start = (f32[3,3,128]{2,1,0:T(4,128)S(1)}, f32[3,3,128]{2,1,0:T(4,128)}, u32[]{:S(2)}) copy-start(f32[3,3,128]{2,1,0:T(4,128)} %filters_ref.5) | copy-start | bytes 13828
  1.6 7.6 %collective-permute-start.3 = (bf16[144,256]{1,0:T(8,128)(2,1)S(1)}, bf16[144,256]{1,0:T(8,128)(2,1)S(1)}, u32[]{:S(2)}, u32[]{:S(2)}) collective-permute-start(bf16[144,256]{1,0:T(8,128)(2,1)S(1)} %pack.1.own_ref.refs_5_), channel_id=1, source_target_pairs={{0,16},{4,20},{8,24},{12,28},{16,0},{20,4},{24,8},{28,12},{1,17},{... | collective-permute-start | bytes 221192 | tf_op jit(solution)/shard_map/ppermute | solution.py:581
  5.7 6.7 %collective-permute-start.2 = (bf16[144,256]{1,0:T(8,128)(2,1)S(1)}, bf16[144,256]{1,0:T(8,128)(2,1)S(1)}, u32[]{:S(2)}, u32[]{:S(2)}) collective-permute-start(bf16[144,256]{1,0:T(8,128)(2,1)S(1)} %pack.1.own_ref.refs_5_), channel_id=1, source_target_pairs={{0,12},{4,8},{8,4},{12,0},{16,28},{20,24},{24,20},{28,16},{1,13},{... | collective-permute-start | bytes 221192 | tf_op jit(solution)/shard_map/ppermute | solution.py:581
  8.2 5.2 %collective-permute-start.1 = (bf16[144,256]{1,0:T(8,128)(2,1)S(1)}, bf16[144,256]{1,0:T(8,128)(2,1)S(1)}, u32[]{:S(2)}, u32[]{:S(2)}) collective-permute-start(bf16[144,256]{1,0:T(8,128)(2,1)S(1)} %pack.1.own_ref.refs_5_), channel_id=1, source_target_pairs={{0,8},{4,12},{8,0},{12,4},{16,24},{20,28},{24,16},{28,20},{1,9},{5... | collective-permute-start | bytes 221192 | tf_op jit(solution)/shard_map/ppermute | solution.py:581
  8.6 5.7 %collective-permute-start = (bf16[144,256]{1,0:T(8,128)(2,1)S(1)}, bf16[144,256]{1,0:T(8,128)(2,1)S(1)}, u32[]{:S(2)}, u32[]{:S(2)}) collective-permute-start(bf16[144,256]{1,0:T(8,128)(2,1)S(1)} %pack.1.own_ref.refs_5_), channel_id=1, source_target_pairs={{0,4},{4,0},{8,12},{12,8},{16,20},{20,16},{24,28},{28,24},{1,5},{5... | collective-permute-start | bytes 221192 | tf_op jit(solution)/shard_map/ppermute | solution.py:581
  9.2 7.0 %collective-permute-start.6 = (bf16[144,256]{1,0:T(8,128)(2,1)S(1)}, bf16[144,256]{1,0:T(8,128)(2,1)S(1)}, u32[]{:S(2)}, u32[]{:S(2)}) collective-permute-start(bf16[144,256]{1,0:T(8,128)(2,1)S(1)} %collective-permute-done.3.refs_6_), channel_id=1, source_target_pairs={{0,12},{4,8},{8,4},{12,0},{16,28},{20,24},{24,20},{28,16},{1,13},{... | collective-permute-start | bytes 221192 | tf_op jit(solution)/shard_map/ppermute | solution.py:581
  11.7 4.5 %collective-permute-start.5 = (bf16[144,256]{1,0:T(8,128)(2,1)S(1)}, bf16[144,256]{1,0:T(8,128)(2,1)S(1)}, u32[]{:S(2)}, u32[]{:S(2)}) collective-permute-start(bf16[144,256]{1,0:T(8,128)(2,1)S(1)} %collective-permute-done.3.refs_6_), channel_id=1, source_target_pairs={{0,8},{4,12},{8,0},{12,4},{16,24},{20,28},{24,16},{28,20},{1,9},{5... | collective-permute-start | bytes 221192 | tf_op jit(solution)/shard_map/ppermute | solution.py:581
  12.4 4.4 %collective-permute-start.4 = (bf16[144,256]{1,0:T(8,128)(2,1)S(1)}, bf16[144,256]{1,0:T(8,128)(2,1)S(1)}, u32[]{:S(2)}, u32[]{:S(2)}) collective-permute-start(bf16[144,256]{1,0:T(8,128)(2,1)S(1)} %collective-permute-done.3.refs_6_), channel_id=1, source_target_pairs={{0,4},{4,0},{8,12},{12,8},{16,20},{20,16},{24,28},{28,24},{1,5},{5... | collective-permute-start | bytes 221192 | tf_op jit(solution)/shard_map/ppermute | solution.py:581
  20.5 7.6 %collective-permute-start.9 = (bf16[160,256]{1,0:T(8,128)(2,1)S(1)}, bf16[160,256]{1,0:T(8,128)(2,1)S(1)}, u32[]{:S(2)}, u32[]{:S(2)}) collective-permute-start(bf16[160,256]{1,0:T(8,128)(2,1)S(1)} %get-tuple-element.36), channel_id=1, source_target_pairs={{0,12},{4,8},{8,4},{12,0},{16,28},{20,24},{24,20},{28,16},{1,13},{... | collective-permute-start | bytes 245768 | tf_op jit(solution)/shard_map/ppermute | solution.py:581
  21.8 5.0 %collective-permute-start.7 = (bf16[144,256]{1,0:T(8,128)(2,1)S(1)}, bf16[144,256]{1,0:T(8,128)(2,1)S(1)}, u32[]{:S(2)}, u32[]{:S(2)}) collective-permute-start(bf16[144,256]{1,0:T(8,128)(2,1)S(1)} %get-tuple-element.34), channel_id=1, source_target_pairs={{0,4},{4,0},{8,12},{12,8},{16,20},{20,16},{24,28},{28,24},{1,5},{5... | collective-permute-start | bytes 221192 | tf_op jit(solution)/shard_map/ppermute | solution.py:581
  23.7 4.4 %collective-permute-start.8 = (bf16[144,256]{1,0:T(8,128)(2,1)S(1)}, bf16[144,256]{1,0:T(8,128)(2,1)S(1)}, u32[]{:S(2)}, u32[]{:S(2)}) collective-permute-start(bf16[144,256]{1,0:T(8,128)(2,1)S(1)} %get-tuple-element.35), channel_id=1, source_target_pairs={{0,8},{4,12},{8,0},{12,4},{16,24},{20,28},{24,16},{28,20},{1,9},{5... | collective-permute-start | bytes 221192 | tf_op jit(solution)/shard_map/ppermute | solution.py:581
  28.2 7.8 %collective-permute-start.10 = (bf16[160,256]{1,0:T(8,128)(2,1)S(1)}, bf16[160,256]{1,0:T(8,128)(2,1)S(1)}, u32[]{:S(2)}, u32[]{:S(2)}) collective-permute-start(bf16[160,256]{1,0:T(8,128)(2,1)S(1)} %get-tuple-element.38), channel_id=1, source_target_pairs={{0,16},{4,20},{8,24},{12,28},{16,0},{20,4},{24,8},{28,12},{1,17},{... | collective-permute-start | bytes 245768 | tf_op jit(solution)/shard_map/ppermute | solution.py:581
  32.4 5.8 %collective-permute-start.11 = (bf16[80,256]{1,0:T(8,128)(2,1)S(1)}, bf16[80,256]{1,0:T(8,128)(2,1)S(1)}, u32[]{:S(2)}, u32[]{:S(2)}) collective-permute-start(bf16[80,256]{1,0:T(8,128)(2,1)S(1)} %get-tuple-element.39), channel_id=1, source_target_pairs={{0,4},{4,0},{8,12},{12,8},{16,20},{20,16},{24,28},{28,24},{1,5},{5... | collective-permute-start | bytes 122888 | tf_op jit(solution)/shard_map/ppermute | solution.py:581
  33.0 5.2 %collective-permute-start.13 = (bf16[80,256]{1,0:T(8,128)(2,1)S(1)}, bf16[80,256]{1,0:T(8,128)(2,1)S(1)}, u32[]{:S(2)}, u32[]{:S(2)}) collective-permute-start(bf16[80,256]{1,0:T(8,128)(2,1)S(1)} %get-tuple-element.41), channel_id=1, source_target_pairs={{0,12},{4,8},{8,4},{12,0},{16,28},{20,24},{24,20},{28,16},{1,13},{... | collective-permute-start | bytes 122888 | tf_op jit(solution)/shard_map/ppermute | solution.py:581
  33.4 4.8 %collective-permute-start.12 = (bf16[64,256]{1,0:T(8,128)(2,1)S(1)}, bf16[64,256]{1,0:T(8,128)(2,1)S(1)}, u32[]{:S(2)}, u32[]{:S(2)}) collective-permute-start(bf16[64,256]{1,0:T(8,128)(2,1)S(1)} %get-tuple-element.40), channel_id=1, source_target_pairs={{0,8},{4,12},{8,0},{12,4},{16,24},{20,28},{24,16},{28,20},{1,9},{5... | collective-permute-start | bytes 98312 | tf_op jit(solution)/shard_map/ppermute | solution.py:581
  35.9 3.6 %collective-permute-start.16 = (f32[3,3,128]{2,1,0:T(4,128)S(1)}, f32[3,3,128]{2,1,0:T(4,128)S(1)}, u32[]{:S(2)}, u32[]{:S(2)}) collective-permute-start(f32[3,3,128]{2,1,0:T(4,128)S(1)} %sums.1), channel_id=1, source_target_pairs={{0,3},{1,2},{2,1},{3,0},{4,7},{5,6},{6,5},{7,4},{8,11},{9,10},{10,... | collective-permute-start | bytes 13832 | tf_op jit(solution)/shard_map/ppermute | solution.py:696
  35.9 3.7 %collective-permute-start.15 = (f32[3,3,128]{2,1,0:T(4,128)S(1)}, f32[3,3,128]{2,1,0:T(4,128)S(1)}, u32[]{:S(2)}, u32[]{:S(2)}) collective-permute-start(f32[3,3,128]{2,1,0:T(4,128)S(1)} %sums.1), channel_id=1, source_target_pairs={{0,2},{1,3},{2,0},{3,1},{4,6},{5,7},{6,4},{7,5},{8,10},{9,11},{10,... | collective-permute-start | bytes 13832 | tf_op jit(solution)/shard_map/ppermute | solution.py:696
  38.3 1.4 %collective-permute-start.14 = (f32[3,3,128]{2,1,0:T(4,128)S(1)}, f32[3,3,128]{2,1,0:T(4,128)S(1)}, u32[]{:S(2)}, u32[]{:S(2)}) collective-permute-start(f32[3,3,128]{2,1,0:T(4,128)S(1)} %sums.1), channel_id=1, source_target_pairs={{0,1},{1,0},{2,3},{3,2},{4,5},{5,4},{6,7},{7,6},{8,9},{9,8},{10,11... | collective-permute-start | bytes 13832 | tf_op jit(solution)/shard_map/ppermute | solution.py:696
where the time goes:
time: 40.2 us
  starting transfers between devices  24.6 us (61%)
  Pallas kernels  7.8 us (19%)
  waiting for transfers between devices  6.47 us (16%)
  between operations  0.73 us (2%)
  other arithmetic  0.6 us (1%)
    ppermute x14, starting transfers between devices, flipped(): return lax.ppermute(array, 'ctx', [(i, i ^ flip) for i in range(ctx_count)])  23 us
    ppermute x14, waiting for transfers between devices, flipped(): return lax.ppermute(array, 'ctx', [(i, i ^ flip) for i in range(ctx_count)])  6.42 us
    pallas_call x1, Pallas kernels, shards(): pl.pallas_call(functools.partial(grads_kernel, ctx_count, direct), out_sh...  3.72 us
    pallas_call x1, Pallas kernels, shards(): pl.pallas_call(functools.partial(prep_kernel, ctx_count, direct), out_sha...  1.79 us
    ppermute x3, starting transfers between devices, shards(): lax.ppermute(sums, 'tp', [(i, i ^ flip) for i in range(count)])  1.59 us
    pallas_call x1, Pallas kernels, shards(): pl.pallas_call(functools.partial(finish_kernel, ctx_count, direct), out_s...  1.3 us
    pallas_call x1, Pallas kernels, shards(): pl.pallas_call(pack_kernel, grid=(1,), out_shape=jax.ShapeDtypeStruct((ms...  0.91 us
  transfers between devices with their start and end apart: 17, of which 7 were waited for; matrix products, arithmetic and copies ran while one was open for 0% of the time, Pallas kernels for 8%

commit v1 on v0

--- a/solution.py
+++ b/solution.py
@@ -65,6 +65,10 @@
             place = lax.rem(self.me, jnp.int32(self.refs[0].shape[0]))
             return self.refs[0].at[partner(place, flip)]
         return self.refs[flip]
+
+
+def splits(direct, flip, group):
+    return not direct or flip == group - 1
 
 
 def partner(me, flip):
@@ -107,7 +111,7 @@
         same_two_ref[rows] = jnp.ones((span, LANES), f32)
         return carry
 
-    loop(blocks, fill, 0)
+    lax.fori_loop(0, blocks, fill, 0, unroll=2)
     zeros = jnp.zeros((8, LANES), f32)
     for rows in (slice(0, 8), slice(8 + length, 16 + length)):
         same_ref[rows] = zeros
@@ -141,15 +145,21 @@
         rows = pl.ds(aligned(first_place[half] + 8, 8), span)
         one, two = same_ref[rows], same_two_ref[rows]
         for head in range(heads):
-            lanes = slice(head * LANES, (head + 1) * LANES)
             at = 2 * (head // 2)
             q_scr[half, head, 6:8] = rims[half][at : at + 2, (head % 2) * LANES : (head % 2 + 1) * LANES]
+
+        def convolve_head(head, carry, half=half, one=one, two=two):
+            lanes = pl.ds(pl.multiple_of(head * LANES, LANES), LANES)
+            target = pl.ds(pl.multiple_of(head * span, 16), span)
             q_scr[half, head, 8:] = q_ref[half, :, lanes].astype(f32)
             total = taps[0] * q_scr[half, head, 8:]
             total = total + one * (taps[1] * q_scr[half, head, 7 : 7 + span])
             total = total + two * (taps[2] * q_scr[half, head, 6 : 6 + span])
-            qc_ref[half, head * span : (head + 1) * span] = total.astype(bf16)
-            do_ref[half, head * span : (head + 1) * span] = d_out_ref[half, :, lanes]
+            qc_ref[half, target] = total.astype(bf16)
+            do_ref[half, target] = d_out_ref[half, :, lanes]
+            return carry
+
+        lax.fori_loop(0, heads, convolve_head, 0)
 
 
 def grads_kernel(ctx_count, direct, lengths_ref, filters_ref, *refs):
@@ -160,9 +170,9 @@
     near_in, far_in, refs = refs[:arrays], refs[arrays : 2 * arrays], refs[2 * arrays :]
     dq_hbm, dq_tail_ref, own_near_ref, own_far_ref = refs[:4]
     arrays = group - 1 if direct else 1
-    first_out, late_out, refs = refs[4 : 4 + arrays], refs[4 + arrays : 4 + 2 * arrays], refs[4 + 2 * arrays :]
+    first_out, late_out, refs = refs[4 : 4 + arrays], refs[4 + arrays : 5 + arrays], refs[5 + arrays :]
     kv_scr, conv_scr, dkv_scr, q_scr, qc_scr, dq_scr = refs[:6]
-    bias_scr, s_scr, dp_scr, dq_ref, sems = refs[6:]
+    bias_scr, s_scr, dp_scr, dq_ref, terms_scr, sems = refs[6:]
     f32, bf16 = jnp.float32, jnp.bfloat16
     span = own_ref.shape[0] // 2 - TAIL // 2
     heads = q_in_ref.shape[1]
@@ -173,7 +183,7 @@
     near_in = Slots((None,) + near_in if direct else near_in, me)
     far_in = Slots((None,) + far_in if direct else far_in, me)
     first_out = Slots((None,) + first_out if direct else first_out, me)
-    late_out = Slots((None,) + late_out if direct else late_out, me)
+    late_out = Slots((None,) * (group - 1) + late_out if direct else late_out, me)
     scale = LANES**-0.5
     log2_scale = scale * 1.4426950408889634
     starts = doc_starts(lengths_ref)
@@ -219,9 +229,31 @@
             conv_scr[tensor, pl.ds(aligned(base, 16), span)] = total.astype(bf16)
         return carry
 
-    loop(blocks, convolve_kv, 0)
-
     first_place = [me * span, (blocks - 1 - me) * span]
+    firsts = []
+    for half in range(2):
+        lowest = jnp.int32(0)
+        for start in starts[1:]:
+            lowest = jnp.where(first_place[half] >= start, start, lowest)
+        firsts.append(lowest // span)
+
+    def over_needed(body, init):
+        carry = lax.fori_loop(firsts[0], me + 1, body, init)
+        return lax.fori_loop(jnp.maximum(firsts[1], me + 1), blocks - me, body, carry)
+
+    def clear(index, carry):
+        for tensor in range(2):
+            rows = pl.ds(pl.multiple_of(index * span, 16), span)
+            conv_scr[tensor, rows] = jnp.zeros((span, LANES), bf16)
+            dkv_scr[tensor, rows] = jnp.zeros((span, LANES), f32)
+        terms_scr[index] = jnp.zeros((span, 2 * LANES), f32)
+        return carry
+
+    lax.fori_loop(0, blocks, clear, 0, unroll=2)
+    for tensor in range(2):
+        dkv_scr[tensor, length:] = zeros
+    over_needed(convolve_kv, 0)
+
     middle = me == ctx_count - 1
     q_scr[...] = q_in_ref[...]
     qc_scr[...] = qc_in_ref[...]
@@ -324,21 +356,9 @@
                 head = at * (wide // span) + part
                 dq_scr[half, head, :span] = dq[part * span : (part + 1) * span]
 
-    def clear(index, carry):
-        for tensor in range(2):
-            dkv_scr[tensor, pl.ds(aligned(index * span, 8), span)] = jnp.zeros((span, LANES), f32)
-        return carry
-
-    loop(blocks, clear, 0)
-    for tensor in range(2):
-        dkv_scr[tensor, length:] = zeros
-
     for half in range(2):
         widest = ctx_count + half
-        lowest = jnp.int32(0)
-        for start in starts[1:]:
-            lowest = jnp.where(first_place[half] >= start, start, lowest)
-        needed = first_place[half] // span - lowest // span + 1
+        needed = first_place[half] // span - firsts[half] + 1
         below = 0
         for count in [count for count in WINDOWS if direct and count < widest] + [widest]:
 
@@ -358,22 +378,27 @@
         ahead_one = same_scr[pl.ds(first_place[half] + 9, span)]
         ahead_two = same_two_scr[pl.ds(first_place[half] + 10, span)]
         zero_tap, one_tap, two_tap = taps(0)
-        for head in range(heads):
-            lanes = slice(head * LANES, (head + 1) * LANES)
+
+        def finish_head(head, carry, half=half, one=one, two=two, ahead_one=ahead_one, ahead_two=ahead_two):
+            lanes = pl.ds(pl.multiple_of(head * LANES, LANES), LANES)
             grads = dq_scr[half, head, :span]
             out = zero_tap * grads
             out = out + ahead_one * (one_tap * dq_scr[half, head, 1 : 1 + span])
             out = out + ahead_two * (two_tap * dq_scr[half, head, 2 : 2 + span])
             dq_ref[half, :, lanes] = out
             dq_tail_ref[half, :, lanes] = out[span - 8 :]
-            sums[0] += fold_rows(grads * q_scr[half, head, 8:])
-            sums[1] += fold_rows(grads * one * q_scr[half, head, 7 : 7 + span])
-            sums[2] += fold_rows(grads * two * q_scr[half, head, 6 : 6 + span])
+            return (
+                carry[0] + fold_rows(grads * q_scr[half, head, 8:]),
+                carry[1] + fold_rows(grads * one * q_scr[half, head, 7 : 7 + span]),
+                carry[2] + fold_rows(grads * two * q_scr[half, head, 6 : 6 + span]),
+            )
+
+        sums = lax.fori_loop(0, heads, finish_head, tuple(sums))
     q_sums = [jnp.sum(term, axis=0, keepdims=True) for term in sums]
     store = pltpu.make_async_copy(dq_ref, dq_hbm, sems.at[0])
     store.start()
 
-    def finish_block(index, carry, target, row):
+    def finish_block(index, carry):
         base = pl.multiple_of(index * span, 8)
         one, two = masks(base, 0)
         ahead_one = same_scr[pl.ds(base + 9, span)]
@@ -386,7 +411,7 @@
             out = out + ahead_one * (one_tap * dkv_scr[tensor, pl.ds(base + 1, span)])
             out = out + ahead_two * (two_tap * dkv_scr[tensor, pl.ds(base + 2, span)])
             lanes = slice(tensor * LANES, (tensor + 1) * LANES)
-            target[row : row + span, lanes] = out.astype(target.dtype)
+            terms_scr[index, :, lanes] = out
             at = 3 * tensor
             carry[at] += fold_rows(own * kv_scr[tensor, pl.ds(base + 8, span)])
             carry[at + 1] += fold_rows(own * one * kv_scr[tensor, pl.ds(base + 7, span)])
@@ -395,23 +420,27 @@
 
     low = me < group
 
-    def finish(step, carry):
+    kv_sums = over_needed(finish_block, (zeros,) * 6)
+    for target, index in ((own_far_ref, partner(me, group)), (own_near_ref, me)):
+        target[:span] = terms_scr[index]
+        target[span : 2 * span] = terms_scr[blocks - 1 - index]
+
+    def send(step, carry):
         flip = step + 1
         owner = partner(me, flip)
         far_owner = partner(me, flip + group)
         near_late = blocks - 1 - owner
         second = jnp.where(low, blocks - 1 - far_owner, owner)
         third = jnp.where(low & (me > owner), owner, near_late)
-        carry = finish_block(far_owner, carry, first_out[flip], 0)
-        carry = finish_block(second, carry, first_out[flip], span)
-        carry = finish_block(third, carry, late_out[flip], 0)
+        first_out[flip][:span] = terms_scr[far_owner].astype(bf16)
+        first_out[flip][span : 2 * span] = terms_scr[second].astype(bf16)
+        if splits(direct, flip, group):
+            late_out[flip][:span] = terms_scr[third].astype(bf16)
+        else:
+            first_out[flip][2 * span : 3 * span] = terms_scr[third].astype(bf16)
         return carry
 
-    kv_sums = (zeros,) * 6
-    for target, index in ((own_far_ref, partner(me, group)), (own_near_ref, me)):
-        kv_sums = finish_block(index, kv_sums, target, 0)
-        kv_sums = finish_block(blocks - 1 - index, kv_sums, target, span)
-    kv_sums = loop(group - 1, finish, kv_sums)
+    loop(group - 1, send, 0, 16 if direct else 1)
     kv_sums = [jnp.sum(term, axis=0, keepdims=True) for term in kv_sums]
 
     padding = [jnp.zeros((2, LANES), f32)]
@@ -432,11 +461,15 @@
     def store_rims(step, carry):
         flip = step + 1
         owner = partner(me, flip)
-        first_out[flip][2 * span : 2 * span + 16] = sums_pair
+        after = (2 if splits(direct, flip, group) else 3) * span
+        first_out[flip][after : after + 16] = sums_pair
         if not direct or flip == group - 1:
-            first_out[flip][2 * span + 16 :] = rim_for(partner(owner, group))
+            first_out[flip][after + 16 :] = rim_for(partner(owner, group))
         if not direct or flip & (flip + 1) == 0:
-            late_out[flip][span:] = rim_for(owner)
+            if splits(direct, flip, group):
+                late_out[flip][span:] = rim_for(owner)
+            else:
+                first_out[flip][after + 16 :] = rim_for(owner)
         return carry
 
     loop(group - 1, store_rims, 0, 16 if direct else 1)
@@ -444,7 +477,8 @@
 
 
 def merge_kernel(ctx_count, direct, own_near_ref, own_far_ref, *refs):
-    received_refs, (near_ref, far_ref, half_sums_ref, sums_scr) = refs[:-4], refs[-4:]
+    received_refs, refs = refs[:-6], refs[-6:]
+    near_ref, far_ref, half_sums_ref, rims_ref, sums_scr, rim_scr = refs
     f32, bf16 = jnp.float32, jnp.bfloat16
     group = ctx_count // 2
     me = lax.axis_index("ctx")
@@ -456,23 +490,34 @@
     sums_scr[place] = own_far_ref[rows:]
     def add(step, carry):
         flip = step + 1
+        source = partner(me, flip)
         message = received[flip]
         early, second = [message[at * span : (at + 1) * span].astype(f32) for at in range(2)]
-        near_early, far_early, far_late = carry
-        sums_scr[partner(place, flip)] = joined(message[rows : rows + 16])
+        near_early, near_late, far_early, far_late = carry
         zero = jnp.zeros_like(second)
-        return (
-            near_early + jnp.where(low, zero, second),
-            far_early + early,
-            far_late + jnp.where(low, second, zero),
-        )
-
-    init = (own_near_ref[:span], own_far_ref[:span], own_far_ref[span:rows])
+        after = (2 if splits(direct, flip, group) else 3) * span
+        sums_scr[partner(place, flip)] = joined(message[after : after + 16])
+        near_early = near_early + jnp.where(low, zero, second)
+        if not splits(direct, flip, group):
+            third = message[2 * span : 3 * span].astype(f32)
+            to_early = low & (source > me)
+            near_early = near_early + jnp.where(to_early, third, zero)
+            near_late = near_late + jnp.where(to_early, zero, third)
+            if flip & (flip + 1) == 0:
+                rim_scr[source] = joined(message[after + 16 :])
+        return near_early, near_late, far_early + early, far_late + jnp.where(low, second, zero)
+
+    neighbours = [jnp.minimum(me + 1, ctx_count - 1), jnp.maximum(me - 1, 0)]
+    for index in neighbours:
+        rim_scr[index] = jnp.zeros(rim_scr.shape[1:], f32)
+    init = (own_near_ref[:span], own_near_ref[span:], own_far_ref[:span], own_far_ref[span:rows])
     totals = loop(group - 1, add, init, 16 if direct else 1)
     near_ref[:span] = totals[0]
-    near_ref[span:] = own_near_ref[span:]
-    far_ref[:span] = totals[1].astype(bf16)
-    far_ref[span:rows] = totals[2].astype(bf16)
+    near_ref[span:] = totals[1]
+    far_ref[:span] = totals[2].astype(bf16)
+    far_ref[span:rows] = totals[3].astype(bf16)
+    for at, index in enumerate(neighbours):
+        rims_ref[at] = rim_scr[index]
     sums = loop(group, lambda index, carry: carry + sums_scr[index], jnp.zeros((8, 2 * LANES), f32))
     pair = jnp.concatenate(split_bits(sums), axis=0)
     half_sums_ref[...] = joined(pair)
@@ -488,7 +533,7 @@
 
 
 def finish_kernel(
-    ctx_count, direct, lengths_ref, filters_ref, dq_in_hbm, tail_ref, near_ref, far_ref, *refs
+    ctx_count, direct, lengths_ref, filters_ref, dq_in_hbm, tail_ref, near_ref, far_ref, rims_ref, *refs
 ):
     received_refs, refs = refs[:-8], refs[-8:]
     dq_hbm, dk_hbm, dv_hbm, dq_ref, dk_ref, dv_ref, rim_scr, sems = refs
@@ -497,12 +542,12 @@
     span = dk_ref.shape[1]
     me = lax.axis_index("ctx")
     low = me < group
-    received = Slots((None,) + received_refs if direct else received_refs, me)
+    received = Slots((None,) * (group - 1) + received_refs if direct else received_refs, me)
     starts = doc_starts(lengths_ref)
     blocks = 2 * ctx_count
     neighbours = [jnp.minimum(me + 1, ctx_count - 1), jnp.maximum(me - 1, 0)]
-    for index in neighbours:
-        rim_scr[index] = jnp.zeros(rim_scr.shape[1:], f32)
+    for at, index in enumerate(neighbours):
+        rim_scr[index] = rims_ref[at]
 
     def add(step, carry):
         flip = step + 1
@@ -516,7 +561,8 @@
         return carry[0] + jnp.where(to_early, terms, zero), carry[1] + jnp.where(to_early, zero, terms)
 
     total = near_ref[...] + far_ref[: 2 * span].astype(f32)
-    total = loop(group - 1, add, (total[:span], total[span:]), 16 if direct else 1)
+    total = (total[:span], total[span:])
+    total = add(group - 2, total) if direct else loop(group - 1, add, total, 1)
     for half in range(2):
         dk_ref[half] = total[half][:, :LANES]
         dv_ref[half] = total[half][:, LANES:]
@@ -611,8 +657,12 @@
     window = span * ctx_count + span
     if direct:
         flips = range(1, group)
-        first_shapes = [(2 * span + (32 if flip == group - 1 else 16), 2 * LANES) for flip in flips]
-        late_shapes = [(span + (16 if flip & (flip + 1) == 0 else 0), 2 * LANES) for flip in flips]
+        first_shapes = []
+        for flip in flips:
+            rows = (2 if splits(direct, flip, group) else 3) * span + 16
+            rows += 16 if flip == group - 1 or flip & (flip + 1) == 0 else 0
+            first_shapes.append((rows, 2 * LANES))
+        late_shapes = [(span + 16, 2 * LANES)]
     else:
         first_shapes = [(group, 2 * span + 32, 2 * LANES)]
         late_shapes = [(group, span + 16, 2 * LANES)]
@@ -651,6 +701,7 @@
         pltpu.VMEM((slots, window, 2 * LANES), f32),
         pltpu.VMEM((slots, window, 2 * LANES), f32),
         pltpu.VMEM(q_pre.shape, f32),
+        pltpu.VMEM((2 * ctx_count, span, 2 * LANES), f32),
         pltpu.SemaphoreType.DMA((1,)),
     ]
     own_shapes = [(2 * span, 2 * LANES), (2 * span + 8, 2 * LANES)]
@@ -670,18 +721,23 @@
         jax.ShapeDtypeStruct((2 * span, 2 * LANES), f32),
         jax.ShapeDtypeStruct((2 * span + 32, 2 * LANES), bf16),
         jax.ShapeDtypeStruct((8, 2 * LANES), f32),
+        jax.ShapeDtypeStruct((2, rim // 2, 2 * LANES), f32),
     ]
-    near, far, half_sums = pl.pallas_call(
+    near, far, half_sums, rims = pl.pallas_call(
         functools.partial(merge_kernel, ctx_count, direct),
         out_shape=merged_shapes,
         in_specs=[vmem] * (2 + len(half_terms)),
         out_specs=[vmem] * len(merged_shapes),
-        scratch_shapes=[pltpu.VMEM((group, 8, 2 * LANES), f32)],
+        scratch_shapes=[
+            pltpu.VMEM((group, 8, 2 * LANES), f32),
+            pltpu.VMEM((ctx_count, rim // 2, 2 * LANES), f32),
+        ],
         compiler_params=pltpu.CompilerParams(vmem_limit_bytes=(4 if direct else 40) * MIB),
         name="merge",
     )(own_near, own_far, *half_terms)
     from_half = flipped(far, group)
-    late_terms = delivered(sent[len(first_shapes) :])
+    late_terms = sent[len(first_shapes) :]
+    late_terms = [flipped(late_terms[0], group - 1)] if direct else delivered(late_terms)
 
     sums = pl.pallas_call(
         functools.partial(sums_kernel, span),
@@ -702,7 +758,7 @@
             jax.ShapeDtypeStruct(k_pre.shape, f32),
             jax.ShapeDtypeStruct(k_pre.shape, f32),
         ),
-        in_specs=[smem, vmem, hbm] + [vmem] * (3 + len(late_terms)),
+        in_specs=[smem, vmem, hbm] + [vmem] * (4 + len(late_terms)),
         out_specs=(hbm, hbm, hbm),
         scratch_shapes=[
             pltpu.VMEM((2, 8, width), f32),
@@ -714,7 +770,7 @@
         input_output_aliases={2: 0},
         compiler_params=pltpu.CompilerParams(vmem_limit_bytes=(4 if direct else 16) * MIB),
         name="finish",
-    )(doc_lengths, filters, d_q_main, d_q_tail, near, from_half, *late_terms)
+    )(doc_lengths, filters, d_q_main, d_q_tail, near, from_half, rims, *late_terms)
     while len(all_sums) > 1:
         all_sums = [all_sums[at] + all_sums[at + 1] for at in range(0, len(all_sums), 2)]
     return (d_q_pre, d_k_pre, d_v_pre, all_sums[0])

time: 40.2 us -> 39.5 us (0.983)
  starting transfers between devices: 24.6 us -> 20.8 us
  waiting for transfers between devices: 6.47 us -> 8.28 us
  Pallas kernels: 7.8 us -> 8.93 us
    ppermute x14 -> x12, starting transfers between devices: 23 us -> 18.9 us  [flipped(): return lax.ppermute(array, 'ctx', [(i, i ^ flip) for i in range(ctx_count)])]
    ppermute x14 -> x12, waiting for transfers between devices: 6.42 us -> 7.74 us  [flipped(): return lax.ppermute(array, 'ctx', [(i, i ^ flip) for i in range(ctx_count)])]
    pallas_call x1, Pallas kernels: 3.72 us -> 4.72 us  [shards(): pl.pallas_call(functools.partial(grads_kernel, ctx_count, direct), out_sh...]
    ppermute x3, waiting for transfers between devices: 0.06 us -> 0.54 us  [shards(): lax.ppermute(sums, 'tp', [(i, i ^ flip) for i in range(count)])]
  transfers between devices with their start and end apart: 17 -> 15, of which waited for: 7 -> 6; matrix products, arithmetic and copies ran while one was open for 0% -> 0% of each run, Pallas kernels for 8% -> 8%
where the time goes in v1:
time: 39.5 us; the launch traced here: 39.3 us
  starting transfers between devices  20.8 us (53%)
  Pallas kernels  8.93 us (23%)
  waiting for transfers between devices  8.28 us (21%)
  between operations  0.72 us (2%)
  other arithmetic  0.6 us (2%)
    ppermute x12, starting transfers between devices, flipped(): return lax.ppermute(array, 'ctx', [(i, i ^ flip) for i in range(ctx_count)])  18.9 us
    ppermute x12, waiting for transfers between devices, flipped(): return lax.ppermute(array, 'ctx', [(i, i ^ flip) for i in range(ctx_count)])  7.74 us
    pallas_call x1, Pallas kernels, shards(): pl.pallas_call(functools.partial(grads_kernel, ctx_count, direct), out_sh...  4.72 us
    pallas_call x1, Pallas kernels, shards(): pl.pallas_call(functools.partial(prep_kernel, ctx_count, direct), out_sha...  1.91 us
    ppermute x3, starting transfers between devices, shards(): lax.ppermute(sums, 'tp', [(i, i ^ flip) for i in range(count)])  1.86 us
    pallas_call x1, Pallas kernels, shards(): pl.pallas_call(functools.partial(finish_kernel, ctx_count, direct), out_s...  1.27 us
    pallas_call x1, Pallas kernels, shards(): pl.pallas_call(pack_kernel, grid=(1,), out_shape=jax.ShapeDtypeStruct((ms...  0.91 us
  transfers between devices with their start and end apart: 15, of which 6 were waited for; matrix products, arithmetic and copies ran while one was open for 0% of the time, Pallas kernels for 8%

profile of v1, /device:TPU:0, one launch (start us, length us, event | category | flops | bytes accessed | tf_op | source)
XLA Modules:
  0.0 39.3 jit_solution(4780410498055013719)
XLA Ops:
  0.6 0.0 copy-start.1
  0.6 0.0 copy-start
  0.7 0.9 %pack.1.own_ref.refs_5_ = bf16[144,256]{1,0:T(8,128)(2,1)S(1)} custom-call(bf16[2,64,128]{2,1,0:T(8,128)(2,1)} %k_ref.1, bf16[2,64,128]{2,1,0:T(8,128)(2,1)} %v_ref.1, bf16[2,64,1024]{2,1,0:T(8,128)(2,1)} %q_hbm.1), custom_call_target="tpu_custom_call" | custom-call | tf_op jit(solution)/shard_map/pack/pallas_call | solution.py:639
  1.6 4.1 %collective-permute-start.3 = (bf16[144,256]{1,0:T(8,128)(2,1)S(1)}, bf16[144,256]{1,0:T(8,128)(2,1)S(1)}, u32[]{:S(2)}, u32[]{:S(2)}) collective-permute-start(bf16[144,256]{1,0:T(8,128)(2,1)S(1)} %pack.1.own_ref.refs_5_), channel_id=1, source_target_pairs={{0,16},{4,20},{8,24},{12,28},{16,0},{20,4},{24,8},{28,12},{1,17},{... | collective-permute-start | bytes 221192 | tf_op jit(solution)/shard_map/ppermute | solution.py:627
  5.7 2.5 %collective-permute-start.2 = (bf16[144,256]{1,0:T(8,128)(2,1)S(1)}, bf16[144,256]{1,0:T(8,128)(2,1)S(1)}, u32[]{:S(2)}, u32[]{:S(2)}) collective-permute-start(bf16[144,256]{1,0:T(8,128)(2,1)S(1)} %pack.1.own_ref.refs_5_), channel_id=1, source_target_pairs={{0,12},{4,8},{8,4},{12,0},{16,28},{20,24},{24,20},{28,16},{1,13},{... | collective-permute-start | bytes 221192 | tf_op jit(solution)/shard_map/ppermute | solution.py:627
  8.2 0.4 %collective-permute-start.1 = (bf16[144,256]{1,0:T(8,128)(2,1)S(1)}, bf16[144,256]{1,0:T(8,128)(2,1)S(1)}, u32[]{:S(2)}, u32[]{:S(2)}) collective-permute-start(bf16[144,256]{1,0:T(8,128)(2,1)S(1)} %pack.1.own_ref.refs_5_), channel_id=1, source_target_pairs={{0,8},{4,12},{8,0},{12,4},{16,24},{20,28},{24,16},{28,20},{1,9},{5... | collective-permute-start | bytes 221192 | tf_op jit(solution)/shard_map/ppermute | solution.py:627
  8.6 0.5 %collective-permute-start = (bf16[144,256]{1,0:T(8,128)(2,1)S(1)}, bf16[144,256]{1,0:T(8,128)(2,1)S(1)}, u32[]{:S(2)}, u32[]{:S(2)}) collective-permute-start(bf16[144,256]{1,0:T(8,128)(2,1)S(1)} %pack.1.own_ref.refs_5_), channel_id=1, source_target_pairs={{0,4},{4,0},{8,12},{12,8},{16,20},{20,16},{24,28},{28,24},{1,5},{5... | collective-permute-start | bytes 221192 | tf_op jit(solution)/shard_map/ppermute | solution.py:627
  9.2 0.0 collective-permute-done.3.refs_6_
  9.2 2.5 %collective-permute-start.6 = (bf16[144,256]{1,0:T(8,128)(2,1)S(1)}, bf16[144,256]{1,0:T(8,128)(2,1)S(1)}, u32[]{:S(2)}, u32[]{:S(2)}) collective-permute-start(bf16[144,256]{1,0:T(8,128)(2,1)S(1)} %collective-permute-done.3.refs_6_), channel_id=1, source_target_pairs={{0,12},{4,8},{8,4},{12,0},{16,28},{20,24},{24,20},{28,16},{1,13},{... | collective-permute-start | bytes 221192 | tf_op jit(solution)/shard_map/ppermute | solution.py:627
  11.7 0.7 %collective-permute-start.5 = (bf16[144,256]{1,0:T(8,128)(2,1)S(1)}, bf16[144,256]{1,0:T(8,128)(2,1)S(1)}, u32[]{:S(2)}, u32[]{:S(2)}) collective-permute-start(bf16[144,256]{1,0:T(8,128)(2,1)S(1)} %collective-permute-done.3.refs_6_), channel_id=1, source_target_pairs={{0,8},{4,12},{8,0},{12,4},{16,24},{20,28},{24,16},{28,20},{1,9},{5... | collective-permute-start | bytes 221192 | tf_op jit(solution)/shard_map/ppermute | solution.py:627
  12.4 0.0 collective-permute-done.2.refs_2_.refs_9_
  12.4 0.9 %collective-permute-start.4 = (bf16[144,256]{1,0:T(8,128)(2,1)S(1)}, bf16[144,256]{1,0:T(8,128)(2,1)S(1)}, u32[]{:S(2)}, u32[]{:S(2)}) collective-permute-start(bf16[144,256]{1,0:T(8,128)(2,1)S(1)} %collective-permute-done.3.refs_6_), channel_id=1, source_target_pairs={{0,4},{4,0},{8,12},{12,8},{16,20},{20,16},{24,28},{28,24},{1,5},{5... | collective-permute-start | bytes 221192 | tf_op jit(solution)/shard_map/ppermute | solution.py:627
  13.3 0.1 collective-permute-done.1.refs_1_.refs_8_
  13.4 0.9 %collective-permute-done.refs_0_.refs_7_ = bf16[144,256]{1,0:T(8,128)(2,1)S(1)} collective-permute-done((bf16[144,256]{1,0:T(8,128)(2,1)S(1)}, bf16[144,256]{1,0:T(8,128)(2,1)S(1)}, u32[]{:S(2)}, u32[]{:S(2)}) %collective-permute-start) | collective-permute-done | bytes 73760 | tf_op jit(solution)/shard_map/ppermute | solution.py:627
  14.3 0.0 copy-done.1
  14.3 0.0 copy-done
  14.3 1.9 %prep.1 = (f32[1040,128]{1,0:T(8,128)S(1)}, f32[1040,128]{1,0:T(8,128)S(1)}, f32[2,8,72,128]{3,2,1,0:T(8,128)S(1)}, bf16[2,512,128]{2,1,0:T(8,128)(2,1)S(1)}, bf16[2,512,128]{2,1,0:T(8,128)(2,1)S(1)}) custom-call(s32[8]{0:T(128)S(1)} %copy-done.1, f32[3,3,128]{2,1,0:T(4,128)S(1)} %copy-done, bf16[2,64,1024]{2,1,0:T(8,128)(2,1)} %q_hbm.1, ...), custom_call_target="tpu_custom_call" | custom-call | tf_op jit(solution)/shard_map/prep/pallas_call | solution.py:673
  16.2 0.0 collective-permute-done.6.refs_12_
  16.2 0.0 collective-permute-done.5.refs_11_
  16.2 0.5 %collective-permute-done.4.refs_10_ = bf16[144,256]{1,0:T(8,128)(2,1)S(1)} collective-permute-done((bf16[144,256]{1,0:T(8,128)(2,1)S(1)}, bf16[144,256]{1,0:T(8,128)(2,1)S(1)}, u32[]{:S(2)}, u32[]{:S(2)}) %collective-permute-start.4) | collective-permute-done | bytes 73760 | tf_op jit(solution)/shard_map/ppermute | solution.py:627
  16.7 4.7 %grads.1 = (f32[2,64,1024]{2,1,0:T(8,128)}, f32[2,8,1024]{2,1,0:T(8,128)S(1)}, f32[128,256]{1,0:T(8,128)S(1)}, f32[136,256]{1,0:T(8,128)S(1)}, bf16[224,256]{1,0...) custom-call(s32[8]{0:T(128)S(1)} %copy-done.1, ...), custom_call_target="tpu_custom_call" | custom-call | tf_op jit(solution)/shard_map/grads/pallas_call | solution.py:708
  21.5 1.0 %collective-permute-start.7 = (bf16[224,256]{1,0:T(8,128)(2,1)S(1)}, bf16[224,256]{1,0:T(8,128)(2,1)S(1)}, u32[]{:S(2)}, u32[]{:S(2)}) collective-permute-start(bf16[224,256]{1,0:T(8,128)(2,1)S(1)} %get-tuple-element.33), channel_id=1, source_target_pairs={{0,4},{4,0},{8,12},{12,8},{16,20},{20,16},{24,28},{28,24},{1,5},{5... | collective-permute-start | bytes 344072 | tf_op jit(solution)/shard_map/ppermute | solution.py:627
  22.4 0.8 %collective-permute-start.8 = (bf16[208,256]{1,0:T(8,128)(2,1)S(1)}, bf16[208,256]{1,0:T(8,128)(2,1)S(1)}, u32[]{:S(2)}, u32[]{:S(2)}) collective-permute-start(bf16[208,256]{1,0:T(8,128)(2,1)S(1)} %get-tuple-element.34), channel_id=1, source_target_pairs={{0,8},{4,12},{8,0},{12,4},{16,24},{20,28},{24,16},{28,20},{1,9},{5... | collective-permute-start | bytes 319496 | tf_op jit(solution)/shard_map/ppermute | solution.py:627
  23.2 1.8 %collective-permute-start.9 = (bf16[160,256]{1,0:T(8,128)(2,1)S(1)}, bf16[160,256]{1,0:T(8,128)(2,1)S(1)}, u32[]{:S(2)}, u32[]{:S(2)}) collective-permute-start(bf16[160,256]{1,0:T(8,128)(2,1)S(1)} %get-tuple-element.35), channel_id=1, source_target_pairs={{0,12},{4,8},{8,4},{12,0},{16,28},{20,24},{24,20},{28,16},{1,13},{... | collective-permute-start | bytes 245768 | tf_op jit(solution)/shard_map/ppermute | solution.py:627
  25.0 3.6 %collective-permute-done.9.refs_2_ = bf16[160,256]{1,0:T(8,128)(2,1)S(1)} collective-permute-done((bf16[160,256]{1,0:T(8,128)(2,1)S(1)}, bf16[160,256]{1,0:T(8,128)(2,1)S(1)}, u32[]{:S(2)}, u32[]{:S(2)}) %collective-permute-start.9) | collective-permute-done | bytes 81952 | tf_op jit(solution)/shard_map/ppermute | solution.py:627
  28.6 0.0 collective-permute-done.8.refs_1_
  28.6 0.0 collective-permute-done.7.refs_0_
  28.6 0.1 merge.1
  28.7 2.6 %collective-permute-start.10 = (bf16[160,256]{1,0:T(8,128)(2,1)S(1)}, bf16[160,256]{1,0:T(8,128)(2,1)S(1)}, u32[]{:S(2)}, u32[]{:S(2)}) collective-permute-start(bf16[160,256]{1,0:T(8,128)(2,1)S(1)} %get-tuple-element.37), channel_id=1, source_target_pairs={{0,16},{4,20},{8,24},{12,28},{16,0},{20,4},{24,8},{28,12},{1,17},{... | collective-permute-start | bytes 245768 | tf_op jit(solution)/shard_map/ppermute | solution.py:627
  31.4 1.0 %collective-permute-start.11 = (bf16[80,256]{1,0:T(8,128)(2,1)S(1)}, bf16[80,256]{1,0:T(8,128)(2,1)S(1)}, u32[]{:S(2)}, u32[]{:S(2)}) collective-permute-start(bf16[80,256]{1,0:T(8,128)(2,1)S(1)} %get-tuple-element.39), channel_id=1, source_target_pairs={{0,12},{4,8},{8,4},{12,0},{16,28},{20,24},{24,20},{28,16},{1,13},{... | collective-permute-start | bytes 122888 | tf_op jit(solution)/shard_map/ppermute | solution.py:627
  32.3 2.7 %collective-permute-done.10.far_ref = bf16[160,256]{1,0:T(8,128)(2,1)S(1)} collective-permute-done((bf16[160,256]{1,0:T(8,128)(2,1)S(1)}, bf16[160,256]{1,0:T(8,128)(2,1)S(1)}, u32[]{:S(2)}, u32[]{:S(2)}) %collective-permute-start.10) | collective-permute-done | bytes 81952 | tf_op jit(solution)/shard_map/ppermute | solution.py:627
  35.0 0.0 collective-permute-start.14
  35.0 1.6 %collective-permute-start.13 = (f32[3,3,128]{2,1,0:T(4,128)S(1)}, f32[3,3,128]{2,1,0:T(4,128)S(1)}, u32[]{:S(2)}, u32[]{:S(2)}) collective-permute-start(f32[3,3,128]{2,1,0:T(4,128)S(1)} %sums.1), channel_id=1, source_target_pairs={{0,2},{1,3},{2,0},{3,1},{4,6},{5,7},{6,4},{7,5},{8,10},{9,11},{10,... | collective-permute-start | bytes 13832 | tf_op jit(solution)/shard_map/ppermute | solution.py:752
  36.6 0.3 collective-permute-start.12
  36.9 0.0 collective-permute-done.11.refs_0_
  36.9 1.3 %finish.1 = (f32[2,64,1024]{2,1,0:T(8,128)}, f32[2,64,128]{2,1,0:T(8,128)}, f32[2,64,128]{2,1,0:T(8,128)}) custom-call(s32[8]{0:T(128)S(1)} %copy-done.1, f32[3,3,128]{2,1,0:T(4,128)S(1)} %copy-done, f32[2,64,1024]{2,1,0:T(8,128)} %get-tuple-element.29.dq_in_hbm, f32[2,8,1024]{2,1,0:T(8,128)S(1)} %get-tuple-element.30.tail_ref, ...), custom_call_target="tpu_custom_call", output_to_operand_aliasing={{0}: (2, {})} | custom-call | tf_op jit(solution)/shard_map/finish/pallas_call | solution.py:754
  38.1 0.0 collective-permute-done.14
  38.1 0.5 %collective-permute-done.13 = f32[3,3,128]{2,1,0:T(4,128)S(1)} collective-permute-done((f32[3,3,128]{2,1,0:T(4,128)S(1)}, f32[3,3,128]{2,1,0:T(4,128)S(1)}, u32[]{:S(2)}, u32[]{:S(2)}) %collective-permute-start.13) | collective-permute-done | bytes 4640 | tf_op jit(solution)/shard_map/ppermute | solution.py:752
  38.7 0.0 collective-permute-done.12
  38.7 0.6 %add_add_fusion = f32[3,3,128]{2,1,0:T(4,128)} fusion(f32[3,3,128]{2,1,0:T(4,128)S(1)} %collective-permute-done.13, f32[3,3,128]{2,1,0:T(4,128)S(1)} %collective-permute-done.14, f32[3,3,128]{2,1,0:T(4,128)S(1)} %sums.1, f32[3,3,128]{2,1,0:T(4,128)S(1)} %collective-permute-done.12), kind=kLoop, calls=%fused_computation | loop fusion | flops 3456 | bytes 23040 | tf_op jit(solution)/shard_map/add | solution.py:775
  (1 shorter events, 0.0 us)
Async XLA Ops:
  0.6 13.7 %copy-start.1 = (s32[8]{0:T(128)S(1)}, s32[8]{0:T(128)}, u32[]{:S(2)}) copy-start(s32[8]{0:T(128)} %lengths_ref.5) | copy-start | bytes 100
  0.6 13.7 %copy-start = (f32[3,3,128]{2,1,0:T(4,128)S(1)}, f32[3,3,128]{2,1,0:T(4,128)}, u32[]{:S(2)}) copy-start(f32[3,3,128]{2,1,0:T(4,128)} %filters_ref.5) | copy-start | bytes 13828
  1.6 7.6 %collective-permute-start.3 = (bf16[144,256]{1,0:T(8,128)(2,1)S(1)}, bf16[144,256]{1,0:T(8,128)(2,1)S(1)}, u32[]{:S(2)}, u32[]{:S(2)}) collective-permute-start(bf16[144,256]{1,0:T(8,128)(2,1)S(1)} %pack.1.own_ref.refs_5_), channel_id=1, source_target_pairs={{0,16},{4,20},{8,24},{12,28},{16,0},{20,4},{24,8},{28,12},{1,17},{... | collective-permute-start | bytes 221192 | tf_op jit(solution)/shard_map/ppermute | solution.py:627
  5.7 6.7 %collective-permute-start.2 = (bf16[144,256]{1,0:T(8,128)(2,1)S(1)}, bf16[144,256]{1,0:T(8,128)(2,1)S(1)}, u32[]{:S(2)}, u32[]{:S(2)}) collective-permute-start(bf16[144,256]{1,0:T(8,128)(2,1)S(1)} %pack.1.own_ref.refs_5_), channel_id=1, source_target_pairs={{0,12},{4,8},{8,4},{12,0},{16,28},{20,24},{24,20},{28,16},{1,13},{... | collective-permute-start | bytes 221192 | tf_op jit(solution)/shard_map/ppermute | solution.py:627
  8.2 5.2 %collective-permute-start.1 = (bf16[144,256]{1,0:T(8,128)(2,1)S(1)}, bf16[144,256]{1,0:T(8,128)(2,1)S(1)}, u32[]{:S(2)}, u32[]{:S(2)}) collective-permute-start(bf16[144,256]{1,0:T(8,128)(2,1)S(1)} %pack.1.own_ref.refs_5_), channel_id=1, source_target_pairs={{0,8},{4,12},{8,0},{12,4},{16,24},{20,28},{24,16},{28,20},{1,9},{5... | collective-permute-start | bytes 221192 | tf_op jit(solution)/shard_map/ppermute | solution.py:627
  8.6 5.7 %collective-permute-start = (bf16[144,256]{1,0:T(8,128)(2,1)S(1)}, bf16[144,256]{1,0:T(8,128)(2,1)S(1)}, u32[]{:S(2)}, u32[]{:S(2)}) collective-permute-start(bf16[144,256]{1,0:T(8,128)(2,1)S(1)} %pack.1.own_ref.refs_5_), channel_id=1, source_target_pairs={{0,4},{4,0},{8,12},{12,8},{16,20},{20,16},{24,28},{28,24},{1,5},{5... | collective-permute-start | bytes 221192 | tf_op jit(solution)/shard_map/ppermute | solution.py:627
  9.2 7.1 %collective-permute-start.6 = (bf16[144,256]{1,0:T(8,128)(2,1)S(1)}, bf16[144,256]{1,0:T(8,128)(2,1)S(1)}, u32[]{:S(2)}, u32[]{:S(2)}) collective-permute-start(bf16[144,256]{1,0:T(8,128)(2,1)S(1)} %collective-permute-done.3.refs_6_), channel_id=1, source_target_pairs={{0,12},{4,8},{8,4},{12,0},{16,28},{20,24},{24,20},{28,16},{1,13},{... | collective-permute-start | bytes 221192 | tf_op jit(solution)/shard_map/ppermute | solution.py:627
  11.7 4.6 %collective-permute-start.5 = (bf16[144,256]{1,0:T(8,128)(2,1)S(1)}, bf16[144,256]{1,0:T(8,128)(2,1)S(1)}, u32[]{:S(2)}, u32[]{:S(2)}) collective-permute-start(bf16[144,256]{1,0:T(8,128)(2,1)S(1)} %collective-permute-done.3.refs_6_), channel_id=1, source_target_pairs={{0,8},{4,12},{8,0},{12,4},{16,24},{20,28},{24,16},{28,20},{1,9},{5... | collective-permute-start | bytes 221192 | tf_op jit(solution)/shard_map/ppermute | solution.py:627
  12.4 4.4 %collective-permute-start.4 = (bf16[144,256]{1,0:T(8,128)(2,1)S(1)}, bf16[144,256]{1,0:T(8,128)(2,1)S(1)}, u32[]{:S(2)}, u32[]{:S(2)}) collective-permute-start(bf16[144,256]{1,0:T(8,128)(2,1)S(1)} %collective-permute-done.3.refs_6_), channel_id=1, source_target_pairs={{0,4},{4,0},{8,12},{12,8},{16,20},{20,16},{24,28},{28,24},{1,5},{5... | collective-permute-start | bytes 221192 | tf_op jit(solution)/shard_map/ppermute | solution.py:627
  21.5 7.1 %collective-permute-start.7 = (bf16[224,256]{1,0:T(8,128)(2,1)S(1)}, bf16[224,256]{1,0:T(8,128)(2,1)S(1)}, u32[]{:S(2)}, u32[]{:S(2)}) collective-permute-start(bf16[224,256]{1,0:T(8,128)(2,1)S(1)} %get-tuple-element.33), channel_id=1, source_target_pairs={{0,4},{4,0},{8,12},{12,8},{16,20},{20,16},{24,28},{28,24},{1,5},{5... | collective-permute-start | bytes 344072 | tf_op jit(solution)/shard_map/ppermute | solution.py:627
  22.4 6.1 %collective-permute-start.8 = (bf16[208,256]{1,0:T(8,128)(2,1)S(1)}, bf16[208,256]{1,0:T(8,128)(2,1)S(1)}, u32[]{:S(2)}, u32[]{:S(2)}) collective-permute-start(bf16[208,256]{1,0:T(8,128)(2,1)S(1)} %get-tuple-element.34), channel_id=1, source_target_pairs={{0,8},{4,12},{8,0},{12,4},{16,24},{20,28},{24,16},{28,20},{1,9},{5... | collective-permute-start | bytes 319496 | tf_op jit(solution)/shard_map/ppermute | solution.py:627
  23.2 5.3 %collective-permute-start.9 = (bf16[160,256]{1,0:T(8,128)(2,1)S(1)}, bf16[160,256]{1,0:T(8,128)(2,1)S(1)}, u32[]{:S(2)}, u32[]{:S(2)}) collective-permute-start(bf16[160,256]{1,0:T(8,128)(2,1)S(1)} %get-tuple-element.35), channel_id=1, source_target_pairs={{0,12},{4,8},{8,4},{12,0},{16,28},{20,24},{24,20},{28,16},{1,13},{... | collective-permute-start | bytes 245768 | tf_op jit(solution)/shard_map/ppermute | solution.py:627
  28.7 6.3 %collective-permute-start.10 = (bf16[160,256]{1,0:T(8,128)(2,1)S(1)}, bf16[160,256]{1,0:T(8,128)(2,1)S(1)}, u32[]{:S(2)}, u32[]{:S(2)}) collective-permute-start(bf16[160,256]{1,0:T(8,128)(2,1)S(1)} %get-tuple-element.37), channel_id=1, source_target_pairs={{0,16},{4,20},{8,24},{12,28},{16,0},{20,4},{24,8},{28,12},{1,17},{... | collective-permute-start | bytes 245768 | tf_op jit(solution)/shard_map/ppermute | solution.py:627
  31.4 5.5 %collective-permute-start.11 = (bf16[80,256]{1,0:T(8,128)(2,1)S(1)}, bf16[80,256]{1,0:T(8,128)(2,1)S(1)}, u32[]{:S(2)}, u32[]{:S(2)}) collective-permute-start(bf16[80,256]{1,0:T(8,128)(2,1)S(1)} %get-tuple-element.39), channel_id=1, source_target_pairs={{0,12},{4,8},{8,4},{12,0},{16,28},{20,24},{24,20},{28,16},{1,13},{... | collective-permute-start | bytes 122888 | tf_op jit(solution)/shard_map/ppermute | solution.py:627
  35.0 3.1 %collective-permute-start.14 = (f32[3,3,128]{2,1,0:T(4,128)S(1)}, f32[3,3,128]{2,1,0:T(4,128)S(1)}, u32[]{:S(2)}, u32[]{:S(2)}) collective-permute-start(f32[3,3,128]{2,1,0:T(4,128)S(1)} %sums.1), channel_id=1, source_target_pairs={{0,3},{1,2},{2,1},{3,0},{4,7},{5,6},{6,5},{7,4},{8,11},{9,10},{10,... | collective-permute-start | bytes 13832 | tf_op jit(solution)/shard_map/ppermute | solution.py:752
  35.0 3.7 %collective-permute-start.13 = (f32[3,3,128]{2,1,0:T(4,128)S(1)}, f32[3,3,128]{2,1,0:T(4,128)S(1)}, u32[]{:S(2)}, u32[]{:S(2)}) collective-permute-start(f32[3,3,128]{2,1,0:T(4,128)S(1)} %sums.1), channel_id=1, source_target_pairs={{0,2},{1,3},{2,0},{3,1},{4,6},{5,7},{6,4},{7,5},{8,10},{9,11},{10,... | collective-permute-start | bytes 13832 | tf_op jit(solution)/shard_map/ppermute | solution.py:752
  36.6 2.1 %collective-permute-start.12 = (f32[3,3,128]{2,1,0:T(4,128)S(1)}, f32[3,3,128]{2,1,0:T(4,128)S(1)}, u32[]{:S(2)}, u32[]{:S(2)}) collective-permute-start(f32[3,3,128]{2,1,0:T(4,128)S(1)} %sums.1), channel_id=1, source_target_pairs={{0,1},{1,0},{2,3},{3,2},{4,5},{5,4},{6,7},{7,6},{8,9},{9,8},{10,11... | collective-permute-start | bytes 13832 | tf_op jit(solution)/shard_map/ppermute | solution.py:752

commit v2 on v1

--- a/solution.py
+++ b/solution.py
@@ -159,7 +159,7 @@
             do_ref[half, target] = d_out_ref[half, :, lanes]
             return carry
 
-        lax.fori_loop(0, heads, convolve_head, 0)
+        lax.fori_loop(0, heads, convolve_head, 0, unroll=4)
 
 
 def grads_kernel(ctx_count, direct, lengths_ref, filters_ref, *refs):
@@ -168,11 +168,11 @@
     same_scr, same_two_scr, q_in_ref, qc_in_ref, do_scr, own_ref, across_ref = refs[:7]
     refs = refs[7:]
     near_in, far_in, refs = refs[:arrays], refs[arrays : 2 * arrays], refs[2 * arrays :]
-    dq_hbm, dq_tail_ref, own_near_ref, own_far_ref = refs[:4]
+    dq_ref, dq_tail_ref, own_near_ref, own_far_ref = refs[:4]
     arrays = group - 1 if direct else 1
     first_out, late_out, refs = refs[4 : 4 + arrays], refs[4 + arrays : 5 + arrays], refs[5 + arrays :]
     kv_scr, conv_scr, dkv_scr, q_scr, qc_scr, dq_scr = refs[:6]
-    bias_scr, s_scr, dp_scr, dq_ref, terms_scr, sems = refs[6:]
+    bias_scr, s_scr, dp_scr, terms_scr = refs[6:]
     f32, bf16 = jnp.float32, jnp.bfloat16
     span = own_ref.shape[0] // 2 - TAIL // 2
     heads = q_in_ref.shape[1]
@@ -393,10 +393,8 @@
                 carry[2] + fold_rows(grads * two * q_scr[half, head, 6 : 6 + span]),
             )
 
-        sums = lax.fori_loop(0, heads, finish_head, tuple(sums))
+        sums = lax.fori_loop(0, heads, finish_head, tuple(sums), unroll=4)
     q_sums = [jnp.sum(term, axis=0, keepdims=True) for term in sums]
-    store = pltpu.make_async_copy(dq_ref, dq_hbm, sems.at[0])
-    store.start()
 
     def finish_block(index, carry):
         base = pl.multiple_of(index * span, 8)
@@ -473,7 +471,6 @@
         return carry
 
     loop(group - 1, store_rims, 0, 16 if direct else 1)
-    store.wait()
 
 
 def merge_kernel(ctx_count, direct, own_near_ref, own_far_ref, *refs):
@@ -523,6 +520,12 @@
     half_sums_ref[...] = joined(pair)
     far_ref[rows : rows + 16] = pair
     far_ref[rows + 16 :] = received[group - 1][rows + 16 :]
+
+
+def save_kernel(source_ref, target_hbm, sem):
+    copy = pltpu.make_async_copy(source_ref, target_hbm, sem)
+    copy.start()
+    copy.wait()
 
 
 def sums_kernel(span, half_sums_ref, far_ref, out_ref):
@@ -700,9 +703,7 @@
         pltpu.VMEM((window, LANES), f32),
         pltpu.VMEM((slots, window, 2 * LANES), f32),
         pltpu.VMEM((slots, window, 2 * LANES), f32),
-        pltpu.VMEM(q_pre.shape, f32),
         pltpu.VMEM((2 * ctx_count, span, 2 * LANES), f32),
-        pltpu.SemaphoreType.DMA((1,)),
     ]
     own_shapes = [(2 * span, 2 * LANES), (2 * span + 8, 2 * LANES)]
     d_q_main, d_q_tail, own_near, own_far, *sent = pl.pallas_call(
@@ -711,11 +712,20 @@
         + [jax.ShapeDtypeStruct(shape, f32) for shape in [(2, 8, width)] + own_shapes]
         + [jax.ShapeDtypeStruct(shape, bf16) for shape in first_shapes + late_shapes],
         in_specs=[smem, vmem] + [vmem] * (len(prepared) + len(received)),
-        out_specs=[hbm] + [vmem] * (3 + len(first_shapes + late_shapes)),
+        out_specs=[vmem] * (4 + len(first_shapes + late_shapes)),
         scratch_shapes=scratch,
         compiler_params=pltpu.CompilerParams(vmem_limit_bytes=(20 if direct else 62) * MIB),
         name="grads",
     )(doc_lengths, filters, *prepared, *received)
+    d_q_main = pl.pallas_call(
+        save_kernel,
+        out_shape=jax.ShapeDtypeStruct(q_pre.shape, f32),
+        in_specs=[vmem],
+        out_specs=hbm,
+        scratch_shapes=[pltpu.SemaphoreType.DMA(())],
+        compiler_params=pltpu.CompilerParams(vmem_limit_bytes=2 * MIB),
+        name="save",
+    )(d_q_main)
     half_terms = delivered(sent[: len(first_shapes)])
     merged_shapes = [
         jax.ShapeDtypeStruct((2 * span, 2 * LANES), f32),

time: 39.5 us -> 39.6 us (level)
  Pallas kernels: 8.93 us -> 9.37 us
    pallas_call x0 -> x1, Pallas kernels: none -> 0.8 us  [shards(): pl.pallas_call(save_kernel, out_shape=jax.ShapeDtypeStruct(q_pre.shape, f...]
    ppermute x3, waiting for transfers between devices: 0.54 us -> 0.01 us  [shards(): lax.ppermute(sums, 'tp', [(i, i ^ flip) for i in range(count)])]
  transfers between devices with their start and end apart: 15 -> 15, of which waited for: 6 -> 5; matrix products, arithmetic and copies ran while one was open for 0% -> 0% of each run, Pallas kernels for 8% -> 10%
where the time goes in v2:
time: 39.6 us; the launch traced here: 39.3 us
  starting transfers between devices  20.6 us (52%)
  Pallas kernels  9.37 us (24%)
  waiting for transfers between devices  7.89 us (20%)
  between operations  0.74 us (2%)
  other arithmetic  0.6 us (2%)
    ppermute x12, starting transfers between devices, flipped(): return lax.ppermute(array, 'ctx', [(i, i ^ flip) for i in range(ctx_count)])  18.8 us
    ppermute x12, waiting for transfers between devices, flipped(): return lax.ppermute(array, 'ctx', [(i, i ^ flip) for i in range(ctx_count)])  7.88 us
    pallas_call x1, Pallas kernels, shards(): pl.pallas_call(functools.partial(grads_kernel, ctx_count, direct), out_sh...  4.39 us
    pallas_call x1, Pallas kernels, shards(): pl.pallas_call(functools.partial(prep_kernel, ctx_count, direct), out_sha...  1.87 us
    ppermute x3, starting transfers between devices, shards(): lax.ppermute(sums, 'tp', [(i, i ^ flip) for i in range(count)])  1.86 us
    pallas_call x1, Pallas kernels, shards(): pl.pallas_call(functools.partial(finish_kernel, ctx_count, direct), out_s...  1.28 us
    pallas_call x1, Pallas kernels, shards(): pl.pallas_call(pack_kernel, grid=(1,), out_shape=jax.ShapeDtypeStruct((ms...  0.91 us
    pallas_call x1, Pallas kernels, shards(): pl.pallas_call(save_kernel, out_shape=jax.ShapeDtypeStruct(q_pre.shape, f...  0.8 us
  transfers between devices with their start and end apart: 15, of which 5 were waited for; matrix products, arithmetic and copies ran while one was open for 0% of the time, Pallas kernels for 10%

profile of v2, /device:TPU:0, one launch (start us, length us, event | category | flops | bytes accessed | tf_op | source)
XLA Modules:
  0.0 39.3 jit_solution(13531784200152885012)
XLA Ops:
  0.6 0.0 copy-start.1
  0.6 0.0 copy-start
  0.7 0.9 %pack.1.own_ref.refs_5_ = bf16[144,256]{1,0:T(8,128)(2,1)S(1)} custom-call(bf16[2,64,128]{2,1,0:T(8,128)(2,1)} %k_ref.1, bf16[2,64,128]{2,1,0:T(8,128)(2,1)} %v_ref.1, bf16[2,64,1024]{2,1,0:T(8,128)(2,1)} %q_hbm.1), custom_call_target="tpu_custom_call" | custom-call | tf_op jit(solution)/shard_map/pack/pallas_call | solution.py:642
  1.6 4.1 %collective-permute-start.3 = (bf16[144,256]{1,0:T(8,128)(2,1)S(1)}, bf16[144,256]{1,0:T(8,128)(2,1)S(1)}, u32[]{:S(2)}, u32[]{:S(2)}) collective-permute-start(bf16[144,256]{1,0:T(8,128)(2,1)S(1)} %pack.1.own_ref.refs_5_), channel_id=1, source_target_pairs={{0,16},{4,20},{8,24},{12,28},{16,0},{20,4},{24,8},{28,12},{1,17},{... | collective-permute-start | bytes 221192 | tf_op jit(solution)/shard_map/ppermute | solution.py:630
  5.7 2.5 %collective-permute-start.2 = (bf16[144,256]{1,0:T(8,128)(2,1)S(1)}, bf16[144,256]{1,0:T(8,128)(2,1)S(1)}, u32[]{:S(2)}, u32[]{:S(2)}) collective-permute-start(bf16[144,256]{1,0:T(8,128)(2,1)S(1)} %pack.1.own_ref.refs_5_), channel_id=1, source_target_pairs={{0,12},{4,8},{8,4},{12,0},{16,28},{20,24},{24,20},{28,16},{1,13},{... | collective-permute-start | bytes 221192 | tf_op jit(solution)/shard_map/ppermute | solution.py:630
  8.2 0.4 %collective-permute-start.1 = (bf16[144,256]{1,0:T(8,128)(2,1)S(1)}, bf16[144,256]{1,0:T(8,128)(2,1)S(1)}, u32[]{:S(2)}, u32[]{:S(2)}) collective-permute-start(bf16[144,256]{1,0:T(8,128)(2,1)S(1)} %pack.1.own_ref.refs_5_), channel_id=1, source_target_pairs={{0,8},{4,12},{8,0},{12,4},{16,24},{20,28},{24,16},{28,20},{1,9},{5... | collective-permute-start | bytes 221192 | tf_op jit(solution)/shard_map/ppermute | solution.py:630
  8.6 0.5 %collective-permute-start = (bf16[144,256]{1,0:T(8,128)(2,1)S(1)}, bf16[144,256]{1,0:T(8,128)(2,1)S(1)}, u32[]{:S(2)}, u32[]{:S(2)}) collective-permute-start(bf16[144,256]{1,0:T(8,128)(2,1)S(1)} %pack.1.own_ref.refs_5_), channel_id=1, source_target_pairs={{0,4},{4,0},{8,12},{12,8},{16,20},{20,16},{24,28},{28,24},{1,5},{5... | collective-permute-start | bytes 221192 | tf_op jit(solution)/shard_map/ppermute | solution.py:630
  9.2 0.0 collective-permute-done.3.refs_6_
  9.2 2.5 %collective-permute-start.6 = (bf16[144,256]{1,0:T(8,128)(2,1)S(1)}, bf16[144,256]{1,0:T(8,128)(2,1)S(1)}, u32[]{:S(2)}, u32[]{:S(2)}) collective-permute-start(bf16[144,256]{1,0:T(8,128)(2,1)S(1)} %collective-permute-done.3.refs_6_), channel_id=1, source_target_pairs={{0,12},{4,8},{8,4},{12,0},{16,28},{20,24},{24,20},{28,16},{1,13},{... | collective-permute-start | bytes 221192 | tf_op jit(solution)/shard_map/ppermute | solution.py:630
  11.7 0.7 %collective-permute-start.5 = (bf16[144,256]{1,0:T(8,128)(2,1)S(1)}, bf16[144,256]{1,0:T(8,128)(2,1)S(1)}, u32[]{:S(2)}, u32[]{:S(2)}) collective-permute-start(bf16[144,256]{1,0:T(8,128)(2,1)S(1)} %collective-permute-done.3.refs_6_), channel_id=1, source_target_pairs={{0,8},{4,12},{8,0},{12,4},{16,24},{20,28},{24,16},{28,20},{1,9},{5... | collective-permute-start | bytes 221192 | tf_op jit(solution)/shard_map/ppermute | solution.py:630
  12.4 0.0 collective-permute-done.2.refs_2_.refs_9_
  12.4 0.9 %collective-permute-start.4 = (bf16[144,256]{1,0:T(8,128)(2,1)S(1)}, bf16[144,256]{1,0:T(8,128)(2,1)S(1)}, u32[]{:S(2)}, u32[]{:S(2)}) collective-permute-start(bf16[144,256]{1,0:T(8,128)(2,1)S(1)} %collective-permute-done.3.refs_6_), channel_id=1, source_target_pairs={{0,4},{4,0},{8,12},{12,8},{16,20},{20,16},{24,28},{28,24},{1,5},{5... | collective-permute-start | bytes 221192 | tf_op jit(solution)/shard_map/ppermute | solution.py:630
  13.3 0.1 collective-permute-done.1.refs_1_.refs_8_
  13.4 0.9 %collective-permute-done.refs_0_.refs_7_ = bf16[144,256]{1,0:T(8,128)(2,1)S(1)} collective-permute-done((bf16[144,256]{1,0:T(8,128)(2,1)S(1)}, bf16[144,256]{1,0:T(8,128)(2,1)S(1)}, u32[]{:S(2)}, u32[]{:S(2)}) %collective-permute-start) | collective-permute-done | bytes 73760 | tf_op jit(solution)/shard_map/ppermute | solution.py:630
  14.3 0.0 copy-done.1
  14.3 0.0 copy-done
  14.3 1.9 %prep.1 = (f32[1040,128]{1,0:T(8,128)S(1)}, f32[1040,128]{1,0:T(8,128)S(1)}, f32[2,8,72,128]{3,2,1,0:T(8,128)S(1)}, bf16[2,512,128]{2,1,0:T(8,128)(2,1)S(1)}, bf16[2,512,128]{2,1,0:T(8,128)(2,1)S(1)}) custom-call(s32[8]{0:T(128)S(1)} %copy-done.1, f32[3,3,128]{2,1,0:T(4,128)S(1)} %copy-done, bf16[2,64,1024]{2,1,0:T(8,128)(2,1)} %q_hbm.1, ...), custom_call_target="tpu_custom_call" | custom-call | tf_op jit(solution)/shard_map/prep/pallas_call | solution.py:676
  16.2 0.0 collective-permute-done.6.refs_12_
  16.2 0.0 collective-permute-done.5.refs_11_
  16.2 0.5 %collective-permute-done.4.refs_10_ = bf16[144,256]{1,0:T(8,128)(2,1)S(1)} collective-permute-done((bf16[144,256]{1,0:T(8,128)(2,1)S(1)}, bf16[144,256]{1,0:T(8,128)(2,1)S(1)}, u32[]{:S(2)}, u32[]{:S(2)}) %collective-permute-start.4) | collective-permute-done | bytes 73760 | tf_op jit(solution)/shard_map/ppermute | solution.py:630
  16.7 4.4 %grads.1 = (f32[2,64,1024]{2,1,0:T(8,128)S(1)}, f32[2,8,1024]{2,1,0:T(8,128)S(1)}, f32[128,256]{1,0:T(8,128)S(1)}, f32[136,256]{1,0:T(8,128)S(1)}, bf16[224,256]...) custom-call(s32[8]{0:T(128)S(1)} %copy-done.1, ...), custom_call_target="tpu_custom_call" | custom-call | tf_op jit(solution)/shard_map/grads/pallas_call | solution.py:709
  21.1 1.0 %collective-permute-start.7 = (bf16[224,256]{1,0:T(8,128)(2,1)S(1)}, bf16[224,256]{1,0:T(8,128)(2,1)S(1)}, u32[]{:S(2)}, u32[]{:S(2)}) collective-permute-start(bf16[224,256]{1,0:T(8,128)(2,1)S(1)} %get-tuple-element.33), channel_id=1, source_target_pairs={{0,4},{4,0},{8,12},{12,8},{16,20},{20,16},{24,28},{28,24},{1,5},{5... | collective-permute-start | bytes 344072 | tf_op jit(solution)/shard_map/ppermute | solution.py:630
  22.1 0.5 %collective-permute-start.8 = (bf16[208,256]{1,0:T(8,128)(2,1)S(1)}, bf16[208,256]{1,0:T(8,128)(2,1)S(1)}, u32[]{:S(2)}, u32[]{:S(2)}) collective-permute-start(bf16[208,256]{1,0:T(8,128)(2,1)S(1)} %get-tuple-element.34), channel_id=1, source_target_pairs={{0,8},{4,12},{8,0},{12,4},{16,24},{20,28},{24,16},{28,20},{1,9},{5... | collective-permute-start | bytes 319496 | tf_op jit(solution)/shard_map/ppermute | solution.py:630
  22.6 2.1 %collective-permute-start.9 = (bf16[160,256]{1,0:T(8,128)(2,1)S(1)}, bf16[160,256]{1,0:T(8,128)(2,1)S(1)}, u32[]{:S(2)}, u32[]{:S(2)}) collective-permute-start(bf16[160,256]{1,0:T(8,128)(2,1)S(1)} %get-tuple-element.35), channel_id=1, source_target_pairs={{0,12},{4,8},{8,4},{12,0},{16,28},{20,24},{24,20},{28,16},{1,13},{... | collective-permute-start | bytes 245768 | tf_op jit(solution)/shard_map/ppermute | solution.py:630
  24.7 3.6 %collective-permute-done.9.refs_2_ = bf16[160,256]{1,0:T(8,128)(2,1)S(1)} collective-permute-done((bf16[160,256]{1,0:T(8,128)(2,1)S(1)}, bf16[160,256]{1,0:T(8,128)(2,1)S(1)}, u32[]{:S(2)}, u32[]{:S(2)}) %collective-permute-start.9) | collective-permute-done | bytes 81952 | tf_op jit(solution)/shard_map/ppermute | solution.py:630
  28.2 0.0 collective-permute-done.8.refs_1_
  28.2 0.0 collective-permute-done.7.refs_0_
  28.3 0.1 merge.1
  28.4 2.0 %collective-permute-start.10 = (bf16[160,256]{1,0:T(8,128)(2,1)S(1)}, bf16[160,256]{1,0:T(8,128)(2,1)S(1)}, u32[]{:S(2)}, u32[]{:S(2)}) collective-permute-start(bf16[160,256]{1,0:T(8,128)(2,1)S(1)} %get-tuple-element.37), channel_id=1, source_target_pairs={{0,16},{4,20},{8,24},{12,28},{16,0},{20,4},{24,8},{28,12},{1,17},{... | collective-permute-start | bytes 245768 | tf_op jit(solution)/shard_map/ppermute | solution.py:630
  30.3 1.6 %collective-permute-start.11 = (bf16[80,256]{1,0:T(8,128)(2,1)S(1)}, bf16[80,256]{1,0:T(8,128)(2,1)S(1)}, u32[]{:S(2)}, u32[]{:S(2)}) collective-permute-start(bf16[80,256]{1,0:T(8,128)(2,1)S(1)} %get-tuple-element.39), channel_id=1, source_target_pairs={{0,12},{4,8},{8,4},{12,0},{16,28},{20,24},{24,20},{28,16},{1,13},{... | collective-permute-start | bytes 122888 | tf_op jit(solution)/shard_map/ppermute | solution.py:630
  31.9 2.8 %collective-permute-done.10.far_ref = bf16[160,256]{1,0:T(8,128)(2,1)S(1)} collective-permute-done((bf16[160,256]{1,0:T(8,128)(2,1)S(1)}, bf16[160,256]{1,0:T(8,128)(2,1)S(1)}, u32[]{:S(2)}, u32[]{:S(2)}) %collective-permute-start.10) | collective-permute-done | bytes 81952 | tf_op jit(solution)/shard_map/ppermute | solution.py:630
  34.7 0.0 collective-permute-start.14
  34.7 1.6 %collective-permute-start.13 = (f32[3,3,128]{2,1,0:T(4,128)S(1)}, f32[3,3,128]{2,1,0:T(4,128)S(1)}, u32[]{:S(2)}, u32[]{:S(2)}) collective-permute-start(f32[3,3,128]{2,1,0:T(4,128)S(1)} %sums.1), channel_id=1, source_target_pairs={{0,2},{1,3},{2,0},{3,1},{4,6},{5,7},{6,4},{7,5},{8,10},{9,11},{10,... | collective-permute-start | bytes 13832 | tf_op jit(solution)/shard_map/ppermute | solution.py:762
  36.2 0.3 collective-permute-start.12
  36.5 0.8 %save.1.dq_in_hbm = f32[2,64,1024]{2,1,0:T(8,128)} custom-call(f32[2,64,1024]{2,1,0:T(8,128)S(1)} %get-tuple-element.29.source_ref), custom_call_target="tpu_custom_call" | custom-call | tf_op jit(solution)/shard_map/save/pallas_call | solution.py:720
  37.3 0.0 collective-permute-done.11.refs_0_
  37.3 1.3 %finish.1 = (f32[2,64,1024]{2,1,0:T(8,128)}, f32[2,64,128]{2,1,0:T(8,128)}, f32[2,64,128]{2,1,0:T(8,128)}) custom-call(s32[8]{0:T(128)S(1)} %copy-done.1, f32[3,3,128]{2,1,0:T(4,128)S(1)} %copy-done, f32[2,64,1024]{2,1,0:T(8,128)} %save.1.dq_in_hbm, f32[2,8,1024]{2,1,0:T(8,128)S(1)} %get-tuple-element.30.tail_ref, ...), custom_call_target="tpu_custom_call", output_to_operand_aliasing={{0}: (2, {})} | custom-call | tf_op jit(solution)/shard_map/finish/pallas_call | solution.py:764
  38.6 0.0 collective-permute-done.14
  38.6 0.0 collective-permute-done.13
  38.6 0.0 collective-permute-done.12
  38.7 0.6 %add_add_fusion = f32[3,3,128]{2,1,0:T(4,128)} fusion(f32[3,3,128]{2,1,0:T(4,128)S(1)} %collective-permute-done.13, f32[3,3,128]{2,1,0:T(4,128)S(1)} %collective-permute-done.14, f32[3,3,128]{2,1,0:T(4,128)S(1)} %sums.1, f32[3,3,128]{2,1,0:T(4,128)S(1)} %collective-permute-done.12), kind=kLoop, calls=%fused_computation | loop fusion | flops 3456 | bytes 23040 | tf_op jit(solution)/shard_map/add | solution.py:785
  (1 shorter events, 0.0 us)
Async XLA Ops:
  0.6 13.7 %copy-start.1 = (s32[8]{0:T(128)S(1)}, s32[8]{0:T(128)}, u32[]{:S(2)}) copy-start(s32[8]{0:T(128)} %lengths_ref.5) | copy-start | bytes 100
  0.6 13.7 %copy-start = (f32[3,3,128]{2,1,0:T(4,128)S(1)}, f32[3,3,128]{2,1,0:T(4,128)}, u32[]{:S(2)}) copy-start(f32[3,3,128]{2,1,0:T(4,128)} %filters_ref.5) | copy-start | bytes 13828
  1.6 7.6 %collective-permute-start.3 = (bf16[144,256]{1,0:T(8,128)(2,1)S(1)}, bf16[144,256]{1,0:T(8,128)(2,1)S(1)}, u32[]{:S(2)}, u32[]{:S(2)}) collective-permute-start(bf16[144,256]{1,0:T(8,128)(2,1)S(1)} %pack.1.own_ref.refs_5_), channel_id=1, source_target_pairs={{0,16},{4,20},{8,24},{12,28},{16,0},{20,4},{24,8},{28,12},{1,17},{... | collective-permute-start | bytes 221192 | tf_op jit(solution)/shard_map/ppermute | solution.py:630
  5.7 6.7 %collective-permute-start.2 = (bf16[144,256]{1,0:T(8,128)(2,1)S(1)}, bf16[144,256]{1,0:T(8,128)(2,1)S(1)}, u32[]{:S(2)}, u32[]{:S(2)}) collective-permute-start(bf16[144,256]{1,0:T(8,128)(2,1)S(1)} %pack.1.own_ref.refs_5_), channel_id=1, source_target_pairs={{0,12},{4,8},{8,4},{12,0},{16,28},{20,24},{24,20},{28,16},{1,13},{... | collective-permute-start | bytes 221192 | tf_op jit(solution)/shard_map/ppermute | solution.py:630
  8.2 5.2 %collective-permute-start.1 = (bf16[144,256]{1,0:T(8,128)(2,1)S(1)}, bf16[144,256]{1,0:T(8,128)(2,1)S(1)}, u32[]{:S(2)}, u32[]{:S(2)}) collective-permute-start(bf16[144,256]{1,0:T(8,128)(2,1)S(1)} %pack.1.own_ref.refs_5_), channel_id=1, source_target_pairs={{0,8},{4,12},{8,0},{12,4},{16,24},{20,28},{24,16},{28,20},{1,9},{5... | collective-permute-start | bytes 221192 | tf_op jit(solution)/shard_map/ppermute | solution.py:630
  8.6 5.7 %collective-permute-start = (bf16[144,256]{1,0:T(8,128)(2,1)S(1)}, bf16[144,256]{1,0:T(8,128)(2,1)S(1)}, u32[]{:S(2)}, u32[]{:S(2)}) collective-permute-start(bf16[144,256]{1,0:T(8,128)(2,1)S(1)} %pack.1.own_ref.refs_5_), channel_id=1, source_target_pairs={{0,4},{4,0},{8,12},{12,8},{16,20},{20,16},{24,28},{28,24},{1,5},{5... | collective-permute-start | bytes 221192 | tf_op jit(solution)/shard_map/ppermute | solution.py:630
  9.2 7.0 %collective-permute-start.6 = (bf16[144,256]{1,0:T(8,128)(2,1)S(1)}, bf16[144,256]{1,0:T(8,128)(2,1)S(1)}, u32[]{:S(2)}, u32[]{:S(2)}) collective-permute-start(bf16[144,256]{1,0:T(8,128)(2,1)S(1)} %collective-permute-done.3.refs_6_), channel_id=1, source_target_pairs={{0,12},{4,8},{8,4},{12,0},{16,28},{20,24},{24,20},{28,16},{1,13},{... | collective-permute-start | bytes 221192 | tf_op jit(solution)/shard_map/ppermute | solution.py:630
  11.7 4.5 %collective-permute-start.5 = (bf16[144,256]{1,0:T(8,128)(2,1)S(1)}, bf16[144,256]{1,0:T(8,128)(2,1)S(1)}, u32[]{:S(2)}, u32[]{:S(2)}) collective-permute-start(bf16[144,256]{1,0:T(8,128)(2,1)S(1)} %collective-permute-done.3.refs_6_), channel_id=1, source_target_pairs={{0,8},{4,12},{8,0},{12,4},{16,24},{20,28},{24,16},{28,20},{1,9},{5... | collective-permute-start | bytes 221192 | tf_op jit(solution)/shard_map/ppermute | solution.py:630
  12.4 4.4 %collective-permute-start.4 = (bf16[144,256]{1,0:T(8,128)(2,1)S(1)}, bf16[144,256]{1,0:T(8,128)(2,1)S(1)}, u32[]{:S(2)}, u32[]{:S(2)}) collective-permute-start(bf16[144,256]{1,0:T(8,128)(2,1)S(1)} %collective-permute-done.3.refs_6_), channel_id=1, source_target_pairs={{0,4},{4,0},{8,12},{12,8},{16,20},{20,16},{24,28},{28,24},{1,5},{5... | collective-permute-start | bytes 221192 | tf_op jit(solution)/shard_map/ppermute | solution.py:630
  21.1 7.1 %collective-permute-start.7 = (bf16[224,256]{1,0:T(8,128)(2,1)S(1)}, bf16[224,256]{1,0:T(8,128)(2,1)S(1)}, u32[]{:S(2)}, u32[]{:S(2)}) collective-permute-start(bf16[224,256]{1,0:T(8,128)(2,1)S(1)} %get-tuple-element.33), channel_id=1, source_target_pairs={{0,4},{4,0},{8,12},{12,8},{16,20},{20,16},{24,28},{28,24},{1,5},{5... | collective-permute-start | bytes 344072 | tf_op jit(solution)/shard_map/ppermute | solution.py:630
  22.1 6.1 %collective-permute-start.8 = (bf16[208,256]{1,0:T(8,128)(2,1)S(1)}, bf16[208,256]{1,0:T(8,128)(2,1)S(1)}, u32[]{:S(2)}, u32[]{:S(2)}) collective-permute-start(bf16[208,256]{1,0:T(8,128)(2,1)S(1)} %get-tuple-element.34), channel_id=1, source_target_pairs={{0,8},{4,12},{8,0},{12,4},{16,24},{20,28},{24,16},{28,20},{1,9},{5... | collective-permute-start | bytes 319496 | tf_op jit(solution)/shard_map/ppermute | solution.py:630
  22.6 5.7 %collective-permute-start.9 = (bf16[160,256]{1,0:T(8,128)(2,1)S(1)}, bf16[160,256]{1,0:T(8,128)(2,1)S(1)}, u32[]{:S(2)}, u32[]{:S(2)}) collective-permute-start(bf16[160,256]{1,0:T(8,128)(2,1)S(1)} %get-tuple-element.35), channel_id=1, source_target_pairs={{0,12},{4,8},{8,4},{12,0},{16,28},{20,24},{24,20},{28,16},{1,13},{... | collective-permute-start | bytes 245768 | tf_op jit(solution)/shard_map/ppermute | solution.py:630
  28.4 6.3 %collective-permute-start.10 = (bf16[160,256]{1,0:T(8,128)(2,1)S(1)}, bf16[160,256]{1,0:T(8,128)(2,1)S(1)}, u32[]{:S(2)}, u32[]{:S(2)}) collective-permute-start(bf16[160,256]{1,0:T(8,128)(2,1)S(1)} %get-tuple-element.37), channel_id=1, source_target_pairs={{0,16},{4,20},{8,24},{12,28},{16,0},{20,4},{24,8},{28,12},{1,17},{... | collective-permute-start | bytes 245768 | tf_op jit(solution)/shard_map/ppermute | solution.py:630
  30.3 7.0 %collective-permute-start.11 = (bf16[80,256]{1,0:T(8,128)(2,1)S(1)}, bf16[80,256]{1,0:T(8,128)(2,1)S(1)}, u32[]{:S(2)}, u32[]{:S(2)}) collective-permute-start(bf16[80,256]{1,0:T(8,128)(2,1)S(1)} %get-tuple-element.39), channel_id=1, source_target_pairs={{0,12},{4,8},{8,4},{12,0},{16,28},{20,24},{24,20},{28,16},{1,13},{... | collective-permute-start | bytes 122888 | tf_op jit(solution)/shard_map/ppermute | solution.py:630
  34.7 4.0 %collective-permute-start.14 = (f32[3,3,128]{2,1,0:T(4,128)S(1)}, f32[3,3,128]{2,1,0:T(4,128)S(1)}, u32[]{:S(2)}, u32[]{:S(2)}) collective-permute-start(f32[3,3,128]{2,1,0:T(4,128)S(1)} %sums.1), channel_id=1, source_target_pairs={{0,3},{1,2},{2,1},{3,0},{4,7},{5,6},{6,5},{7,4},{8,11},{9,10},{10,... | collective-permute-start | bytes 13832 | tf_op jit(solution)/shard_map/ppermute | solution.py:762
  34.7 4.0 %collective-permute-start.13 = (f32[3,3,128]{2,1,0:T(4,128)S(1)}, f32[3,3,128]{2,1,0:T(4,128)S(1)}, u32[]{:S(2)}, u32[]{:S(2)}) collective-permute-start(f32[3,3,128]{2,1,0:T(4,128)S(1)} %sums.1), channel_id=1, source_target_pairs={{0,2},{1,3},{2,0},{3,1},{4,6},{5,7},{6,4},{7,5},{8,10},{9,11},{10,... | collective-permute-start | bytes 13832 | tf_op jit(solution)/shard_map/ppermute | solution.py:762
  36.2 2.4 %collective-permute-start.12 = (f32[3,3,128]{2,1,0:T(4,128)S(1)}, f32[3,3,128]{2,1,0:T(4,128)S(1)}, u32[]{:S(2)}, u32[]{:S(2)}) collective-permute-start(f32[3,3,128]{2,1,0:T(4,128)S(1)} %sums.1), channel_id=1, source_target_pairs={{0,1},{1,0},{2,3},{3,2},{4,5},{5,4},{6,7},{7,6},{8,9},{9,8},{10,11... | collective-permute-start | bytes 13832 | tf_op jit(solution)/shard_map/ppermute | solution.py:762

commit v3 on v2

--- a/solution.py
+++ b/solution.py
@@ -172,7 +172,7 @@
     arrays = group - 1 if direct else 1
     first_out, late_out, refs = refs[4 : 4 + arrays], refs[4 + arrays : 5 + arrays], refs[5 + arrays :]
     kv_scr, conv_scr, dkv_scr, q_scr, qc_scr, dq_scr = refs[:6]
-    bias_scr, s_scr, dp_scr, terms_scr = refs[6:]
+    bias_scr, s_scr, dp_scr, terms_scr, p_scr, ds_scr = refs[6:]
     f32, bf16 = jnp.float32, jnp.bfloat16
     span = own_ref.shape[0] // 2 - TAIL // 2
     heads = q_in_ref.shape[1]
@@ -276,30 +276,85 @@
                 total = total + two * (two_tap * q_scr[half, head, 6 : 6 + TAIL])
                 qc_scr[half, head * span : head * span + TAIL] = total.astype(bf16)
 
+    wide = 2 * LANES
+    parts = heads * span // wide
+
+    def reach(half):
+        lane = lax.broadcasted_iota(jnp.int32, (1, LANES), 1)
+        query = first_place[half] + lax.rem(lane, jnp.int32(span))
+        lowest = jnp.zeros((1, LANES), jnp.int32)
+        for start in starts[1:]:
+            lowest = jnp.where(query >= start, start, lowest)
+        return query, lowest
+
+    def attend_at_once(window):
+        units = [(half, at) for half in range(2) for at in range(parts)]
+        keys_rows, tops, scaled = [], [], []
+        for half in range(2):
+            first_key = pl.multiple_of(jnp.maximum(first_place[half] + span - window, 0), 16)
+            keys_rows.append(pl.ds(first_key, window))
+            query, lowest = reach(half)
+            places = first_key + lax.broadcasted_iota(jnp.int32, (window, LANES), 0)
+            allowed = (places >= lowest) & (places <= query)
+            bias_scr[half, :window] = jnp.where(allowed, 0.0, -1e30)
+        for slot, (half, at) in enumerate(units):
+            queries = qc_scr[half, at * wide : (at + 1) * wide]
+            scores = lax.dot_general(
+                conv_scr[0, keys_rows[half]], queries, NT, preferred_element_type=f32
+            )
+            bias = bias_scr[half, :window]
+            scores = scores + jnp.concatenate([bias, bias], axis=1)
+            s_scr[slot, :window] = scores
+            tops.append(jnp.max(scores, axis=0, keepdims=True))
+        for slot, (half, at) in enumerate(units):
+            grads = do_scr[half, at * wide : (at + 1) * wide]
+            prob_grads = lax.dot_general(
+                conv_scr[1, keys_rows[half]], grads, NT, preferred_element_type=f32
+            )
+            weights = jnp.exp2((s_scr[slot, :window] - tops[slot]) * log2_scale)
+            s_scr[slot, :window] = weights
+            dp_scr[slot, :window] = prob_grads
+            total = jnp.sum(weights, axis=0, keepdims=True)
+            weighted = jnp.sum(weights * prob_grads, axis=0, keepdims=True)
+            inverse = 1.0 / total
+            scaled.append((inverse, weighted * inverse, inverse * scale))
+        for slot, (half, at) in enumerate(units):
+            inverse, mean, slope = scaled[slot]
+            weights = s_scr[slot, :window]
+            cols = slice(at * wide, (at + 1) * wide)
+            p_scr[half, :window, cols] = (weights * inverse).astype(bf16)
+            ds_scr[half, :window, cols] = (weights * slope * (dp_scr[slot, :window] - mean)).astype(bf16)
+        for half in range(2):
+            score_grads = ds_scr[half, :window]
+            keys_t = conv_scr[0, keys_rows[half]].T
+            dq = lax.dot_general(keys_t, score_grads, NN, preferred_element_type=f32).T
+            for head in range(heads):
+                dq_scr[half, head, :span] = dq[head * span : (head + 1) * span]
+            dkv_scr[0, keys_rows[half]] += lax.dot_general(
+                score_grads, qc_scr[half], NN, preferred_element_type=f32
+            )
+            dkv_scr[1, keys_rows[half]] += lax.dot_general(
+                p_scr[half, :window], do_scr[half], NN, preferred_element_type=f32
+            )
+
     def attend(half, window, first_key):
         chunks = 1
         while window // chunks > MAX_CHUNK or window % (16 * chunks):
             chunks += 1
         size = window // chunks
-        query = first_place[half] + lax.rem(
-            lax.broadcasted_iota(jnp.int32, (1, LANES), 1), jnp.int32(span)
-        )
-        lowest = jnp.zeros((1, LANES), jnp.int32)
-        for start in starts[1:]:
-            lowest = jnp.where(query >= start, start, lowest)
-        wide = 2 * LANES
+        query, lowest = reach(half)
 
         def fill_bias(step, carry):
             places = first_key + step * size + lax.broadcasted_iota(jnp.int32, (size, LANES), 0)
             allowed = (places >= lowest) & (places <= query)
-            bias_scr[pl.ds(aligned(step * size, 16), size)] = jnp.where(allowed, 0.0, -1e30)
+            bias_scr[0, pl.ds(aligned(step * size, 16), size)] = jnp.where(allowed, 0.0, -1e30)
             return carry
 
         loop(chunks, fill_bias, 0, 1)
         whole_window = pl.ds(aligned(first_key, 16), window)
         keys_t = conv_scr[0, whole_window].T if chunks == 1 else None
-        for at in range(heads * span // wide):
-            slot = (half * (heads * span // wide) + at) % s_scr.shape[0]
+        for at in range(parts):
+            slot = 0
             cols = slice(at * wide, (at + 1) * wide)
             queries = qc_scr[half, cols]
             grads = do_scr[half, cols]
@@ -310,7 +365,7 @@
             def score(step, top):
                 keys = conv_scr[0, key_rows(step)]
                 scores = lax.dot_general(keys, queries, NT, preferred_element_type=f32)
-                bias = bias_scr[pl.ds(aligned(step * size, 16), size)]
+                bias = bias_scr[0, pl.ds(aligned(step * size, 16), size)]
                 scores = scores + jnp.concatenate([bias, bias], axis=1)
                 s_scr[slot, pl.ds(aligned(step * size, 16), size)] = scores
                 return jnp.maximum(top, jnp.max(scores, axis=0, keepdims=True))
@@ -356,18 +411,19 @@
                 head = at * (wide // span) + part
                 dq_scr[half, head, :span] = dq[part * span : (part + 1) * span]
 
-    for half in range(2):
-        widest = ctx_count + half
-        needed = first_place[half] // span - firsts[half] + 1
-        below = 0
-        for count in [count for count in WINDOWS if direct and count < widest] + [widest]:
-
-            @pl.when((needed > below) & (needed <= count))
-            def _(half=half, count=count):
-                first_key = jnp.maximum(first_place[half] + span - count * span, 0)
-                attend(half, count * span, first_key)
+    needed = [first_place[half] // span - firsts[half] + 1 for half in range(2)]
+    if direct:
+        below, both = 0, jnp.maximum(needed[0], needed[1])
+        for count in [count for count in WINDOWS if count <= ctx_count] + [ctx_count + 1]:
+
+            @pl.when((both > below) & (both <= count))
+            def _(count=count):
+                attend_at_once(count * span)
 
             below = count
+    else:
+        for half in range(2):
+            attend(half, half_rows + half * span, half * (ctx_count - 1 - me) * span)
 
     next_rows = jnp.where(middle, dq_scr[1, :, :8], 0.0)
     dq_scr[0, :, span:] = next_rows
@@ -700,10 +756,12 @@
         pltpu.VMEM(padded, f32),
         pltpu.VMEM(by_head, bf16),
         pltpu.VMEM(padded, f32),
-        pltpu.VMEM((window, LANES), f32),
+        pltpu.VMEM((2, window, LANES), f32),
         pltpu.VMEM((slots, window, 2 * LANES), f32),
         pltpu.VMEM((slots, window, 2 * LANES), f32),
         pltpu.VMEM((2 * ctx_count, span, 2 * LANES), f32),
+        pltpu.VMEM((2, window, heads * span) if direct else (2, 16, LANES), bf16),
+        pltpu.VMEM((2, window, heads * span) if direct else (2, 16, LANES), bf16),
     ]
     own_shapes = [(2 * span, 2 * LANES), (2 * span + 8, 2 * LANES)]
     d_q_main, d_q_tail, own_near, own_far, *sent = pl.pallas_call(
@@ -727,6 +785,7 @@
         name="save",
     )(d_q_main)
     half_terms = delivered(sent[: len(first_shapes)])
+    d_q_main, *half_terms = lax.optimization_barrier((d_q_main, *half_terms))
     merged_shapes = [
         jax.ShapeDtypeStruct((2 * span, 2 * LANES), f32),
         jax.ShapeDtypeStruct((2 * span + 32, 2 * LANES), bf16),

time: 39.6 us -> 39.3 us (level)
  Pallas kernels: 9.37 us -> 7.33 us
  starting transfers between devices: 20.6 us -> 21.6 us
  waiting for transfers between devices: 7.89 us -> 8.61 us
    pallas_call x1, Pallas kernels: 4.39 us -> 2.36 us  [shards(): pl.pallas_call(functools.partial(grads_kernel, ctx_count, direct), out_sh...]
    ppermute x12, starting transfers between devices: 18.8 us -> 19.7 us  [flipped(): return lax.ppermute(array, 'ctx', [(i, i ^ flip) for i in range(ctx_count)])]
    ppermute x3, waiting for transfers between devices: 0.01 us -> 0.54 us  [shards(): lax.ppermute(sums, 'tp', [(i, i ^ flip) for i in range(count)])]
  transfers between devices with their start and end apart: 15 -> 15, of which waited for: 5 -> 6; matrix products, arithmetic and copies ran while one was open for 0% -> 0% of each run, Pallas kernels for 10% -> 10%
where the time goes in v3:
time: 39.3 us; the launch traced here: 38.9 us
  starting transfers between devices  21.6 us (55%)
  waiting for transfers between devices  8.61 us (22%)
  Pallas kernels  7.33 us (19%)
  between operations  0.72 us (2%)
  other arithmetic  0.6 us (2%)
    ppermute x12, starting transfers between devices, flipped(): return lax.ppermute(array, 'ctx', [(i, i ^ flip) for i in range(ctx_count)])  19.7 us
    ppermute x12, waiting for transfers between devices, flipped(): return lax.ppermute(array, 'ctx', [(i, i ^ flip) for i in range(ctx_count)])  8.07 us
    pallas_call x1, Pallas kernels, shards(): pl.pallas_call(functools.partial(grads_kernel, ctx_count, direct), out_sh...  2.36 us
    pallas_call x1, Pallas kernels, shards(): pl.pallas_call(functools.partial(prep_kernel, ctx_count, direct), out_sha...  1.87 us
    ppermute x3, starting transfers between devices, shards(): lax.ppermute(sums, 'tp', [(i, i ^ flip) for i in range(count)])  1.86 us
    pallas_call x1, Pallas kernels, shards(): pl.pallas_call(functools.partial(finish_kernel, ctx_count, direct), out_s...  1.27 us
    pallas_call x1, Pallas kernels, shards(): pl.pallas_call(pack_kernel, grid=(1,), out_shape=jax.ShapeDtypeStruct((ms...  0.91 us
    pallas_call x1, Pallas kernels, shards(): pl.pallas_call(save_kernel, out_shape=jax.ShapeDtypeStruct(q_pre.shape, f...  0.8 us
  transfers between devices with their start and end apart: 15, of which 6 were waited for; matrix products, arithmetic and copies ran while one was open for 0% of the time, Pallas kernels for 10%

profile of v3, /device:TPU:0, one launch (start us, length us, event | category | flops | bytes accessed | tf_op | source)
XLA Modules:
  0.0 38.9 jit_solution(15597271994446745283)
XLA Ops:
  0.6 0.0 copy-start.1
  0.6 0.0 copy-start
  0.7 0.9 %pack.1.own_ref.refs_5_ = bf16[144,256]{1,0:T(8,128)(2,1)S(1)} custom-call(bf16[2,64,128]{2,1,0:T(8,128)(2,1)} %k_ref.1, bf16[2,64,128]{2,1,0:T(8,128)(2,1)} %v_ref.1, bf16[2,64,1024]{2,1,0:T(8,128)(2,1)} %q_hbm.1), custom_call_target="tpu_custom_call" | custom-call | tf_op jit(solution)/shard_map/pack/pallas_call | solution.py:698
  1.6 4.1 %collective-permute-start.3 = (bf16[144,256]{1,0:T(8,128)(2,1)S(1)}, bf16[144,256]{1,0:T(8,128)(2,1)S(1)}, u32[]{:S(2)}, u32[]{:S(2)}) collective-permute-start(bf16[144,256]{1,0:T(8,128)(2,1)S(1)} %pack.1.own_ref.refs_5_), channel_id=1, source_target_pairs={{0,16},{4,20},{8,24},{12,28},{16,0},{20,4},{24,8},{28,12},{1,17},{... | collective-permute-start | bytes 221192 | tf_op jit(solution)/shard_map/ppermute | solution.py:686
  5.7 2.5 %collective-permute-start.2 = (bf16[144,256]{1,0:T(8,128)(2,1)S(1)}, bf16[144,256]{1,0:T(8,128)(2,1)S(1)}, u32[]{:S(2)}, u32[]{:S(2)}) collective-permute-start(bf16[144,256]{1,0:T(8,128)(2,1)S(1)} %pack.1.own_ref.refs_5_), channel_id=1, source_target_pairs={{0,12},{4,8},{8,4},{12,0},{16,28},{20,24},{24,20},{28,16},{1,13},{... | collective-permute-start | bytes 221192 | tf_op jit(solution)/shard_map/ppermute | solution.py:686
  8.2 0.4 %collective-permute-start.1 = (bf16[144,256]{1,0:T(8,128)(2,1)S(1)}, bf16[144,256]{1,0:T(8,128)(2,1)S(1)}, u32[]{:S(2)}, u32[]{:S(2)}) collective-permute-start(bf16[144,256]{1,0:T(8,128)(2,1)S(1)} %pack.1.own_ref.refs_5_), channel_id=1, source_target_pairs={{0,8},{4,12},{8,0},{12,4},{16,24},{20,28},{24,16},{28,20},{1,9},{5... | collective-permute-start | bytes 221192 | tf_op jit(solution)/shard_map/ppermute | solution.py:686
  8.6 0.5 %collective-permute-start = (bf16[144,256]{1,0:T(8,128)(2,1)S(1)}, bf16[144,256]{1,0:T(8,128)(2,1)S(1)}, u32[]{:S(2)}, u32[]{:S(2)}) collective-permute-start(bf16[144,256]{1,0:T(8,128)(2,1)S(1)} %pack.1.own_ref.refs_5_), channel_id=1, source_target_pairs={{0,4},{4,0},{8,12},{12,8},{16,20},{20,16},{24,28},{28,24},{1,5},{5... | collective-permute-start | bytes 221192 | tf_op jit(solution)/shard_map/ppermute | solution.py:686
  9.2 0.0 collective-permute-done.3.refs_6_
  9.2 2.5 %collective-permute-start.6 = (bf16[144,256]{1,0:T(8,128)(2,1)S(1)}, bf16[144,256]{1,0:T(8,128)(2,1)S(1)}, u32[]{:S(2)}, u32[]{:S(2)}) collective-permute-start(bf16[144,256]{1,0:T(8,128)(2,1)S(1)} %collective-permute-done.3.refs_6_), channel_id=1, source_target_pairs={{0,12},{4,8},{8,4},{12,0},{16,28},{20,24},{24,20},{28,16},{1,13},{... | collective-permute-start | bytes 221192 | tf_op jit(solution)/shard_map/ppermute | solution.py:686
  11.7 0.7 %collective-permute-start.5 = (bf16[144,256]{1,0:T(8,128)(2,1)S(1)}, bf16[144,256]{1,0:T(8,128)(2,1)S(1)}, u32[]{:S(2)}, u32[]{:S(2)}) collective-permute-start(bf16[144,256]{1,0:T(8,128)(2,1)S(1)} %collective-permute-done.3.refs_6_), channel_id=1, source_target_pairs={{0,8},{4,12},{8,0},{12,4},{16,24},{20,28},{24,16},{28,20},{1,9},{5... | collective-permute-start | bytes 221192 | tf_op jit(solution)/shard_map/ppermute | solution.py:686
  12.4 0.0 collective-permute-done.2.refs_2_.refs_9_
  12.4 0.9 %collective-permute-start.4 = (bf16[144,256]{1,0:T(8,128)(2,1)S(1)}, bf16[144,256]{1,0:T(8,128)(2,1)S(1)}, u32[]{:S(2)}, u32[]{:S(2)}) collective-permute-start(bf16[144,256]{1,0:T(8,128)(2,1)S(1)} %collective-permute-done.3.refs_6_), channel_id=1, source_target_pairs={{0,4},{4,0},{8,12},{12,8},{16,20},{20,16},{24,28},{28,24},{1,5},{5... | collective-permute-start | bytes 221192 | tf_op jit(solution)/shard_map/ppermute | solution.py:686
  13.3 0.1 collective-permute-done.1.refs_1_.refs_8_
  13.4 0.9 %collective-permute-done.refs_0_.refs_7_ = bf16[144,256]{1,0:T(8,128)(2,1)S(1)} collective-permute-done((bf16[144,256]{1,0:T(8,128)(2,1)S(1)}, bf16[144,256]{1,0:T(8,128)(2,1)S(1)}, u32[]{:S(2)}, u32[]{:S(2)}) %collective-permute-start) | collective-permute-done | bytes 73760 | tf_op jit(solution)/shard_map/ppermute | solution.py:686
  14.3 0.0 copy-done.1
  14.3 0.0 copy-done
  14.3 1.9 %prep.1 = (f32[1040,128]{1,0:T(8,128)S(1)}, f32[1040,128]{1,0:T(8,128)S(1)}, f32[2,8,72,128]{3,2,1,0:T(8,128)S(1)}, bf16[2,512,128]{2,1,0:T(8,128)(2,1)S(1)}, bf16[2,512,128]{2,1,0:T(8,128)(2,1)S(1)}) custom-call(s32[8]{0:T(128)S(1)} %copy-done.1, f32[3,3,128]{2,1,0:T(4,128)S(1)} %copy-done, bf16[2,64,1024]{2,1,0:T(8,128)(2,1)} %q_hbm.1, ...), custom_call_target="tpu_custom_call" | custom-call | tf_op jit(solution)/shard_map/prep/pallas_call | solution.py:732
  16.2 0.0 collective-permute-done.6.refs_12_
  16.2 0.0 collective-permute-done.5.refs_11_
  16.2 0.5 %collective-permute-done.4.refs_10_ = bf16[144,256]{1,0:T(8,128)(2,1)S(1)} collective-permute-done((bf16[144,256]{1,0:T(8,128)(2,1)S(1)}, bf16[144,256]{1,0:T(8,128)(2,1)S(1)}, u32[]{:S(2)}, u32[]{:S(2)}) %collective-permute-start.4) | collective-permute-done | bytes 73760 | tf_op jit(solution)/shard_map/ppermute | solution.py:686
  16.7 2.4 %grads.1 = (f32[2,64,1024]{2,1,0:T(8,128)S(1)}, f32[2,8,1024]{2,1,0:T(8,128)S(1)}, f32[128,256]{1,0:T(8,128)S(1)}, f32[136,256]{1,0:T(8,128)S(1)}, bf16[224,256]...) custom-call(s32[8]{0:T(128)S(1)} %copy-done.1, ...), custom_call_target="tpu_custom_call" | custom-call | tf_op jit(solution)/shard_map/grads/pallas_call | solution.py:767
  19.1 1.6 %collective-permute-start.7 = (bf16[224,256]{1,0:T(8,128)(2,1)S(1)}, bf16[224,256]{1,0:T(8,128)(2,1)S(1)}, u32[]{:S(2)}, u32[]{:S(2)}) collective-permute-start(bf16[224,256]{1,0:T(8,128)(2,1)S(1)} %get-tuple-element.34), channel_id=1, source_target_pairs={{0,4},{4,0},{8,12},{12,8},{16,20},{20,16},{24,28},{28,24},{1,5},{5... | collective-permute-start | bytes 344072 | tf_op jit(solution)/shard_map/ppermute | solution.py:686
  20.7 2.6 %collective-permute-start.8 = (bf16[208,256]{1,0:T(8,128)(2,1)S(1)}, bf16[208,256]{1,0:T(8,128)(2,1)S(1)}, u32[]{:S(2)}, u32[]{:S(2)}) collective-permute-start(bf16[208,256]{1,0:T(8,128)(2,1)S(1)} %get-tuple-element.35), channel_id=1, source_target_pairs={{0,8},{4,12},{8,0},{12,4},{16,24},{20,28},{24,16},{28,20},{1,9},{5... | collective-permute-start | bytes 319496 | tf_op jit(solution)/shard_map/ppermute | solution.py:686
  23.4 0.0 collective-permute-start.9
  23.4 0.8 %save.1.dq_in_hbm = f32[2,64,1024]{2,1,0:T(8,128)} custom-call(f32[2,64,1024]{2,1,0:T(8,128)S(1)} %get-tuple-element.33.source_ref), custom_call_target="tpu_custom_call" | custom-call | tf_op jit(solution)/shard_map/save/pallas_call | solution.py:778
  24.2 4.5 %collective-permute-done.9.refs_2_ = bf16[160,256]{1,0:T(8,128)(2,1)S(1)} collective-permute-done((bf16[160,256]{1,0:T(8,128)(2,1)S(1)}, bf16[160,256]{1,0:T(8,128)(2,1)S(1)}, u32[]{:S(2)}, u32[]{:S(2)}) %collective-permute-start.9) | collective-permute-done | bytes 81952 | tf_op jit(solution)/shard_map/ppermute | solution.py:686
  28.7 0.0 collective-permute-done.8.refs_1_
  28.7 0.0 collective-permute-done.7.refs_0_
  28.7 0.1 merge.1
  28.8 2.0 %collective-permute-start.10 = (bf16[160,256]{1,0:T(8,128)(2,1)S(1)}, bf16[160,256]{1,0:T(8,128)(2,1)S(1)}, u32[]{:S(2)}, u32[]{:S(2)}) collective-permute-start(bf16[160,256]{1,0:T(8,128)(2,1)S(1)} %get-tuple-element.45), channel_id=1, source_target_pairs={{0,16},{4,20},{8,24},{12,28},{16,0},{20,4},{24,8},{28,12},{1,17},{... | collective-permute-start | bytes 245768 | tf_op jit(solution)/shard_map/ppermute | solution.py:686
  30.9 1.7 %collective-permute-start.11 = (bf16[80,256]{1,0:T(8,128)(2,1)S(1)}, bf16[80,256]{1,0:T(8,128)(2,1)S(1)}, u32[]{:S(2)}, u32[]{:S(2)}) collective-permute-start(bf16[80,256]{1,0:T(8,128)(2,1)S(1)} %get-tuple-element.47), channel_id=1, source_target_pairs={{0,12},{4,8},{8,4},{12,0},{16,28},{20,24},{24,20},{28,16},{1,13},{... | collective-permute-start | bytes 122888 | tf_op jit(solution)/shard_map/ppermute | solution.py:686
  32.6 2.0 %collective-permute-done.10.far_ref = bf16[160,256]{1,0:T(8,128)(2,1)S(1)} collective-permute-done((bf16[160,256]{1,0:T(8,128)(2,1)S(1)}, bf16[160,256]{1,0:T(8,128)(2,1)S(1)}, u32[]{:S(2)}, u32[]{:S(2)}) %collective-permute-start.10) | collective-permute-done | bytes 81952 | tf_op jit(solution)/shard_map/ppermute | solution.py:686
  34.6 0.0 collective-permute-start.14
  34.6 1.6 %collective-permute-start.13 = (f32[3,3,128]{2,1,0:T(4,128)S(1)}, f32[3,3,128]{2,1,0:T(4,128)S(1)}, u32[]{:S(2)}, u32[]{:S(2)}) collective-permute-start(f32[3,3,128]{2,1,0:T(4,128)S(1)} %sums.1), channel_id=1, source_target_pairs={{0,2},{1,3},{2,0},{3,1},{4,6},{5,7},{6,4},{7,5},{8,10},{9,11},{10,... | collective-permute-start | bytes 13832 | tf_op jit(solution)/shard_map/ppermute | solution.py:821
  36.1 0.3 collective-permute-start.12
  36.4 0.0 collective-permute-done.11.refs_0_
  36.4 1.3 %finish.1 = (f32[2,64,1024]{2,1,0:T(8,128)}, f32[2,64,128]{2,1,0:T(8,128)}, f32[2,64,128]{2,1,0:T(8,128)}) custom-call(s32[8]{0:T(128)S(1)} %copy-done.1, f32[3,3,128]{2,1,0:T(4,128)S(1)} %copy-done, f32[2,64,1024]{2,1,0:T(8,128)} %save.1.dq_in_hbm, f32[2,8,1024]{2,1,0:T(8,128)S(1)} %get-tuple-element.38.tail_ref, ...), custom_call_target="tpu_custom_call", output_to_operand_aliasing={{0}: (2, {})} | custom-call | tf_op jit(solution)/shard_map/finish/pallas_call | solution.py:823
  37.7 0.0 collective-permute-done.14
  37.7 0.5 %collective-permute-done.13 = f32[3,3,128]{2,1,0:T(4,128)S(1)} collective-permute-done((f32[3,3,128]{2,1,0:T(4,128)S(1)}, f32[3,3,128]{2,1,0:T(4,128)S(1)}, u32[]{:S(2)}, u32[]{:S(2)}) %collective-permute-start.13) | collective-permute-done | bytes 4640 | tf_op jit(solution)/shard_map/ppermute | solution.py:821
  38.3 0.0 collective-permute-done.12
  38.3 0.6 %add_add_fusion = f32[3,3,128]{2,1,0:T(4,128)} fusion(f32[3,3,128]{2,1,0:T(4,128)S(1)} %collective-permute-done.13, f32[3,3,128]{2,1,0:T(4,128)S(1)} %collective-permute-done.14, f32[3,3,128]{2,1,0:T(4,128)S(1)} %sums.1, f32[3,3,128]{2,1,0:T(4,128)S(1)} %collective-permute-done.12), kind=kLoop, calls=%fused_computation | loop fusion | flops 3456 | bytes 23040 | tf_op jit(solution)/shard_map/add | solution.py:844
  (1 shorter events, 0.0 us)
Async XLA Ops:
  0.6 13.7 %copy-start.1 = (s32[8]{0:T(128)S(1)}, s32[8]{0:T(128)}, u32[]{:S(2)}) copy-start(s32[8]{0:T(128)} %lengths_ref.5) | copy-start | bytes 100
  0.6 13.7 %copy-start = (f32[3,3,128]{2,1,0:T(4,128)S(1)}, f32[3,3,128]{2,1,0:T(4,128)}, u32[]{:S(2)}) copy-start(f32[3,3,128]{2,1,0:T(4,128)} %filters_ref.5) | copy-start | bytes 13828
  1.6 7.6 %collective-permute-start.3 = (bf16[144,256]{1,0:T(8,128)(2,1)S(1)}, bf16[144,256]{1,0:T(8,128)(2,1)S(1)}, u32[]{:S(2)}, u32[]{:S(2)}) collective-permute-start(bf16[144,256]{1,0:T(8,128)(2,1)S(1)} %pack.1.own_ref.refs_5_), channel_id=1, source_target_pairs={{0,16},{4,20},{8,24},{12,28},{16,0},{20,4},{24,8},{28,12},{1,17},{... | collective-permute-start | bytes 221192 | tf_op jit(solution)/shard_map/ppermute | solution.py:686
  5.7 6.7 %collective-permute-start.2 = (bf16[144,256]{1,0:T(8,128)(2,1)S(1)}, bf16[144,256]{1,0:T(8,128)(2,1)S(1)}, u32[]{:S(2)}, u32[]{:S(2)}) collective-permute-start(bf16[144,256]{1,0:T(8,128)(2,1)S(1)} %pack.1.own_ref.refs_5_), channel_id=1, source_target_pairs={{0,12},{4,8},{8,4},{12,0},{16,28},{20,24},{24,20},{28,16},{1,13},{... | collective-permute-start | bytes 221192 | tf_op jit(solution)/shard_map/ppermute | solution.py:686
  8.2 5.2 %collective-permute-start.1 = (bf16[144,256]{1,0:T(8,128)(2,1)S(1)}, bf16[144,256]{1,0:T(8,128)(2,1)S(1)}, u32[]{:S(2)}, u32[]{:S(2)}) collective-permute-start(bf16[144,256]{1,0:T(8,128)(2,1)S(1)} %pack.1.own_ref.refs_5_), channel_id=1, source_target_pairs={{0,8},{4,12},{8,0},{12,4},{16,24},{20,28},{24,16},{28,20},{1,9},{5... | collective-permute-start | bytes 221192 | tf_op jit(solution)/shard_map/ppermute | solution.py:686
  8.6 5.7 %collective-permute-start = (bf16[144,256]{1,0:T(8,128)(2,1)S(1)}, bf16[144,256]{1,0:T(8,128)(2,1)S(1)}, u32[]{:S(2)}, u32[]{:S(2)}) collective-permute-start(bf16[144,256]{1,0:T(8,128)(2,1)S(1)} %pack.1.own_ref.refs_5_), channel_id=1, source_target_pairs={{0,4},{4,0},{8,12},{12,8},{16,20},{20,16},{24,28},{28,24},{1,5},{5... | collective-permute-start | bytes 221192 | tf_op jit(solution)/shard_map/ppermute | solution.py:686
  9.2 7.0 %collective-permute-start.6 = (bf16[144,256]{1,0:T(8,128)(2,1)S(1)}, bf16[144,256]{1,0:T(8,128)(2,1)S(1)}, u32[]{:S(2)}, u32[]{:S(2)}) collective-permute-start(bf16[144,256]{1,0:T(8,128)(2,1)S(1)} %collective-permute-done.3.refs_6_), channel_id=1, source_target_pairs={{0,12},{4,8},{8,4},{12,0},{16,28},{20,24},{24,20},{28,16},{1,13},{... | collective-permute-start | bytes 221192 | tf_op jit(solution)/shard_map/ppermute | solution.py:686
  11.7 4.5 %collective-permute-start.5 = (bf16[144,256]{1,0:T(8,128)(2,1)S(1)}, bf16[144,256]{1,0:T(8,128)(2,1)S(1)}, u32[]{:S(2)}, u32[]{:S(2)}) collective-permute-start(bf16[144,256]{1,0:T(8,128)(2,1)S(1)} %collective-permute-done.3.refs_6_), channel_id=1, source_target_pairs={{0,8},{4,12},{8,0},{12,4},{16,24},{20,28},{24,16},{28,20},{1,9},{5... | collective-permute-start | bytes 221192 | tf_op jit(solution)/shard_map/ppermute | solution.py:686
  12.4 4.4 %collective-permute-start.4 = (bf16[144,256]{1,0:T(8,128)(2,1)S(1)}, bf16[144,256]{1,0:T(8,128)(2,1)S(1)}, u32[]{:S(2)}, u32[]{:S(2)}) collective-permute-start(bf16[144,256]{1,0:T(8,128)(2,1)S(1)} %collective-permute-done.3.refs_6_), channel_id=1, source_target_pairs={{0,4},{4,0},{8,12},{12,8},{16,20},{20,16},{24,28},{28,24},{1,5},{5... | collective-permute-start | bytes 221192 | tf_op jit(solution)/shard_map/ppermute | solution.py:686
  19.1 9.6 %collective-permute-start.7 = (bf16[224,256]{1,0:T(8,128)(2,1)S(1)}, bf16[224,256]{1,0:T(8,128)(2,1)S(1)}, u32[]{:S(2)}, u32[]{:S(2)}) collective-permute-start(bf16[224,256]{1,0:T(8,128)(2,1)S(1)} %get-tuple-element.34), channel_id=1, source_target_pairs={{0,4},{4,0},{8,12},{12,8},{16,20},{20,16},{24,28},{28,24},{1,5},{5... | collective-permute-start | bytes 344072 | tf_op jit(solution)/shard_map/ppermute | solution.py:686
  20.7 8.0 %collective-permute-start.8 = (bf16[208,256]{1,0:T(8,128)(2,1)S(1)}, bf16[208,256]{1,0:T(8,128)(2,1)S(1)}, u32[]{:S(2)}, u32[]{:S(2)}) collective-permute-start(bf16[208,256]{1,0:T(8,128)(2,1)S(1)} %get-tuple-element.35), channel_id=1, source_target_pairs={{0,8},{4,12},{8,0},{12,4},{16,24},{20,28},{24,16},{28,20},{1,9},{5... | collective-permute-start | bytes 319496 | tf_op jit(solution)/shard_map/ppermute | solution.py:686
  23.4 5.3 %collective-permute-start.9 = (bf16[160,256]{1,0:T(8,128)(2,1)S(1)}, bf16[160,256]{1,0:T(8,128)(2,1)S(1)}, u32[]{:S(2)}, u32[]{:S(2)}) collective-permute-start(bf16[160,256]{1,0:T(8,128)(2,1)S(1)} %get-tuple-element.36), channel_id=1, source_target_pairs={{0,12},{4,8},{8,4},{12,0},{16,28},{20,24},{24,20},{28,16},{1,13},{... | collective-permute-start | bytes 245768 | tf_op jit(solution)/shard_map/ppermute | solution.py:686
  28.8 5.7 %collective-permute-start.10 = (bf16[160,256]{1,0:T(8,128)(2,1)S(1)}, bf16[160,256]{1,0:T(8,128)(2,1)S(1)}, u32[]{:S(2)}, u32[]{:S(2)}) collective-permute-start(bf16[160,256]{1,0:T(8,128)(2,1)S(1)} %get-tuple-element.45), channel_id=1, source_target_pairs={{0,16},{4,20},{8,24},{12,28},{16,0},{20,4},{24,8},{28,12},{1,17},{... | collective-permute-start | bytes 245768 | tf_op jit(solution)/shard_map/ppermute | solution.py:686
  30.9 5.5 %collective-permute-start.11 = (bf16[80,256]{1,0:T(8,128)(2,1)S(1)}, bf16[80,256]{1,0:T(8,128)(2,1)S(1)}, u32[]{:S(2)}, u32[]{:S(2)}) collective-permute-start(bf16[80,256]{1,0:T(8,128)(2,1)S(1)} %get-tuple-element.47), channel_id=1, source_target_pairs={{0,12},{4,8},{8,4},{12,0},{16,28},{20,24},{24,20},{28,16},{1,13},{... | collective-permute-start | bytes 122888 | tf_op jit(solution)/shard_map/ppermute | solution.py:686
  34.6 3.1 %collective-permute-start.14 = (f32[3,3,128]{2,1,0:T(4,128)S(1)}, f32[3,3,128]{2,1,0:T(4,128)S(1)}, u32[]{:S(2)}, u32[]{:S(2)}) collective-permute-start(f32[3,3,128]{2,1,0:T(4,128)S(1)} %sums.1), channel_id=1, source_target_pairs={{0,3},{1,2},{2,1},{3,0},{4,7},{5,6},{6,5},{7,4},{8,11},{9,10},{10,... | collective-permute-start | bytes 13832 | tf_op jit(solution)/shard_map/ppermute | solution.py:821
  34.6 3.7 %collective-permute-start.13 = (f32[3,3,128]{2,1,0:T(4,128)S(1)}, f32[3,3,128]{2,1,0:T(4,128)S(1)}, u32[]{:S(2)}, u32[]{:S(2)}) collective-permute-start(f32[3,3,128]{2,1,0:T(4,128)S(1)} %sums.1), channel_id=1, source_target_pairs={{0,2},{1,3},{2,0},{3,1},{4,6},{5,7},{6,4},{7,5},{8,10},{9,11},{10,... | collective-permute-start | bytes 13832 | tf_op jit(solution)/shard_map/ppermute | solution.py:821
  36.1 2.1 %collective-permute-start.12 = (f32[3,3,128]{2,1,0:T(4,128)S(1)}, f32[3,3,128]{2,1,0:T(4,128)S(1)}, u32[]{:S(2)}, u32[]{:S(2)}) collective-permute-start(f32[3,3,128]{2,1,0:T(4,128)S(1)} %sums.1), channel_id=1, source_target_pairs={{0,1},{1,0},{2,3},{3,2},{4,5},{5,4},{6,7},{7,6},{8,9},{9,8},{10,11... | collective-permute-start | bytes 13832 | tf_op jit(solution)/shard_map/ppermute | solution.py:821

commit v4 on v3

--- a/solution.py
+++ b/solution.py
@@ -16,7 +16,7 @@
 MAX_CHUNK = 640
 RIM = 8
 MAX_DIRECT = 4
-WINDOWS = (2, 4, 6)
+WINDOWS = ((2, 2), (4, 4), (6, 6), (4, 9), (9, 4), (9, 9))
 MIB = 1 << 20
 
 
@@ -287,10 +287,10 @@
             lowest = jnp.where(query >= start, start, lowest)
         return query, lowest
 
-    def attend_at_once(window):
+    def attend_at_once(windows):
         units = [(half, at) for half in range(2) for at in range(parts)]
         keys_rows, tops, scaled = [], [], []
-        for half in range(2):
+        for half, window in enumerate(windows):
             first_key = pl.multiple_of(jnp.maximum(first_place[half] + span - window, 0), 16)
             keys_rows.append(pl.ds(first_key, window))
             query, lowest = reach(half)
@@ -298,6 +298,7 @@
             allowed = (places >= lowest) & (places <= query)
             bias_scr[half, :window] = jnp.where(allowed, 0.0, -1e30)
         for slot, (half, at) in enumerate(units):
+            window = windows[half]
             queries = qc_scr[half, at * wide : (at + 1) * wide]
             scores = lax.dot_general(
                 conv_scr[0, keys_rows[half]], queries, NT, preferred_element_type=f32
@@ -307,6 +308,7 @@
             s_scr[slot, :window] = scores
             tops.append(jnp.max(scores, axis=0, keepdims=True))
         for slot, (half, at) in enumerate(units):
+            window = windows[half]
             grads = do_scr[half, at * wide : (at + 1) * wide]
             prob_grads = lax.dot_general(
                 conv_scr[1, keys_rows[half]], grads, NT, preferred_element_type=f32
@@ -319,12 +321,13 @@
             inverse = 1.0 / total
             scaled.append((inverse, weighted * inverse, inverse * scale))
         for slot, (half, at) in enumerate(units):
+            window = windows[half]
             inverse, mean, slope = scaled[slot]
             weights = s_scr[slot, :window]
             cols = slice(at * wide, (at + 1) * wide)
             p_scr[half, :window, cols] = (weights * inverse).astype(bf16)
             ds_scr[half, :window, cols] = (weights * slope * (dp_scr[slot, :window] - mean)).astype(bf16)
-        for half in range(2):
+        for half, window in enumerate(windows):
             score_grads = ds_scr[half, :window]
             keys_t = conv_scr[0, keys_rows[half]].T
             dq = lax.dot_general(keys_t, score_grads, NN, preferred_element_type=f32).T
@@ -413,14 +416,16 @@
 
     needed = [first_place[half] // span - firsts[half] + 1 for half in range(2)]
     if direct:
-        below, both = 0, jnp.maximum(needed[0], needed[1])
-        for count in [count for count in WINDOWS if count <= ctx_count] + [ctx_count + 1]:
-
-            @pl.when((both > below) & (both <= count))
-            def _(count=count):
-                attend_at_once(count * span)
-
-            below = count
+        done = jnp.bool_(False)
+        for sizes in WINDOWS:
+            sizes = [min(size, ctx_count + 1) for size in sizes]
+            fits = (needed[0] <= sizes[0]) & (needed[1] <= sizes[1])
+
+            @pl.when(fits & jnp.logical_not(done))
+            def _(sizes=sizes):
+                attend_at_once([size * span for size in sizes])
+
+            done = done | fits
     else:
         for half in range(2):
             attend(half, half_rows + half * span, half * (ctx_count - 1 - me) * span)

time: 39.3 us -> 39 us (level); the launches traced: 38.9 us -> 39.1 us
  waiting for transfers between devices: 8.61 us -> 7.79 us
  Pallas kernels: 7.33 us -> 7.91 us
  starting transfers between devices: 21.6 us -> 22.1 us
    ppermute x12, waiting for transfers between devices: 8.07 us -> 7.25 us  [flipped(): return lax.ppermute(array, 'ctx', [(i, i ^ flip) for i in range(ctx_count)])]
    pallas_call x1, Pallas kernels: 2.36 us -> 2.95 us  [shards(): pl.pallas_call(functools.partial(grads_kernel, ctx_count, direct), out_sh...]
    ppermute x12, starting transfers between devices: 19.7 us -> 20.2 us  [flipped(): return lax.ppermute(array, 'ctx', [(i, i ^ flip) for i in range(ctx_count)])]
where the time goes in v4:
time: 39 us; the launch traced here: 39.1 us
  starting transfers between devices  22.1 us (57%)
  Pallas kernels  7.91 us (20%)
  waiting for transfers between devices  7.79 us (20%)
  between operations  0.72 us (2%)
  other arithmetic  0.6 us (2%)
    ppermute x12, starting transfers between devices, flipped(): return lax.ppermute(array, 'ctx', [(i, i ^ flip) for i in range(ctx_count)])  20.2 us
    ppermute x12, waiting for transfers between devices, flipped(): return lax.ppermute(array, 'ctx', [(i, i ^ flip) for i in range(ctx_count)])  7.25 us
    pallas_call x1, Pallas kernels, shards(): pl.pallas_call(functools.partial(grads_kernel, ctx_count, direct), out_sh...  2.95 us
    pallas_call x1, Pallas kernels, shards(): pl.pallas_call(functools.partial(prep_kernel, ctx_count, direct), out_sha...  1.87 us
    ppermute x3, starting transfers between devices, shards(): lax.ppermute(sums, 'tp', [(i, i ^ flip) for i in range(count)])  1.86 us
    pallas_call x1, Pallas kernels, shards(): pl.pallas_call(functools.partial(finish_kernel, ctx_count, direct), out_s...  1.27 us
    pallas_call x1, Pallas kernels, shards(): pl.pallas_call(pack_kernel, grid=(1,), out_shape=jax.ShapeDtypeStruct((ms...  0.91 us
    pallas_call x1, Pallas kernels, shards(): pl.pallas_call(save_kernel, out_shape=jax.ShapeDtypeStruct(q_pre.shape, f...  0.8 us
  transfers between devices with their start and end apart: 15, of which 6 were waited for; matrix products, arithmetic and copies ran while one was open for 0% of the time, Pallas kernels for 10%

profile of v4, /device:TPU:0, one launch (start us, length us, event | category | flops | bytes accessed | tf_op | source)
XLA Modules:
  0.0 39.1 jit_solution(5743589088472501016)
XLA Ops:
  0.6 0.0 copy-start.1
  0.6 0.0 copy-start
  0.7 0.9 %pack.1.own_ref.refs_5_ = bf16[144,256]{1,0:T(8,128)(2,1)S(1)} custom-call(bf16[2,64,128]{2,1,0:T(8,128)(2,1)} %k_ref.1, bf16[2,64,128]{2,1,0:T(8,128)(2,1)} %v_ref.1, bf16[2,64,1024]{2,1,0:T(8,128)(2,1)} %q_hbm.1), custom_call_target="tpu_custom_call" | custom-call | tf_op jit(solution)/shard_map/pack/pallas_call | solution.py:703
  1.6 4.1 %collective-permute-start.3 = (bf16[144,256]{1,0:T(8,128)(2,1)S(1)}, bf16[144,256]{1,0:T(8,128)(2,1)S(1)}, u32[]{:S(2)}, u32[]{:S(2)}) collective-permute-start(bf16[144,256]{1,0:T(8,128)(2,1)S(1)} %pack.1.own_ref.refs_5_), channel_id=1, source_target_pairs={{0,16},{4,20},{8,24},{12,28},{16,0},{20,4},{24,8},{28,12},{1,17},{... | collective-permute-start | bytes 221192 | tf_op jit(solution)/shard_map/ppermute | solution.py:691
  5.7 2.5 %collective-permute-start.2 = (bf16[144,256]{1,0:T(8,128)(2,1)S(1)}, bf16[144,256]{1,0:T(8,128)(2,1)S(1)}, u32[]{:S(2)}, u32[]{:S(2)}) collective-permute-start(bf16[144,256]{1,0:T(8,128)(2,1)S(1)} %pack.1.own_ref.refs_5_), channel_id=1, source_target_pairs={{0,12},{4,8},{8,4},{12,0},{16,28},{20,24},{24,20},{28,16},{1,13},{... | collective-permute-start | bytes 221192 | tf_op jit(solution)/shard_map/ppermute | solution.py:691
  8.2 0.4 %collective-permute-start.1 = (bf16[144,256]{1,0:T(8,128)(2,1)S(1)}, bf16[144,256]{1,0:T(8,128)(2,1)S(1)}, u32[]{:S(2)}, u32[]{:S(2)}) collective-permute-start(bf16[144,256]{1,0:T(8,128)(2,1)S(1)} %pack.1.own_ref.refs_5_), channel_id=1, source_target_pairs={{0,8},{4,12},{8,0},{12,4},{16,24},{20,28},{24,16},{28,20},{1,9},{5... | collective-permute-start | bytes 221192 | tf_op jit(solution)/shard_map/ppermute | solution.py:691
  8.6 0.5 %collective-permute-start = (bf16[144,256]{1,0:T(8,128)(2,1)S(1)}, bf16[144,256]{1,0:T(8,128)(2,1)S(1)}, u32[]{:S(2)}, u32[]{:S(2)}) collective-permute-start(bf16[144,256]{1,0:T(8,128)(2,1)S(1)} %pack.1.own_ref.refs_5_), channel_id=1, source_target_pairs={{0,4},{4,0},{8,12},{12,8},{16,20},{20,16},{24,28},{28,24},{1,5},{5... | collective-permute-start | bytes 221192 | tf_op jit(solution)/shard_map/ppermute | solution.py:691
  9.2 0.0 collective-permute-done.3.refs_6_
  9.2 2.5 %collective-permute-start.6 = (bf16[144,256]{1,0:T(8,128)(2,1)S(1)}, bf16[144,256]{1,0:T(8,128)(2,1)S(1)}, u32[]{:S(2)}, u32[]{:S(2)}) collective-permute-start(bf16[144,256]{1,0:T(8,128)(2,1)S(1)} %collective-permute-done.3.refs_6_), channel_id=1, source_target_pairs={{0,12},{4,8},{8,4},{12,0},{16,28},{20,24},{24,20},{28,16},{1,13},{... | collective-permute-start | bytes 221192 | tf_op jit(solution)/shard_map/ppermute | solution.py:691
  11.7 0.7 %collective-permute-start.5 = (bf16[144,256]{1,0:T(8,128)(2,1)S(1)}, bf16[144,256]{1,0:T(8,128)(2,1)S(1)}, u32[]{:S(2)}, u32[]{:S(2)}) collective-permute-start(bf16[144,256]{1,0:T(8,128)(2,1)S(1)} %collective-permute-done.3.refs_6_), channel_id=1, source_target_pairs={{0,8},{4,12},{8,0},{12,4},{16,24},{20,28},{24,16},{28,20},{1,9},{5... | collective-permute-start | bytes 221192 | tf_op jit(solution)/shard_map/ppermute | solution.py:691
  12.4 0.0 collective-permute-done.2.refs_2_.refs_9_
  12.4 0.9 %collective-permute-start.4 = (bf16[144,256]{1,0:T(8,128)(2,1)S(1)}, bf16[144,256]{1,0:T(8,128)(2,1)S(1)}, u32[]{:S(2)}, u32[]{:S(2)}) collective-permute-start(bf16[144,256]{1,0:T(8,128)(2,1)S(1)} %collective-permute-done.3.refs_6_), channel_id=1, source_target_pairs={{0,4},{4,0},{8,12},{12,8},{16,20},{20,16},{24,28},{28,24},{1,5},{5... | collective-permute-start | bytes 221192 | tf_op jit(solution)/shard_map/ppermute | solution.py:691
  13.3 0.1 collective-permute-done.1.refs_1_.refs_8_
  13.4 0.9 %collective-permute-done.refs_0_.refs_7_ = bf16[144,256]{1,0:T(8,128)(2,1)S(1)} collective-permute-done((bf16[144,256]{1,0:T(8,128)(2,1)S(1)}, bf16[144,256]{1,0:T(8,128)(2,1)S(1)}, u32[]{:S(2)}, u32[]{:S(2)}) %collective-permute-start) | collective-permute-done | bytes 73760 | tf_op jit(solution)/shard_map/ppermute | solution.py:691
  14.3 0.0 copy-done.1
  14.3 0.0 copy-done
  14.3 1.9 %prep.1 = (f32[1040,128]{1,0:T(8,128)S(1)}, f32[1040,128]{1,0:T(8,128)S(1)}, f32[2,8,72,128]{3,2,1,0:T(8,128)S(1)}, bf16[2,512,128]{2,1,0:T(8,128)(2,1)S(1)}, bf16[2,512,128]{2,1,0:T(8,128)(2,1)S(1)}) custom-call(s32[8]{0:T(128)S(1)} %copy-done.1, f32[3,3,128]{2,1,0:T(4,128)S(1)} %copy-done, bf16[2,64,1024]{2,1,0:T(8,128)(2,1)} %q_hbm.1, ...), custom_call_target="tpu_custom_call" | custom-call | tf_op jit(solution)/shard_map/prep/pallas_call | solution.py:737
  16.2 0.0 collective-permute-done.6.refs_12_
  16.2 0.0 collective-permute-done.5.refs_11_
  16.2 0.5 %collective-permute-done.4.refs_10_ = bf16[144,256]{1,0:T(8,128)(2,1)S(1)} collective-permute-done((bf16[144,256]{1,0:T(8,128)(2,1)S(1)}, bf16[144,256]{1,0:T(8,128)(2,1)S(1)}, u32[]{:S(2)}, u32[]{:S(2)}) %collective-permute-start.4) | collective-permute-done | bytes 73760 | tf_op jit(solution)/shard_map/ppermute | solution.py:691
  16.7 2.9 %grads.1 = (f32[2,64,1024]{2,1,0:T(8,128)S(1)}, f32[2,8,1024]{2,1,0:T(8,128)S(1)}, f32[128,256]{1,0:T(8,128)S(1)}, f32[136,256]{1,0:T(8,128)S(1)}, bf16[224,256]...) custom-call(s32[8]{0:T(128)S(1)} %copy-done.1, ...), custom_call_target="tpu_custom_call" | custom-call | tf_op jit(solution)/shard_map/grads/pallas_call | solution.py:772
  19.7 0.5 %collective-permute-start.7 = (bf16[224,256]{1,0:T(8,128)(2,1)S(1)}, bf16[224,256]{1,0:T(8,128)(2,1)S(1)}, u32[]{:S(2)}, u32[]{:S(2)}) collective-permute-start(bf16[224,256]{1,0:T(8,128)(2,1)S(1)} %get-tuple-element.34), channel_id=1, source_target_pairs={{0,4},{4,0},{8,12},{12,8},{16,20},{20,16},{24,28},{28,24},{1,5},{5... | collective-permute-start | bytes 344072 | tf_op jit(solution)/shard_map/ppermute | solution.py:691
  20.2 1.7 %collective-permute-start.8 = (bf16[208,256]{1,0:T(8,128)(2,1)S(1)}, bf16[208,256]{1,0:T(8,128)(2,1)S(1)}, u32[]{:S(2)}, u32[]{:S(2)}) collective-permute-start(bf16[208,256]{1,0:T(8,128)(2,1)S(1)} %get-tuple-element.35), channel_id=1, source_target_pairs={{0,8},{4,12},{8,0},{12,4},{16,24},{20,28},{24,16},{28,20},{1,9},{5... | collective-permute-start | bytes 319496 | tf_op jit(solution)/shard_map/ppermute | solution.py:691
  21.9 1.3 %collective-permute-start.9 = (bf16[160,256]{1,0:T(8,128)(2,1)S(1)}, bf16[160,256]{1,0:T(8,128)(2,1)S(1)}, u32[]{:S(2)}, u32[]{:S(2)}) collective-permute-start(bf16[160,256]{1,0:T(8,128)(2,1)S(1)} %get-tuple-element.36), channel_id=1, source_target_pairs={{0,12},{4,8},{8,4},{12,0},{16,28},{20,24},{24,20},{28,16},{1,13},{... | collective-permute-start | bytes 245768 | tf_op jit(solution)/shard_map/ppermute | solution.py:691
  23.2 0.8 %save.1.dq_in_hbm = f32[2,64,1024]{2,1,0:T(8,128)} custom-call(f32[2,64,1024]{2,1,0:T(8,128)S(1)} %get-tuple-element.33.source_ref), custom_call_target="tpu_custom_call" | custom-call | tf_op jit(solution)/shard_map/save/pallas_call | solution.py:783
  24.0 3.2 %collective-permute-done.9.refs_2_ = bf16[160,256]{1,0:T(8,128)(2,1)S(1)} collective-permute-done((bf16[160,256]{1,0:T(8,128)(2,1)S(1)}, bf16[160,256]{1,0:T(8,128)(2,1)S(1)}, u32[]{:S(2)}, u32[]{:S(2)}) %collective-permute-start.9) | collective-permute-done | bytes 81952 | tf_op jit(solution)/shard_map/ppermute | solution.py:691
  27.2 0.0 collective-permute-done.8.refs_1_
  27.2 0.0 collective-permute-done.7.refs_0_
  27.2 0.1 merge.1
  27.4 4.1 %collective-permute-start.10 = (bf16[160,256]{1,0:T(8,128)(2,1)S(1)}, bf16[160,256]{1,0:T(8,128)(2,1)S(1)}, u32[]{:S(2)}, u32[]{:S(2)}) collective-permute-start(bf16[160,256]{1,0:T(8,128)(2,1)S(1)} %get-tuple-element.45), channel_id=1, source_target_pairs={{0,16},{4,20},{8,24},{12,28},{16,0},{20,4},{24,8},{28,12},{1,17},{... | collective-permute-start | bytes 245768 | tf_op jit(solution)/shard_map/ppermute | solution.py:691
  31.5 0.8 %collective-permute-start.11 = (bf16[80,256]{1,0:T(8,128)(2,1)S(1)}, bf16[80,256]{1,0:T(8,128)(2,1)S(1)}, u32[]{:S(2)}, u32[]{:S(2)}) collective-permute-start(bf16[80,256]{1,0:T(8,128)(2,1)S(1)} %get-tuple-element.47), channel_id=1, source_target_pairs={{0,12},{4,8},{8,4},{12,0},{16,28},{20,24},{24,20},{28,16},{1,13},{... | collective-permute-start | bytes 122888 | tf_op jit(solution)/shard_map/ppermute | solution.py:691
  32.3 2.5 %collective-permute-done.10.far_ref = bf16[160,256]{1,0:T(8,128)(2,1)S(1)} collective-permute-done((bf16[160,256]{1,0:T(8,128)(2,1)S(1)}, bf16[160,256]{1,0:T(8,128)(2,1)S(1)}, u32[]{:S(2)}, u32[]{:S(2)}) %collective-permute-start.10) | collective-permute-done | bytes 81952 | tf_op jit(solution)/shard_map/ppermute | solution.py:691
  34.8 0.0 collective-permute-start.14
  34.8 1.6 %collective-permute-start.13 = (f32[3,3,128]{2,1,0:T(4,128)S(1)}, f32[3,3,128]{2,1,0:T(4,128)S(1)}, u32[]{:S(2)}, u32[]{:S(2)}) collective-permute-start(f32[3,3,128]{2,1,0:T(4,128)S(1)} %sums.1), channel_id=1, source_target_pairs={{0,2},{1,3},{2,0},{3,1},{4,6},{5,7},{6,4},{7,5},{8,10},{9,11},{10,... | collective-permute-start | bytes 13832 | tf_op jit(solution)/shard_map/ppermute | solution.py:826
  36.4 0.3 collective-permute-start.12
  36.7 0.0 collective-permute-done.11.refs_0_
  36.7 1.3 %finish.1 = (f32[2,64,1024]{2,1,0:T(8,128)}, f32[2,64,128]{2,1,0:T(8,128)}, f32[2,64,128]{2,1,0:T(8,128)}) custom-call(s32[8]{0:T(128)S(1)} %copy-done.1, f32[3,3,128]{2,1,0:T(4,128)S(1)} %copy-done, f32[2,64,1024]{2,1,0:T(8,128)} %save.1.dq_in_hbm, f32[2,8,1024]{2,1,0:T(8,128)S(1)} %get-tuple-element.38.tail_ref, ...), custom_call_target="tpu_custom_call", output_to_operand_aliasing={{0}: (2, {})} | custom-call | tf_op jit(solution)/shard_map/finish/pallas_call | solution.py:828
  37.9 0.0 collective-permute-done.14
  38.0 0.5 %collective-permute-done.13 = f32[3,3,128]{2,1,0:T(4,128)S(1)} collective-permute-done((f32[3,3,128]{2,1,0:T(4,128)S(1)}, f32[3,3,128]{2,1,0:T(4,128)S(1)}, u32[]{:S(2)}, u32[]{:S(2)}) %collective-permute-start.13) | collective-permute-done | bytes 4640 | tf_op jit(solution)/shard_map/ppermute | solution.py:826
  38.5 0.0 collective-permute-done.12
  38.5 0.6 %add_add_fusion = f32[3,3,128]{2,1,0:T(4,128)} fusion(f32[3,3,128]{2,1,0:T(4,128)S(1)} %collective-permute-done.13, f32[3,3,128]{2,1,0:T(4,128)S(1)} %collective-permute-done.14, f32[3,3,128]{2,1,0:T(4,128)S(1)} %sums.1, f32[3,3,128]{2,1,0:T(4,128)S(1)} %collective-permute-done.12), kind=kLoop, calls=%fused_computation | loop fusion | flops 3456 | bytes 23040 | tf_op jit(solution)/shard_map/add | solution.py:849
  (1 shorter events, 0.0 us)
Async XLA Ops:
  0.6 13.7 %copy-start.1 = (s32[8]{0:T(128)S(1)}, s32[8]{0:T(128)}, u32[]{:S(2)}) copy-start(s32[8]{0:T(128)} %lengths_ref.5) | copy-start | bytes 100
  0.6 13.7 %copy-start = (f32[3,3,128]{2,1,0:T(4,128)S(1)}, f32[3,3,128]{2,1,0:T(4,128)}, u32[]{:S(2)}) copy-start(f32[3,3,128]{2,1,0:T(4,128)} %filters_ref.5) | copy-start | bytes 13828
  1.6 7.6 %collective-permute-start.3 = (bf16[144,256]{1,0:T(8,128)(2,1)S(1)}, bf16[144,256]{1,0:T(8,128)(2,1)S(1)}, u32[]{:S(2)}, u32[]{:S(2)}) collective-permute-start(bf16[144,256]{1,0:T(8,128)(2,1)S(1)} %pack.1.own_ref.refs_5_), channel_id=1, source_target_pairs={{0,16},{4,20},{8,24},{12,28},{16,0},{20,4},{24,8},{28,12},{1,17},{... | collective-permute-start | bytes 221192 | tf_op jit(solution)/shard_map/ppermute | solution.py:691
  5.7 6.7 %collective-permute-start.2 = (bf16[144,256]{1,0:T(8,128)(2,1)S(1)}, bf16[144,256]{1,0:T(8,128)(2,1)S(1)}, u32[]{:S(2)}, u32[]{:S(2)}) collective-permute-start(bf16[144,256]{1,0:T(8,128)(2,1)S(1)} %pack.1.own_ref.refs_5_), channel_id=1, source_target_pairs={{0,12},{4,8},{8,4},{12,0},{16,28},{20,24},{24,20},{28,16},{1,13},{... | collective-permute-start | bytes 221192 | tf_op jit(solution)/shard_map/ppermute | solution.py:691
  8.2 5.2 %collective-permute-start.1 = (bf16[144,256]{1,0:T(8,128)(2,1)S(1)}, bf16[144,256]{1,0:T(8,128)(2,1)S(1)}, u32[]{:S(2)}, u32[]{:S(2)}) collective-permute-start(bf16[144,256]{1,0:T(8,128)(2,1)S(1)} %pack.1.own_ref.refs_5_), channel_id=1, source_target_pairs={{0,8},{4,12},{8,0},{12,4},{16,24},{20,28},{24,16},{28,20},{1,9},{5... | collective-permute-start | bytes 221192 | tf_op jit(solution)/shard_map/ppermute | solution.py:691
  8.6 5.7 %collective-permute-start = (bf16[144,256]{1,0:T(8,128)(2,1)S(1)}, bf16[144,256]{1,0:T(8,128)(2,1)S(1)}, u32[]{:S(2)}, u32[]{:S(2)}) collective-permute-start(bf16[144,256]{1,0:T(8,128)(2,1)S(1)} %pack.1.own_ref.refs_5_), channel_id=1, source_target_pairs={{0,4},{4,0},{8,12},{12,8},{16,20},{20,16},{24,28},{28,24},{1,5},{5... | collective-permute-start | bytes 221192 | tf_op jit(solution)/shard_map/ppermute | solution.py:691
  9.2 7.0 %collective-permute-start.6 = (bf16[144,256]{1,0:T(8,128)(2,1)S(1)}, bf16[144,256]{1,0:T(8,128)(2,1)S(1)}, u32[]{:S(2)}, u32[]{:S(2)}) collective-permute-start(bf16[144,256]{1,0:T(8,128)(2,1)S(1)} %collective-permute-done.3.refs_6_), channel_id=1, source_target_pairs={{0,12},{4,8},{8,4},{12,0},{16,28},{20,24},{24,20},{28,16},{1,13},{... | collective-permute-start | bytes 221192 | tf_op jit(solution)/shard_map/ppermute | solution.py:691
  11.7 4.5 %collective-permute-start.5 = (bf16[144,256]{1,0:T(8,128)(2,1)S(1)}, bf16[144,256]{1,0:T(8,128)(2,1)S(1)}, u32[]{:S(2)}, u32[]{:S(2)}) collective-permute-start(bf16[144,256]{1,0:T(8,128)(2,1)S(1)} %collective-permute-done.3.refs_6_), channel_id=1, source_target_pairs={{0,8},{4,12},{8,0},{12,4},{16,24},{20,28},{24,16},{28,20},{1,9},{5... | collective-permute-start | bytes 221192 | tf_op jit(solution)/shard_map/ppermute | solution.py:691
  12.4 4.4 %collective-permute-start.4 = (bf16[144,256]{1,0:T(8,128)(2,1)S(1)}, bf16[144,256]{1,0:T(8,128)(2,1)S(1)}, u32[]{:S(2)}, u32[]{:S(2)}) collective-permute-start(bf16[144,256]{1,0:T(8,128)(2,1)S(1)} %collective-permute-done.3.refs_6_), channel_id=1, source_target_pairs={{0,4},{4,0},{8,12},{12,8},{16,20},{20,16},{24,28},{28,24},{1,5},{5... | collective-permute-start | bytes 221192 | tf_op jit(solution)/shard_map/ppermute | solution.py:691
  19.7 7.6 %collective-permute-start.7 = (bf16[224,256]{1,0:T(8,128)(2,1)S(1)}, bf16[224,256]{1,0:T(8,128)(2,1)S(1)}, u32[]{:S(2)}, u32[]{:S(2)}) collective-permute-start(bf16[224,256]{1,0:T(8,128)(2,1)S(1)} %get-tuple-element.34), channel_id=1, source_target_pairs={{0,4},{4,0},{8,12},{12,8},{16,20},{20,16},{24,28},{28,24},{1,5},{5... | collective-permute-start | bytes 344072 | tf_op jit(solution)/shard_map/ppermute | solution.py:691
  20.2 7.1 %collective-permute-start.8 = (bf16[208,256]{1,0:T(8,128)(2,1)S(1)}, bf16[208,256]{1,0:T(8,128)(2,1)S(1)}, u32[]{:S(2)}, u32[]{:S(2)}) collective-permute-start(bf16[208,256]{1,0:T(8,128)(2,1)S(1)} %get-tuple-element.35), channel_id=1, source_target_pairs={{0,8},{4,12},{8,0},{12,4},{16,24},{20,28},{24,16},{28,20},{1,9},{5... | collective-permute-start | bytes 319496 | tf_op jit(solution)/shard_map/ppermute | solution.py:691
  21.9 5.3 %collective-permute-start.9 = (bf16[160,256]{1,0:T(8,128)(2,1)S(1)}, bf16[160,256]{1,0:T(8,128)(2,1)S(1)}, u32[]{:S(2)}, u32[]{:S(2)}) collective-permute-start(bf16[160,256]{1,0:T(8,128)(2,1)S(1)} %get-tuple-element.36), channel_id=1, source_target_pairs={{0,12},{4,8},{8,4},{12,0},{16,28},{20,24},{24,20},{28,16},{1,13},{... | collective-permute-start | bytes 245768 | tf_op jit(solution)/shard_map/ppermute | solution.py:691
  27.4 7.4 %collective-permute-start.10 = (bf16[160,256]{1,0:T(8,128)(2,1)S(1)}, bf16[160,256]{1,0:T(8,128)(2,1)S(1)}, u32[]{:S(2)}, u32[]{:S(2)}) collective-permute-start(bf16[160,256]{1,0:T(8,128)(2,1)S(1)} %get-tuple-element.45), channel_id=1, source_target_pairs={{0,16},{4,20},{8,24},{12,28},{16,0},{20,4},{24,8},{28,12},{1,17},{... | collective-permute-start | bytes 245768 | tf_op jit(solution)/shard_map/ppermute | solution.py:691
  31.5 5.2 %collective-permute-start.11 = (bf16[80,256]{1,0:T(8,128)(2,1)S(1)}, bf16[80,256]{1,0:T(8,128)(2,1)S(1)}, u32[]{:S(2)}, u32[]{:S(2)}) collective-permute-start(bf16[80,256]{1,0:T(8,128)(2,1)S(1)} %get-tuple-element.47), channel_id=1, source_target_pairs={{0,12},{4,8},{8,4},{12,0},{16,28},{20,24},{24,20},{28,16},{1,13},{... | collective-permute-start | bytes 122888 | tf_op jit(solution)/shard_map/ppermute | solution.py:691
  34.8 3.1 %collective-permute-start.14 = (f32[3,3,128]{2,1,0:T(4,128)S(1)}, f32[3,3,128]{2,1,0:T(4,128)S(1)}, u32[]{:S(2)}, u32[]{:S(2)}) collective-permute-start(f32[3,3,128]{2,1,0:T(4,128)S(1)} %sums.1), channel_id=1, source_target_pairs={{0,3},{1,2},{2,1},{3,0},{4,7},{5,6},{6,5},{7,4},{8,11},{9,10},{10,... | collective-permute-start | bytes 13832 | tf_op jit(solution)/shard_map/ppermute | solution.py:826
  34.8 3.7 %collective-permute-start.13 = (f32[3,3,128]{2,1,0:T(4,128)S(1)}, f32[3,3,128]{2,1,0:T(4,128)S(1)}, u32[]{:S(2)}, u32[]{:S(2)}) collective-permute-start(f32[3,3,128]{2,1,0:T(4,128)S(1)} %sums.1), channel_id=1, source_target_pairs={{0,2},{1,3},{2,0},{3,1},{4,6},{5,7},{6,4},{7,5},{8,10},{9,11},{10,... | collective-permute-start | bytes 13832 | tf_op jit(solution)/shard_map/ppermute | solution.py:826
  36.4 2.1 %collective-permute-start.12 = (f32[3,3,128]{2,1,0:T(4,128)S(1)}, f32[3,3,128]{2,1,0:T(4,128)S(1)}, u32[]{:S(2)}, u32[]{:S(2)}) collective-permute-start(f32[3,3,128]{2,1,0:T(4,128)S(1)} %sums.1), channel_id=1, source_target_pairs={{0,1},{1,0},{2,3},{3,2},{4,5},{5,4},{6,7},{7,6},{8,9},{9,8},{10,11... | collective-permute-start | bytes 13832 | tf_op jit(solution)/shard_map/ppermute | solution.py:826

commit v5 on v4

--- a/solution.py
+++ b/solution.py
@@ -16,7 +16,7 @@
 MAX_CHUNK = 640
 RIM = 8
 MAX_DIRECT = 4
-WINDOWS = ((2, 2), (4, 4), (6, 6), (4, 9), (9, 4), (9, 9))
+WINDOWS = ((2, 2), (4, 4), (2, 9), (6, 6), (4, 9), (9, 4), (6, 9), (9, 9))
 MIB = 1 << 20
 
 
@@ -75,8 +75,17 @@
     return lax.bitwise_xor(me, jnp.int32(flip))
 
 
-def pack_kernel(k_ref, v_ref, q_ref, out_ref):
+def pack_kernel(k_hbm, v_hbm, q_hbm, out_ref, k_ref, v_ref, q_ref, sems):
     span = k_ref.shape[1]
+    loads = [
+        pltpu.make_async_copy(k_hbm, k_ref, sems.at[0]),
+        pltpu.make_async_copy(v_hbm, v_ref, sems.at[1]),
+        pltpu.make_async_copy(q_hbm.at[:, pl.ds(span - TAIL, TAIL)], q_ref, sems.at[2]),
+    ]
+    for load in loads:
+        load.start()
+    for load in loads:
+        load.wait()
     kv = jnp.concatenate([k_ref[...], v_ref[...]], axis=2).reshape(2 * span, 2 * LANES)
     tails = []
     for half in range(2):
@@ -702,14 +711,15 @@
 
     packed = pl.pallas_call(
         pack_kernel,
-        grid=(1,),
         out_shape=jax.ShapeDtypeStruct((msg_rows, 2 * LANES), bf16),
-        in_specs=[
-            whole(k_pre.shape),
-            whole(k_pre.shape),
-            pl.BlockSpec((2, TAIL, width), lambda i: (0, span // TAIL - 1, 0)),
+        in_specs=[hbm] * 3,
+        out_specs=vmem,
+        scratch_shapes=[
+            pltpu.VMEM(k_pre.shape, bf16),
+            pltpu.VMEM(k_pre.shape, bf16),
+            pltpu.VMEM((2, TAIL, width), bf16),
+            pltpu.SemaphoreType.DMA((3,)),
         ],
-        out_specs=whole((msg_rows, 2 * LANES)),
         compiler_params=pltpu.CompilerParams(vmem_limit_bytes=4 * MIB),
         name="pack",
     )(*[in_hbm(array) for array in (k_pre, value_before_filter, q_pre)])

time: 39 us -> 39.2 us (level)
  waiting for transfers between devices: 7.79 us -> 8.53 us
  starting transfers between devices: 22.1 us -> 21.5 us
    ppermute x12, waiting for transfers between devices: 7.25 us -> 7.99 us  [flipped(): return lax.ppermute(array, 'ctx', [(i, i ^ flip) for i in range(ctx_count)])]
    ppermute x12, starting transfers between devices: 20.2 us -> 19.7 us  [flipped(): return lax.ppermute(array, 'ctx', [(i, i ^ flip) for i in range(ctx_count)])]
where the time goes in v5:
time: 39.2 us; the launch traced here: 38.9 us
  starting transfers between devices  21.5 us (55%)
  waiting for transfers between devices  8.53 us (22%)
  Pallas kernels  7.55 us (19%)
  between operations  0.73 us (2%)
  other arithmetic  0.6 us (2%)
    ppermute x12, starting transfers between devices, flipped(): return lax.ppermute(array, 'ctx', [(i, i ^ flip) for i in range(ctx_count)])  19.7 us
    ppermute x12, waiting for transfers between devices, flipped(): return lax.ppermute(array, 'ctx', [(i, i ^ flip) for i in range(ctx_count)])  7.99 us
    pallas_call x1, Pallas kernels, shards(): pl.pallas_call(functools.partial(grads_kernel, ctx_count, direct), out_sh...  2.56 us
    pallas_call x1, Pallas kernels, shards(): pl.pallas_call(functools.partial(prep_kernel, ctx_count, direct), out_sha...  1.87 us
    ppermute x3, starting transfers between devices, shards(): lax.ppermute(sums, 'tp', [(i, i ^ flip) for i in range(count)])  1.86 us
    pallas_call x1, Pallas kernels, shards(): pl.pallas_call(functools.partial(finish_kernel, ctx_count, direct), out_s...  1.27 us
    pallas_call x1, Pallas kernels, shards(): pl.pallas_call(pack_kernel, out_shape=jax.ShapeDtypeStruct((msg_rows, 2 *...  0.93 us
    pallas_call x1, Pallas kernels, shards(): pl.pallas_call(save_kernel, out_shape=jax.ShapeDtypeStruct(q_pre.shape, f...  0.8 us
  transfers between devices with their start and end apart: 15, of which 6 were waited for; matrix products, arithmetic and copies ran while one was open for 0% of the time, Pallas kernels for 10%

profile of v5, /device:TPU:0, one launch (start us, length us, event | category | flops | bytes accessed | tf_op | source)
XLA Modules:
  0.0 38.9 jit_solution(7722917536124938612)
XLA Ops:
  0.6 0.0 copy-start.1
  0.6 0.0 copy-start
  0.7 0.9 %pack.1.own_ref.refs_5_ = bf16[144,256]{1,0:T(8,128)(2,1)S(1)} custom-call(bf16[2,64,128]{2,1,0:T(8,128)(2,1)} %k_hbm.1, bf16[2,64,128]{2,1,0:T(8,128)(2,1)} %v_hbm.1, bf16[2,64,1024]{2,1,0:T(8,128)(2,1)} %q_hbm.3), custom_call_target="tpu_custom_call" | custom-call | tf_op jit(solution)/shard_map/pack/pallas_call | solution.py:712
  1.6 4.1 %collective-permute-start.3 = (bf16[144,256]{1,0:T(8,128)(2,1)S(1)}, bf16[144,256]{1,0:T(8,128)(2,1)S(1)}, u32[]{:S(2)}, u32[]{:S(2)}) collective-permute-start(bf16[144,256]{1,0:T(8,128)(2,1)S(1)} %pack.1.own_ref.refs_5_), channel_id=1, source_target_pairs={{0,16},{4,20},{8,24},{12,28},{16,0},{20,4},{24,8},{28,12},{1,17},{... | collective-permute-start | bytes 221192 | tf_op jit(solution)/shard_map/ppermute | solution.py:700
  5.7 2.5 %collective-permute-start.2 = (bf16[144,256]{1,0:T(8,128)(2,1)S(1)}, bf16[144,256]{1,0:T(8,128)(2,1)S(1)}, u32[]{:S(2)}, u32[]{:S(2)}) collective-permute-start(bf16[144,256]{1,0:T(8,128)(2,1)S(1)} %pack.1.own_ref.refs_5_), channel_id=1, source_target_pairs={{0,12},{4,8},{8,4},{12,0},{16,28},{20,24},{24,20},{28,16},{1,13},{... | collective-permute-start | bytes 221192 | tf_op jit(solution)/shard_map/ppermute | solution.py:700
  8.2 0.4 %collective-permute-start.1 = (bf16[144,256]{1,0:T(8,128)(2,1)S(1)}, bf16[144,256]{1,0:T(8,128)(2,1)S(1)}, u32[]{:S(2)}, u32[]{:S(2)}) collective-permute-start(bf16[144,256]{1,0:T(8,128)(2,1)S(1)} %pack.1.own_ref.refs_5_), channel_id=1, source_target_pairs={{0,8},{4,12},{8,0},{12,4},{16,24},{20,28},{24,16},{28,20},{1,9},{5... | collective-permute-start | bytes 221192 | tf_op jit(solution)/shard_map/ppermute | solution.py:700
  8.6 0.5 %collective-permute-start = (bf16[144,256]{1,0:T(8,128)(2,1)S(1)}, bf16[144,256]{1,0:T(8,128)(2,1)S(1)}, u32[]{:S(2)}, u32[]{:S(2)}) collective-permute-start(bf16[144,256]{1,0:T(8,128)(2,1)S(1)} %pack.1.own_ref.refs_5_), channel_id=1, source_target_pairs={{0,4},{4,0},{8,12},{12,8},{16,20},{20,16},{24,28},{28,24},{1,5},{5... | collective-permute-start | bytes 221192 | tf_op jit(solution)/shard_map/ppermute | solution.py:700
  9.2 0.0 collective-permute-done.3.refs_6_
  9.2 2.5 %collective-permute-start.6 = (bf16[144,256]{1,0:T(8,128)(2,1)S(1)}, bf16[144,256]{1,0:T(8,128)(2,1)S(1)}, u32[]{:S(2)}, u32[]{:S(2)}) collective-permute-start(bf16[144,256]{1,0:T(8,128)(2,1)S(1)} %collective-permute-done.3.refs_6_), channel_id=1, source_target_pairs={{0,12},{4,8},{8,4},{12,0},{16,28},{20,24},{24,20},{28,16},{1,13},{... | collective-permute-start | bytes 221192 | tf_op jit(solution)/shard_map/ppermute | solution.py:700
  11.7 0.7 %collective-permute-start.5 = (bf16[144,256]{1,0:T(8,128)(2,1)S(1)}, bf16[144,256]{1,0:T(8,128)(2,1)S(1)}, u32[]{:S(2)}, u32[]{:S(2)}) collective-permute-start(bf16[144,256]{1,0:T(8,128)(2,1)S(1)} %collective-permute-done.3.refs_6_), channel_id=1, source_target_pairs={{0,8},{4,12},{8,0},{12,4},{16,24},{20,28},{24,16},{28,20},{1,9},{5... | collective-permute-start | bytes 221192 | tf_op jit(solution)/shard_map/ppermute | solution.py:700
  12.4 0.0 collective-permute-done.2.refs_2_.refs_9_
  12.4 0.9 %collective-permute-start.4 = (bf16[144,256]{1,0:T(8,128)(2,1)S(1)}, bf16[144,256]{1,0:T(8,128)(2,1)S(1)}, u32[]{:S(2)}, u32[]{:S(2)}) collective-permute-start(bf16[144,256]{1,0:T(8,128)(2,1)S(1)} %collective-permute-done.3.refs_6_), channel_id=1, source_target_pairs={{0,4},{4,0},{8,12},{12,8},{16,20},{20,16},{24,28},{28,24},{1,5},{5... | collective-permute-start | bytes 221192 | tf_op jit(solution)/shard_map/ppermute | solution.py:700
  13.3 0.1 collective-permute-done.1.refs_1_.refs_8_
  13.4 0.9 %collective-permute-done.refs_0_.refs_7_ = bf16[144,256]{1,0:T(8,128)(2,1)S(1)} collective-permute-done((bf16[144,256]{1,0:T(8,128)(2,1)S(1)}, bf16[144,256]{1,0:T(8,128)(2,1)S(1)}, u32[]{:S(2)}, u32[]{:S(2)}) %collective-permute-start) | collective-permute-done | bytes 73760 | tf_op jit(solution)/shard_map/ppermute | solution.py:700
  14.3 0.0 copy-done.1
  14.3 0.0 copy-done
  14.3 1.9 %prep.1 = (f32[1040,128]{1,0:T(8,128)S(1)}, f32[1040,128]{1,0:T(8,128)S(1)}, f32[2,8,72,128]{3,2,1,0:T(8,128)S(1)}, bf16[2,512,128]{2,1,0:T(8,128)(2,1)S(1)}, bf16[2,512,128]{2,1,0:T(8,128)(2,1)S(1)}) custom-call(s32[8]{0:T(128)S(1)} %copy-done.1, f32[3,3,128]{2,1,0:T(4,128)S(1)} %copy-done, bf16[2,64,1024]{2,1,0:T(8,128)(2,1)} %q_hbm.3, ...), custom_call_target="tpu_custom_call" | custom-call | tf_op jit(solution)/shard_map/prep/pallas_call | solution.py:747
  16.2 0.0 collective-permute-done.6.refs_12_
  16.2 0.0 collective-permute-done.5.refs_11_
  16.2 0.5 %collective-permute-done.4.refs_10_ = bf16[144,256]{1,0:T(8,128)(2,1)S(1)} collective-permute-done((bf16[144,256]{1,0:T(8,128)(2,1)S(1)}, bf16[144,256]{1,0:T(8,128)(2,1)S(1)}, u32[]{:S(2)}, u32[]{:S(2)}) %collective-permute-start.4) | collective-permute-done | bytes 73760 | tf_op jit(solution)/shard_map/ppermute | solution.py:700
  16.8 2.6 %grads.1 = (f32[2,64,1024]{2,1,0:T(8,128)S(1)}, f32[2,8,1024]{2,1,0:T(8,128)S(1)}, f32[128,256]{1,0:T(8,128)S(1)}, f32[136,256]{1,0:T(8,128)S(1)}, bf16[224,256]...) custom-call(s32[8]{0:T(128)S(1)} %copy-done.1, ...), custom_call_target="tpu_custom_call" | custom-call | tf_op jit(solution)/shard_map/grads/pallas_call | solution.py:782
  19.3 2.4 %collective-permute-start.7 = (bf16[224,256]{1,0:T(8,128)(2,1)S(1)}, bf16[224,256]{1,0:T(8,128)(2,1)S(1)}, u32[]{:S(2)}, u32[]{:S(2)}) collective-permute-start(bf16[224,256]{1,0:T(8,128)(2,1)S(1)} %get-tuple-element.34), channel_id=1, source_target_pairs={{0,4},{4,0},{8,12},{12,8},{16,20},{20,16},{24,28},{28,24},{1,5},{5... | collective-permute-start | bytes 344072 | tf_op jit(solution)/shard_map/ppermute | solution.py:700
  21.8 1.1 %collective-permute-start.8 = (bf16[208,256]{1,0:T(8,128)(2,1)S(1)}, bf16[208,256]{1,0:T(8,128)(2,1)S(1)}, u32[]{:S(2)}, u32[]{:S(2)}) collective-permute-start(bf16[208,256]{1,0:T(8,128)(2,1)S(1)} %get-tuple-element.35), channel_id=1, source_target_pairs={{0,8},{4,12},{8,0},{12,4},{16,24},{20,28},{24,16},{28,20},{1,9},{5... | collective-permute-start | bytes 319496 | tf_op jit(solution)/shard_map/ppermute | solution.py:700
  22.9 0.7 %collective-permute-start.9 = (bf16[160,256]{1,0:T(8,128)(2,1)S(1)}, bf16[160,256]{1,0:T(8,128)(2,1)S(1)}, u32[]{:S(2)}, u32[]{:S(2)}) collective-permute-start(bf16[160,256]{1,0:T(8,128)(2,1)S(1)} %get-tuple-element.36), channel_id=1, source_target_pairs={{0,12},{4,8},{8,4},{12,0},{16,28},{20,24},{24,20},{28,16},{1,13},{... | collective-permute-start | bytes 245768 | tf_op jit(solution)/shard_map/ppermute | solution.py:700
  23.6 0.8 %save.1.dq_in_hbm = f32[2,64,1024]{2,1,0:T(8,128)} custom-call(f32[2,64,1024]{2,1,0:T(8,128)S(1)} %get-tuple-element.33.source_ref), custom_call_target="tpu_custom_call" | custom-call | tf_op jit(solution)/shard_map/save/pallas_call | solution.py:793
  24.4 3.9 %collective-permute-done.9.refs_2_ = bf16[160,256]{1,0:T(8,128)(2,1)S(1)} collective-permute-done((bf16[160,256]{1,0:T(8,128)(2,1)S(1)}, bf16[160,256]{1,0:T(8,128)(2,1)S(1)}, u32[]{:S(2)}, u32[]{:S(2)}) %collective-permute-start.9) | collective-permute-done | bytes 81952 | tf_op jit(solution)/shard_map/ppermute | solution.py:700
  28.2 0.0 collective-permute-done.8.refs_1_
  28.2 0.0 collective-permute-done.7.refs_0_
  28.2 0.1 merge.1
  28.4 1.9 %collective-permute-start.10 = (bf16[160,256]{1,0:T(8,128)(2,1)S(1)}, bf16[160,256]{1,0:T(8,128)(2,1)S(1)}, u32[]{:S(2)}, u32[]{:S(2)}) collective-permute-start(bf16[160,256]{1,0:T(8,128)(2,1)S(1)} %get-tuple-element.45), channel_id=1, source_target_pairs={{0,16},{4,20},{8,24},{12,28},{16,0},{20,4},{24,8},{28,12},{1,17},{... | collective-permute-start | bytes 245768 | tf_op jit(solution)/shard_map/ppermute | solution.py:700
  30.3 1.8 %collective-permute-start.11 = (bf16[80,256]{1,0:T(8,128)(2,1)S(1)}, bf16[80,256]{1,0:T(8,128)(2,1)S(1)}, u32[]{:S(2)}, u32[]{:S(2)}) collective-permute-start(bf16[80,256]{1,0:T(8,128)(2,1)S(1)} %get-tuple-element.47), channel_id=1, source_target_pairs={{0,12},{4,8},{8,4},{12,0},{16,28},{20,24},{24,20},{28,16},{1,13},{... | collective-permute-start | bytes 122888 | tf_op jit(solution)/shard_map/ppermute | solution.py:700
  32.1 2.6 %collective-permute-done.10.far_ref = bf16[160,256]{1,0:T(8,128)(2,1)S(1)} collective-permute-done((bf16[160,256]{1,0:T(8,128)(2,1)S(1)}, bf16[160,256]{1,0:T(8,128)(2,1)S(1)}, u32[]{:S(2)}, u32[]{:S(2)}) %collective-permute-start.10) | collective-permute-done | bytes 81952 | tf_op jit(solution)/shard_map/ppermute | solution.py:700
  34.6 0.0 collective-permute-start.14
  34.7 1.6 %collective-permute-start.13 = (f32[3,3,128]{2,1,0:T(4,128)S(1)}, f32[3,3,128]{2,1,0:T(4,128)S(1)}, u32[]{:S(2)}, u32[]{:S(2)}) collective-permute-start(f32[3,3,128]{2,1,0:T(4,128)S(1)} %sums.1), channel_id=1, source_target_pairs={{0,2},{1,3},{2,0},{3,1},{4,6},{5,7},{6,4},{7,5},{8,10},{9,11},{10,... | collective-permute-start | bytes 13832 | tf_op jit(solution)/shard_map/ppermute | solution.py:836
  36.2 0.3 collective-permute-start.12
  36.5 0.0 collective-permute-done.11.refs_0_
  36.5 1.3 %finish.1 = (f32[2,64,1024]{2,1,0:T(8,128)}, f32[2,64,128]{2,1,0:T(8,128)}, f32[2,64,128]{2,1,0:T(8,128)}) custom-call(s32[8]{0:T(128)S(1)} %copy-done.1, f32[3,3,128]{2,1,0:T(4,128)S(1)} %copy-done, f32[2,64,1024]{2,1,0:T(8,128)} %save.1.dq_in_hbm, f32[2,8,1024]{2,1,0:T(8,128)S(1)} %get-tuple-element.38.tail_ref, ...), custom_call_target="tpu_custom_call", output_to_operand_aliasing={{0}: (2, {})} | custom-call | tf_op jit(solution)/shard_map/finish/pallas_call | solution.py:838
  37.8 0.0 collective-permute-done.14
  37.8 0.5 %collective-permute-done.13 = f32[3,3,128]{2,1,0:T(4,128)S(1)} collective-permute-done((f32[3,3,128]{2,1,0:T(4,128)S(1)}, f32[3,3,128]{2,1,0:T(4,128)S(1)}, u32[]{:S(2)}, u32[]{:S(2)}) %collective-permute-start.13) | collective-permute-done | bytes 4640 | tf_op jit(solution)/shard_map/ppermute | solution.py:836
  38.3 0.0 collective-permute-done.12
  38.3 0.6 %add_add_fusion = f32[3,3,128]{2,1,0:T(4,128)} fusion(f32[3,3,128]{2,1,0:T(4,128)S(1)} %collective-permute-done.13, f32[3,3,128]{2,1,0:T(4,128)S(1)} %collective-permute-done.14, f32[3,3,128]{2,1,0:T(4,128)S(1)} %sums.1, f32[3,3,128]{2,1,0:T(4,128)S(1)} %collective-permute-done.12), kind=kLoop, calls=%fused_computation | loop fusion | flops 3456 | bytes 23040 | tf_op jit(solution)/shard_map/add | solution.py:859
  (1 shorter events, 0.0 us)
Async XLA Ops:
  0.6 13.7 %copy-start.1 = (s32[8]{0:T(128)S(1)}, s32[8]{0:T(128)}, u32[]{:S(2)}) copy-start(s32[8]{0:T(128)} %lengths_ref.5) | copy-start | bytes 100
  0.6 13.7 %copy-start = (f32[3,3,128]{2,1,0:T(4,128)S(1)}, f32[3,3,128]{2,1,0:T(4,128)}, u32[]{:S(2)}) copy-start(f32[3,3,128]{2,1,0:T(4,128)} %filters_ref.5) | copy-start | bytes 13828
  1.6 7.6 %collective-permute-start.3 = (bf16[144,256]{1,0:T(8,128)(2,1)S(1)}, bf16[144,256]{1,0:T(8,128)(2,1)S(1)}, u32[]{:S(2)}, u32[]{:S(2)}) collective-permute-start(bf16[144,256]{1,0:T(8,128)(2,1)S(1)} %pack.1.own_ref.refs_5_), channel_id=1, source_target_pairs={{0,16},{4,20},{8,24},{12,28},{16,0},{20,4},{24,8},{28,12},{1,17},{... | collective-permute-start | bytes 221192 | tf_op jit(solution)/shard_map/ppermute | solution.py:700
  5.7 6.7 %collective-permute-start.2 = (bf16[144,256]{1,0:T(8,128)(2,1)S(1)}, bf16[144,256]{1,0:T(8,128)(2,1)S(1)}, u32[]{:S(2)}, u32[]{:S(2)}) collective-permute-start(bf16[144,256]{1,0:T(8,128)(2,1)S(1)} %pack.1.own_ref.refs_5_), channel_id=1, source_target_pairs={{0,12},{4,8},{8,4},{12,0},{16,28},{20,24},{24,20},{28,16},{1,13},{... | collective-permute-start | bytes 221192 | tf_op jit(solution)/shard_map/ppermute | solution.py:700
  8.2 5.2 %collective-permute-start.1 = (bf16[144,256]{1,0:T(8,128)(2,1)S(1)}, bf16[144,256]{1,0:T(8,128)(2,1)S(1)}, u32[]{:S(2)}, u32[]{:S(2)}) collective-permute-start(bf16[144,256]{1,0:T(8,128)(2,1)S(1)} %pack.1.own_ref.refs_5_), channel_id=1, source_target_pairs={{0,8},{4,12},{8,0},{12,4},{16,24},{20,28},{24,16},{28,20},{1,9},{5... | collective-permute-start | bytes 221192 | tf_op jit(solution)/shard_map/ppermute | solution.py:700
  8.6 5.7 %collective-permute-start = (bf16[144,256]{1,0:T(8,128)(2,1)S(1)}, bf16[144,256]{1,0:T(8,128)(2,1)S(1)}, u32[]{:S(2)}, u32[]{:S(2)}) collective-permute-start(bf16[144,256]{1,0:T(8,128)(2,1)S(1)} %pack.1.own_ref.refs_5_), channel_id=1, source_target_pairs={{0,4},{4,0},{8,12},{12,8},{16,20},{20,16},{24,28},{28,24},{1,5},{5... | collective-permute-start | bytes 221192 | tf_op jit(solution)/shard_map/ppermute | solution.py:700
  9.2 7.0 %collective-permute-start.6 = (bf16[144,256]{1,0:T(8,128)(2,1)S(1)}, bf16[144,256]{1,0:T(8,128)(2,1)S(1)}, u32[]{:S(2)}, u32[]{:S(2)}) collective-permute-start(bf16[144,256]{1,0:T(8,128)(2,1)S(1)} %collective-permute-done.3.refs_6_), channel_id=1, source_target_pairs={{0,12},{4,8},{8,4},{12,0},{16,28},{20,24},{24,20},{28,16},{1,13},{... | collective-permute-start | bytes 221192 | tf_op jit(solution)/shard_map/ppermute | solution.py:700
  11.7 4.5 %collective-permute-start.5 = (bf16[144,256]{1,0:T(8,128)(2,1)S(1)}, bf16[144,256]{1,0:T(8,128)(2,1)S(1)}, u32[]{:S(2)}, u32[]{:S(2)}) collective-permute-start(bf16[144,256]{1,0:T(8,128)(2,1)S(1)} %collective-permute-done.3.refs_6_), channel_id=1, source_target_pairs={{0,8},{4,12},{8,0},{12,4},{16,24},{20,28},{24,16},{28,20},{1,9},{5... | collective-permute-start | bytes 221192 | tf_op jit(solution)/shard_map/ppermute | solution.py:700
  12.4 4.4 %collective-permute-start.4 = (bf16[144,256]{1,0:T(8,128)(2,1)S(1)}, bf16[144,256]{1,0:T(8,128)(2,1)S(1)}, u32[]{:S(2)}, u32[]{:S(2)}) collective-permute-start(bf16[144,256]{1,0:T(8,128)(2,1)S(1)} %collective-permute-done.3.refs_6_), channel_id=1, source_target_pairs={{0,4},{4,0},{8,12},{12,8},{16,20},{20,16},{24,28},{28,24},{1,5},{5... | collective-permute-start | bytes 221192 | tf_op jit(solution)/shard_map/ppermute | solution.py:700
  19.3 8.9 %collective-permute-start.7 = (bf16[224,256]{1,0:T(8,128)(2,1)S(1)}, bf16[224,256]{1,0:T(8,128)(2,1)S(1)}, u32[]{:S(2)}, u32[]{:S(2)}) collective-permute-start(bf16[224,256]{1,0:T(8,128)(2,1)S(1)} %get-tuple-element.34), channel_id=1, source_target_pairs={{0,4},{4,0},{8,12},{12,8},{16,20},{20,16},{24,28},{28,24},{1,5},{5... | collective-permute-start | bytes 344072 | tf_op jit(solution)/shard_map/ppermute | solution.py:700
  21.8 6.5 %collective-permute-start.8 = (bf16[208,256]{1,0:T(8,128)(2,1)S(1)}, bf16[208,256]{1,0:T(8,128)(2,1)S(1)}, u32[]{:S(2)}, u32[]{:S(2)}) collective-permute-start(bf16[208,256]{1,0:T(8,128)(2,1)S(1)} %get-tuple-element.35), channel_id=1, source_target_pairs={{0,8},{4,12},{8,0},{12,4},{16,24},{20,28},{24,16},{28,20},{1,9},{5... | collective-permute-start | bytes 319496 | tf_op jit(solution)/shard_map/ppermute | solution.py:700
  22.9 5.3 %collective-permute-start.9 = (bf16[160,256]{1,0:T(8,128)(2,1)S(1)}, bf16[160,256]{1,0:T(8,128)(2,1)S(1)}, u32[]{:S(2)}, u32[]{:S(2)}) collective-permute-start(bf16[160,256]{1,0:T(8,128)(2,1)S(1)} %get-tuple-element.36), channel_id=1, source_target_pairs={{0,12},{4,8},{8,4},{12,0},{16,28},{20,24},{24,20},{28,16},{1,13},{... | collective-permute-start | bytes 245768 | tf_op jit(solution)/shard_map/ppermute | solution.py:700
  28.4 6.3 %collective-permute-start.10 = (bf16[160,256]{1,0:T(8,128)(2,1)S(1)}, bf16[160,256]{1,0:T(8,128)(2,1)S(1)}, u32[]{:S(2)}, u32[]{:S(2)}) collective-permute-start(bf16[160,256]{1,0:T(8,128)(2,1)S(1)} %get-tuple-element.45), channel_id=1, source_target_pairs={{0,16},{4,20},{8,24},{12,28},{16,0},{20,4},{24,8},{28,12},{1,17},{... | collective-permute-start | bytes 245768 | tf_op jit(solution)/shard_map/ppermute | solution.py:700
  30.3 6.2 %collective-permute-start.11 = (bf16[80,256]{1,0:T(8,128)(2,1)S(1)}, bf16[80,256]{1,0:T(8,128)(2,1)S(1)}, u32[]{:S(2)}, u32[]{:S(2)}) collective-permute-start(bf16[80,256]{1,0:T(8,128)(2,1)S(1)} %get-tuple-element.47), channel_id=1, source_target_pairs={{0,12},{4,8},{8,4},{12,0},{16,28},{20,24},{24,20},{28,16},{1,13},{... | collective-permute-start | bytes 122888 | tf_op jit(solution)/shard_map/ppermute | solution.py:700
  34.6 3.1 %collective-permute-start.14 = (f32[3,3,128]{2,1,0:T(4,128)S(1)}, f32[3,3,128]{2,1,0:T(4,128)S(1)}, u32[]{:S(2)}, u32[]{:S(2)}) collective-permute-start(f32[3,3,128]{2,1,0:T(4,128)S(1)} %sums.1), channel_id=1, source_target_pairs={{0,3},{1,2},{2,1},{3,0},{4,7},{5,6},{6,5},{7,4},{8,11},{9,10},{10,... | collective-permute-start | bytes 13832 | tf_op jit(solution)/shard_map/ppermute | solution.py:836
  34.7 3.7 %collective-permute-start.13 = (f32[3,3,128]{2,1,0:T(4,128)S(1)}, f32[3,3,128]{2,1,0:T(4,128)S(1)}, u32[]{:S(2)}, u32[]{:S(2)}) collective-permute-start(f32[3,3,128]{2,1,0:T(4,128)S(1)} %sums.1), channel_id=1, source_target_pairs={{0,2},{1,3},{2,0},{3,1},{4,6},{5,7},{6,4},{7,5},{8,10},{9,11},{10,... | collective-permute-start | bytes 13832 | tf_op jit(solution)/shard_map/ppermute | solution.py:836
  36.2 2.1 %collective-permute-start.12 = (f32[3,3,128]{2,1,0:T(4,128)S(1)}, f32[3,3,128]{2,1,0:T(4,128)S(1)}, u32[]{:S(2)}, u32[]{:S(2)}) collective-permute-start(f32[3,3,128]{2,1,0:T(4,128)S(1)} %sums.1), channel_id=1, source_target_pairs={{0,1},{1,0},{2,3},{3,2},{4,5},{5,4},{6,7},{7,6},{8,9},{9,8},{10,11... | collective-permute-start | bytes 13832 | tf_op jit(solution)/shard_map/ppermute | solution.py:836

commit v6 on v5

--- a/solution.py
+++ b/solution.py
@@ -16,7 +16,7 @@
 MAX_CHUNK = 640
 RIM = 8
 MAX_DIRECT = 4
-WINDOWS = ((2, 2), (4, 4), (2, 9), (6, 6), (4, 9), (9, 4), (6, 9), (9, 9))
+WINDOWS = ((2, 2), (4, 4), (2, 9), (6, 6), (8, 4), (4, 9), (6, 9), (8, 9))
 MIB = 1 << 20
 
 
@@ -313,7 +313,7 @@
                 conv_scr[0, keys_rows[half]], queries, NT, preferred_element_type=f32
             )
             bias = bias_scr[half, :window]
-            scores = scores + jnp.concatenate([bias, bias], axis=1)
+            scores = scores * log2_scale + jnp.concatenate([bias, bias], axis=1)
             s_scr[slot, :window] = scores
             tops.append(jnp.max(scores, axis=0, keepdims=True))
         for slot, (half, at) in enumerate(units):
@@ -322,20 +322,19 @@
             prob_grads = lax.dot_general(
                 conv_scr[1, keys_rows[half]], grads, NT, preferred_element_type=f32
             )
-            weights = jnp.exp2((s_scr[slot, :window] - tops[slot]) * log2_scale)
-            s_scr[slot, :window] = weights
             dp_scr[slot, :window] = prob_grads
+            weights = jnp.exp2(s_scr[slot, :window] - tops[slot])
             total = jnp.sum(weights, axis=0, keepdims=True)
             weighted = jnp.sum(weights * prob_grads, axis=0, keepdims=True)
-            inverse = 1.0 / total
-            scaled.append((inverse, weighted * inverse, inverse * scale))
+            scaled.append((tops[slot] + jnp.log2(total), weighted / total))
         for slot, (half, at) in enumerate(units):
             window = windows[half]
-            inverse, mean, slope = scaled[slot]
-            weights = s_scr[slot, :window]
+            log_total, mean = scaled[slot]
+            probs = jnp.exp2(s_scr[slot, :window] - log_total)
             cols = slice(at * wide, (at + 1) * wide)
-            p_scr[half, :window, cols] = (weights * inverse).astype(bf16)
-            ds_scr[half, :window, cols] = (weights * slope * (dp_scr[slot, :window] - mean)).astype(bf16)
+            p_scr[half, :window, cols] = probs.astype(bf16)
+            score_grads = probs * (dp_scr[slot, :window] - mean) * scale
+            ds_scr[half, :window, cols] = score_grads.astype(bf16)
         for half, window in enumerate(windows):
             score_grads = ds_scr[half, :window]
             keys_t = conv_scr[0, keys_rows[half]].T
@@ -427,7 +426,7 @@
     if direct:
         done = jnp.bool_(False)
         for sizes in WINDOWS:
-            sizes = [min(size, ctx_count + 1) for size in sizes]
+            sizes = [min(size, ctx_count + half) for half, size in enumerate(sizes)]
             fits = (needed[0] <= sizes[0]) & (needed[1] <= sizes[1])
 
             @pl.when(fits & jnp.logical_not(done))

time: 39.2 us -> 38.5 us (0.982); the launches traced: 38.9 us -> 38.7 us
  waiting for transfers between devices: 8.53 us -> 7.77 us
  Pallas kernels: 7.55 us -> 8.16 us
    ppermute x12, waiting for transfers between devices: 7.99 us -> 7.23 us  [flipped(): return lax.ppermute(array, 'ctx', [(i, i ^ flip) for i in range(ctx_count)])]
    pallas_call x1, Pallas kernels: 2.56 us -> 3.17 us  [shards(): pl.pallas_call(functools.partial(grads_kernel, ctx_count, direct), out_sh...]
where the time goes in v6:
time: 38.5 us; the launch traced here: 38.7 us
  starting transfers between devices  21.5 us (56%)
  Pallas kernels  8.16 us (21%)
  waiting for transfers between devices  7.77 us (20%)
  between operations  0.73 us (2%)
  other arithmetic  0.6 us (2%)
    ppermute x12, starting transfers between devices, flipped(): return lax.ppermute(array, 'ctx', [(i, i ^ flip) for i in range(ctx_count)])  19.6 us
    ppermute x12, waiting for transfers between devices, flipped(): return lax.ppermute(array, 'ctx', [(i, i ^ flip) for i in range(ctx_count)])  7.23 us
    pallas_call x1, Pallas kernels, shards(): pl.pallas_call(functools.partial(grads_kernel, ctx_count, direct), out_sh...  3.17 us
    pallas_call x1, Pallas kernels, shards(): pl.pallas_call(functools.partial(prep_kernel, ctx_count, direct), out_sha...  1.87 us
    ppermute x3, starting transfers between devices, shards(): lax.ppermute(sums, 'tp', [(i, i ^ flip) for i in range(count)])  1.86 us
    pallas_call x1, Pallas kernels, shards(): pl.pallas_call(functools.partial(finish_kernel, ctx_count, direct), out_s...  1.27 us
    pallas_call x1, Pallas kernels, shards(): pl.pallas_call(pack_kernel, out_shape=jax.ShapeDtypeStruct((msg_rows, 2 *...  0.93 us
    pallas_call x1, Pallas kernels, shards(): pl.pallas_call(save_kernel, out_shape=jax.ShapeDtypeStruct(q_pre.shape, f...  0.8 us
  transfers between devices with their start and end apart: 15, of which 6 were waited for; matrix products, arithmetic and copies ran while one was open for 0% of the time, Pallas kernels for 10%

profile of v6, /device:TPU:0, one launch (start us, length us, event | category | flops | bytes accessed | tf_op | source)
XLA Modules:
  0.0 38.7 jit_solution(2857003587422074387)
XLA Ops:
  0.6 0.0 copy-start.1
  0.6 0.0 copy-start
  0.7 0.9 %pack.1.own_ref.refs_5_ = bf16[144,256]{1,0:T(8,128)(2,1)S(1)} custom-call(bf16[2,64,128]{2,1,0:T(8,128)(2,1)} %k_hbm.1, bf16[2,64,128]{2,1,0:T(8,128)(2,1)} %v_hbm.1, bf16[2,64,1024]{2,1,0:T(8,128)(2,1)} %q_hbm.3), custom_call_target="tpu_custom_call" | custom-call | tf_op jit(solution)/shard_map/pack/pallas_call | solution.py:711
  1.6 4.1 %collective-permute-start.3 = (bf16[144,256]{1,0:T(8,128)(2,1)S(1)}, bf16[144,256]{1,0:T(8,128)(2,1)S(1)}, u32[]{:S(2)}, u32[]{:S(2)}) collective-permute-start(bf16[144,256]{1,0:T(8,128)(2,1)S(1)} %pack.1.own_ref.refs_5_), channel_id=1, source_target_pairs={{0,16},{4,20},{8,24},{12,28},{16,0},{20,4},{24,8},{28,12},{1,17},{... | collective-permute-start | bytes 221192 | tf_op jit(solution)/shard_map/ppermute | solution.py:699
  5.7 2.5 %collective-permute-start.2 = (bf16[144,256]{1,0:T(8,128)(2,1)S(1)}, bf16[144,256]{1,0:T(8,128)(2,1)S(1)}, u32[]{:S(2)}, u32[]{:S(2)}) collective-permute-start(bf16[144,256]{1,0:T(8,128)(2,1)S(1)} %pack.1.own_ref.refs_5_), channel_id=1, source_target_pairs={{0,12},{4,8},{8,4},{12,0},{16,28},{20,24},{24,20},{28,16},{1,13},{... | collective-permute-start | bytes 221192 | tf_op jit(solution)/shard_map/ppermute | solution.py:699
  8.2 0.4 %collective-permute-start.1 = (bf16[144,256]{1,0:T(8,128)(2,1)S(1)}, bf16[144,256]{1,0:T(8,128)(2,1)S(1)}, u32[]{:S(2)}, u32[]{:S(2)}) collective-permute-start(bf16[144,256]{1,0:T(8,128)(2,1)S(1)} %pack.1.own_ref.refs_5_), channel_id=1, source_target_pairs={{0,8},{4,12},{8,0},{12,4},{16,24},{20,28},{24,16},{28,20},{1,9},{5... | collective-permute-start | bytes 221192 | tf_op jit(solution)/shard_map/ppermute | solution.py:699
  8.6 0.5 %collective-permute-start = (bf16[144,256]{1,0:T(8,128)(2,1)S(1)}, bf16[144,256]{1,0:T(8,128)(2,1)S(1)}, u32[]{:S(2)}, u32[]{:S(2)}) collective-permute-start(bf16[144,256]{1,0:T(8,128)(2,1)S(1)} %pack.1.own_ref.refs_5_), channel_id=1, source_target_pairs={{0,4},{4,0},{8,12},{12,8},{16,20},{20,16},{24,28},{28,24},{1,5},{5... | collective-permute-start | bytes 221192 | tf_op jit(solution)/shard_map/ppermute | solution.py:699
  9.2 0.0 collective-permute-done.3.refs_6_
  9.2 2.5 %collective-permute-start.6 = (bf16[144,256]{1,0:T(8,128)(2,1)S(1)}, bf16[144,256]{1,0:T(8,128)(2,1)S(1)}, u32[]{:S(2)}, u32[]{:S(2)}) collective-permute-start(bf16[144,256]{1,0:T(8,128)(2,1)S(1)} %collective-permute-done.3.refs_6_), channel_id=1, source_target_pairs={{0,12},{4,8},{8,4},{12,0},{16,28},{20,24},{24,20},{28,16},{1,13},{... | collective-permute-start | bytes 221192 | tf_op jit(solution)/shard_map/ppermute | solution.py:699
  11.7 0.7 %collective-permute-start.5 = (bf16[144,256]{1,0:T(8,128)(2,1)S(1)}, bf16[144,256]{1,0:T(8,128)(2,1)S(1)}, u32[]{:S(2)}, u32[]{:S(2)}) collective-permute-start(bf16[144,256]{1,0:T(8,128)(2,1)S(1)} %collective-permute-done.3.refs_6_), channel_id=1, source_target_pairs={{0,8},{4,12},{8,0},{12,4},{16,24},{20,28},{24,16},{28,20},{1,9},{5... | collective-permute-start | bytes 221192 | tf_op jit(solution)/shard_map/ppermute | solution.py:699
  12.4 0.0 collective-permute-done.2.refs_2_.refs_9_
  12.4 0.9 %collective-permute-start.4 = (bf16[144,256]{1,0:T(8,128)(2,1)S(1)}, bf16[144,256]{1,0:T(8,128)(2,1)S(1)}, u32[]{:S(2)}, u32[]{:S(2)}) collective-permute-start(bf16[144,256]{1,0:T(8,128)(2,1)S(1)} %collective-permute-done.3.refs_6_), channel_id=1, source_target_pairs={{0,4},{4,0},{8,12},{12,8},{16,20},{20,16},{24,28},{28,24},{1,5},{5... | collective-permute-start | bytes 221192 | tf_op jit(solution)/shard_map/ppermute | solution.py:699
  13.3 0.1 collective-permute-done.1.refs_1_.refs_8_
  13.4 0.9 %collective-permute-done.refs_0_.refs_7_ = bf16[144,256]{1,0:T(8,128)(2,1)S(1)} collective-permute-done((bf16[144,256]{1,0:T(8,128)(2,1)S(1)}, bf16[144,256]{1,0:T(8,128)(2,1)S(1)}, u32[]{:S(2)}, u32[]{:S(2)}) %collective-permute-start) | collective-permute-done | bytes 73760 | tf_op jit(solution)/shard_map/ppermute | solution.py:699
  14.3 0.0 copy-done.1
  14.3 0.0 copy-done
  14.3 1.9 %prep.1 = (f32[1040,128]{1,0:T(8,128)S(1)}, f32[1040,128]{1,0:T(8,128)S(1)}, f32[2,8,72,128]{3,2,1,0:T(8,128)S(1)}, bf16[2,512,128]{2,1,0:T(8,128)(2,1)S(1)}, bf16[2,512,128]{2,1,0:T(8,128)(2,1)S(1)}) custom-call(s32[8]{0:T(128)S(1)} %copy-done.1, f32[3,3,128]{2,1,0:T(4,128)S(1)} %copy-done, bf16[2,64,1024]{2,1,0:T(8,128)(2,1)} %q_hbm.3, ...), custom_call_target="tpu_custom_call" | custom-call | tf_op jit(solution)/shard_map/prep/pallas_call | solution.py:746
  16.2 0.0 collective-permute-done.6.refs_12_
  16.2 0.0 collective-permute-done.5.refs_11_
  16.2 0.5 %collective-permute-done.4.refs_10_ = bf16[144,256]{1,0:T(8,128)(2,1)S(1)} collective-permute-done((bf16[144,256]{1,0:T(8,128)(2,1)S(1)}, bf16[144,256]{1,0:T(8,128)(2,1)S(1)}, u32[]{:S(2)}, u32[]{:S(2)}) %collective-permute-start.4) | collective-permute-done | bytes 73760 | tf_op jit(solution)/shard_map/ppermute | solution.py:699
  16.8 3.2 %grads.1 = (f32[2,64,1024]{2,1,0:T(8,128)S(1)}, f32[2,8,1024]{2,1,0:T(8,128)S(1)}, f32[128,256]{1,0:T(8,128)S(1)}, f32[136,256]{1,0:T(8,128)S(1)}, bf16[224,256]...) custom-call(s32[8]{0:T(128)S(1)} %copy-done.1, ...), custom_call_target="tpu_custom_call" | custom-call | tf_op jit(solution)/shard_map/grads/pallas_call | solution.py:781
  19.9 0.4 %collective-permute-start.7 = (bf16[224,256]{1,0:T(8,128)(2,1)S(1)}, bf16[224,256]{1,0:T(8,128)(2,1)S(1)}, u32[]{:S(2)}, u32[]{:S(2)}) collective-permute-start(bf16[224,256]{1,0:T(8,128)(2,1)S(1)} %get-tuple-element.34), channel_id=1, source_target_pairs={{0,4},{4,0},{8,12},{12,8},{16,20},{20,16},{24,28},{28,24},{1,5},{5... | collective-permute-start | bytes 344072 | tf_op jit(solution)/shard_map/ppermute | solution.py:699
  20.4 2.3 %collective-permute-start.8 = (bf16[208,256]{1,0:T(8,128)(2,1)S(1)}, bf16[208,256]{1,0:T(8,128)(2,1)S(1)}, u32[]{:S(2)}, u32[]{:S(2)}) collective-permute-start(bf16[208,256]{1,0:T(8,128)(2,1)S(1)} %get-tuple-element.35), channel_id=1, source_target_pairs={{0,8},{4,12},{8,0},{12,4},{16,24},{20,28},{24,16},{28,20},{1,9},{5... | collective-permute-start | bytes 319496 | tf_op jit(solution)/shard_map/ppermute | solution.py:699
  22.7 1.0 %collective-permute-start.9 = (bf16[160,256]{1,0:T(8,128)(2,1)S(1)}, bf16[160,256]{1,0:T(8,128)(2,1)S(1)}, u32[]{:S(2)}, u32[]{:S(2)}) collective-permute-start(bf16[160,256]{1,0:T(8,128)(2,1)S(1)} %get-tuple-element.36), channel_id=1, source_target_pairs={{0,12},{4,8},{8,4},{12,0},{16,28},{20,24},{24,20},{28,16},{1,13},{... | collective-permute-start | bytes 245768 | tf_op jit(solution)/shard_map/ppermute | solution.py:699
  23.7 0.8 %save.1.dq_in_hbm = f32[2,64,1024]{2,1,0:T(8,128)} custom-call(f32[2,64,1024]{2,1,0:T(8,128)S(1)} %get-tuple-element.33.source_ref), custom_call_target="tpu_custom_call" | custom-call | tf_op jit(solution)/shard_map/save/pallas_call | solution.py:792
  24.5 3.6 %collective-permute-done.9.refs_2_ = bf16[160,256]{1,0:T(8,128)(2,1)S(1)} collective-permute-done((bf16[160,256]{1,0:T(8,128)(2,1)S(1)}, bf16[160,256]{1,0:T(8,128)(2,1)S(1)}, u32[]{:S(2)}, u32[]{:S(2)}) %collective-permute-start.9) | collective-permute-done | bytes 81952 | tf_op jit(solution)/shard_map/ppermute | solution.py:699
  28.0 0.0 collective-permute-done.8.refs_1_
  28.0 0.0 collective-permute-done.7.refs_0_
  28.0 0.1 merge.1
  28.2 2.4 %collective-permute-start.10 = (bf16[160,256]{1,0:T(8,128)(2,1)S(1)}, bf16[160,256]{1,0:T(8,128)(2,1)S(1)}, u32[]{:S(2)}, u32[]{:S(2)}) collective-permute-start(bf16[160,256]{1,0:T(8,128)(2,1)S(1)} %get-tuple-element.45), channel_id=1, source_target_pairs={{0,16},{4,20},{8,24},{12,28},{16,0},{20,4},{24,8},{28,12},{1,17},{... | collective-permute-start | bytes 245768 | tf_op jit(solution)/shard_map/ppermute | solution.py:699
  30.5 1.8 %collective-permute-start.11 = (bf16[80,256]{1,0:T(8,128)(2,1)S(1)}, bf16[80,256]{1,0:T(8,128)(2,1)S(1)}, u32[]{:S(2)}, u32[]{:S(2)}) collective-permute-start(bf16[80,256]{1,0:T(8,128)(2,1)S(1)} %get-tuple-element.47), channel_id=1, source_target_pairs={{0,12},{4,8},{8,4},{12,0},{16,28},{20,24},{24,20},{28,16},{1,13},{... | collective-permute-start | bytes 122888 | tf_op jit(solution)/shard_map/ppermute | solution.py:699
  32.3 2.1 %collective-permute-done.10.far_ref = bf16[160,256]{1,0:T(8,128)(2,1)S(1)} collective-permute-done((bf16[160,256]{1,0:T(8,128)(2,1)S(1)}, bf16[160,256]{1,0:T(8,128)(2,1)S(1)}, u32[]{:S(2)}, u32[]{:S(2)}) %collective-permute-start.10) | collective-permute-done | bytes 81952 | tf_op jit(solution)/shard_map/ppermute | solution.py:699
  34.5 0.0 collective-permute-start.14
  34.5 1.6 %collective-permute-start.13 = (f32[3,3,128]{2,1,0:T(4,128)S(1)}, f32[3,3,128]{2,1,0:T(4,128)S(1)}, u32[]{:S(2)}, u32[]{:S(2)}) collective-permute-start(f32[3,3,128]{2,1,0:T(4,128)S(1)} %sums.1), channel_id=1, source_target_pairs={{0,2},{1,3},{2,0},{3,1},{4,6},{5,7},{6,4},{7,5},{8,10},{9,11},{10,... | collective-permute-start | bytes 13832 | tf_op jit(solution)/shard_map/ppermute | solution.py:835
  36.0 0.3 collective-permute-start.12
  36.3 0.0 collective-permute-done.11.refs_0_
  36.3 1.3 %finish.1 = (f32[2,64,1024]{2,1,0:T(8,128)}, f32[2,64,128]{2,1,0:T(8,128)}, f32[2,64,128]{2,1,0:T(8,128)}) custom-call(s32[8]{0:T(128)S(1)} %copy-done.1, f32[3,3,128]{2,1,0:T(4,128)S(1)} %copy-done, f32[2,64,1024]{2,1,0:T(8,128)} %save.1.dq_in_hbm, f32[2,8,1024]{2,1,0:T(8,128)S(1)} %get-tuple-element.38.tail_ref, ...), custom_call_target="tpu_custom_call", output_to_operand_aliasing={{0}: (2, {})} | custom-call | tf_op jit(solution)/shard_map/finish/pallas_call | solution.py:837
  37.6 0.0 collective-permute-done.14
  37.6 0.5 %collective-permute-done.13 = f32[3,3,128]{2,1,0:T(4,128)S(1)} collective-permute-done((f32[3,3,128]{2,1,0:T(4,128)S(1)}, f32[3,3,128]{2,1,0:T(4,128)S(1)}, u32[]{:S(2)}, u32[]{:S(2)}) %collective-permute-start.13) | collective-permute-done | bytes 4640 | tf_op jit(solution)/shard_map/ppermute | solution.py:835
  38.1 0.0 collective-permute-done.12
  38.1 0.6 %add_add_fusion = f32[3,3,128]{2,1,0:T(4,128)} fusion(f32[3,3,128]{2,1,0:T(4,128)S(1)} %collective-permute-done.13, f32[3,3,128]{2,1,0:T(4,128)S(1)} %collective-permute-done.14, f32[3,3,128]{2,1,0:T(4,128)S(1)} %sums.1, f32[3,3,128]{2,1,0:T(4,128)S(1)} %collective-permute-done.12), kind=kLoop, calls=%fused_computation | loop fusion | flops 3456 | bytes 23040 | tf_op jit(solution)/shard_map/add | solution.py:858
  (1 shorter events, 0.0 us)
Async XLA Ops:
  0.6 13.7 %copy-start.1 = (s32[8]{0:T(128)S(1)}, s32[8]{0:T(128)}, u32[]{:S(2)}) copy-start(s32[8]{0:T(128)} %lengths_ref.5) | copy-start | bytes 100
  0.6 13.7 %copy-start = (f32[3,3,128]{2,1,0:T(4,128)S(1)}, f32[3,3,128]{2,1,0:T(4,128)}, u32[]{:S(2)}) copy-start(f32[3,3,128]{2,1,0:T(4,128)} %filters_ref.5) | copy-start | bytes 13828
  1.6 7.6 %collective-permute-start.3 = (bf16[144,256]{1,0:T(8,128)(2,1)S(1)}, bf16[144,256]{1,0:T(8,128)(2,1)S(1)}, u32[]{:S(2)}, u32[]{:S(2)}) collective-permute-start(bf16[144,256]{1,0:T(8,128)(2,1)S(1)} %pack.1.own_ref.refs_5_), channel_id=1, source_target_pairs={{0,16},{4,20},{8,24},{12,28},{16,0},{20,4},{24,8},{28,12},{1,17},{... | collective-permute-start | bytes 221192 | tf_op jit(solution)/shard_map/ppermute | solution.py:699
  5.7 6.7 %collective-permute-start.2 = (bf16[144,256]{1,0:T(8,128)(2,1)S(1)}, bf16[144,256]{1,0:T(8,128)(2,1)S(1)}, u32[]{:S(2)}, u32[]{:S(2)}) collective-permute-start(bf16[144,256]{1,0:T(8,128)(2,1)S(1)} %pack.1.own_ref.refs_5_), channel_id=1, source_target_pairs={{0,12},{4,8},{8,4},{12,0},{16,28},{20,24},{24,20},{28,16},{1,13},{... | collective-permute-start | bytes 221192 | tf_op jit(solution)/shard_map/ppermute | solution.py:699
  8.2 5.2 %collective-permute-start.1 = (bf16[144,256]{1,0:T(8,128)(2,1)S(1)}, bf16[144,256]{1,0:T(8,128)(2,1)S(1)}, u32[]{:S(2)}, u32[]{:S(2)}) collective-permute-start(bf16[144,256]{1,0:T(8,128)(2,1)S(1)} %pack.1.own_ref.refs_5_), channel_id=1, source_target_pairs={{0,8},{4,12},{8,0},{12,4},{16,24},{20,28},{24,16},{28,20},{1,9},{5... | collective-permute-start | bytes 221192 | tf_op jit(solution)/shard_map/ppermute | solution.py:699
  8.6 5.7 %collective-permute-start = (bf16[144,256]{1,0:T(8,128)(2,1)S(1)}, bf16[144,256]{1,0:T(8,128)(2,1)S(1)}, u32[]{:S(2)}, u32[]{:S(2)}) collective-permute-start(bf16[144,256]{1,0:T(8,128)(2,1)S(1)} %pack.1.own_ref.refs_5_), channel_id=1, source_target_pairs={{0,4},{4,0},{8,12},{12,8},{16,20},{20,16},{24,28},{28,24},{1,5},{5... | collective-permute-start | bytes 221192 | tf_op jit(solution)/shard_map/ppermute | solution.py:699
  9.2 7.0 %collective-permute-start.6 = (bf16[144,256]{1,0:T(8,128)(2,1)S(1)}, bf16[144,256]{1,0:T(8,128)(2,1)S(1)}, u32[]{:S(2)}, u32[]{:S(2)}) collective-permute-start(bf16[144,256]{1,0:T(8,128)(2,1)S(1)} %collective-permute-done.3.refs_6_), channel_id=1, source_target_pairs={{0,12},{4,8},{8,4},{12,0},{16,28},{20,24},{24,20},{28,16},{1,13},{... | collective-permute-start | bytes 221192 | tf_op jit(solution)/shard_map/ppermute | solution.py:699
  11.7 4.5 %collective-permute-start.5 = (bf16[144,256]{1,0:T(8,128)(2,1)S(1)}, bf16[144,256]{1,0:T(8,128)(2,1)S(1)}, u32[]{:S(2)}, u32[]{:S(2)}) collective-permute-start(bf16[144,256]{1,0:T(8,128)(2,1)S(1)} %collective-permute-done.3.refs_6_), channel_id=1, source_target_pairs={{0,8},{4,12},{8,0},{12,4},{16,24},{20,28},{24,16},{28,20},{1,9},{5... | collective-permute-start | bytes 221192 | tf_op jit(solution)/shard_map/ppermute | solution.py:699
  12.4 4.4 %collective-permute-start.4 = (bf16[144,256]{1,0:T(8,128)(2,1)S(1)}, bf16[144,256]{1,0:T(8,128)(2,1)S(1)}, u32[]{:S(2)}, u32[]{:S(2)}) collective-permute-start(bf16[144,256]{1,0:T(8,128)(2,1)S(1)} %collective-permute-done.3.refs_6_), channel_id=1, source_target_pairs={{0,4},{4,0},{8,12},{12,8},{16,20},{20,16},{24,28},{28,24},{1,5},{5... | collective-permute-start | bytes 221192 | tf_op jit(solution)/shard_map/ppermute | solution.py:699
  19.9 8.1 %collective-permute-start.7 = (bf16[224,256]{1,0:T(8,128)(2,1)S(1)}, bf16[224,256]{1,0:T(8,128)(2,1)S(1)}, u32[]{:S(2)}, u32[]{:S(2)}) collective-permute-start(bf16[224,256]{1,0:T(8,128)(2,1)S(1)} %get-tuple-element.34), channel_id=1, source_target_pairs={{0,4},{4,0},{8,12},{12,8},{16,20},{20,16},{24,28},{28,24},{1,5},{5... | collective-permute-start | bytes 344072 | tf_op jit(solution)/shard_map/ppermute | solution.py:699
  20.4 7.7 %collective-permute-start.8 = (bf16[208,256]{1,0:T(8,128)(2,1)S(1)}, bf16[208,256]{1,0:T(8,128)(2,1)S(1)}, u32[]{:S(2)}, u32[]{:S(2)}) collective-permute-start(bf16[208,256]{1,0:T(8,128)(2,1)S(1)} %get-tuple-element.35), channel_id=1, source_target_pairs={{0,8},{4,12},{8,0},{12,4},{16,24},{20,28},{24,16},{28,20},{1,9},{5... | collective-permute-start | bytes 319496 | tf_op jit(solution)/shard_map/ppermute | solution.py:699
  22.7 5.3 %collective-permute-start.9 = (bf16[160,256]{1,0:T(8,128)(2,1)S(1)}, bf16[160,256]{1,0:T(8,128)(2,1)S(1)}, u32[]{:S(2)}, u32[]{:S(2)}) collective-permute-start(bf16[160,256]{1,0:T(8,128)(2,1)S(1)} %get-tuple-element.36), channel_id=1, source_target_pairs={{0,12},{4,8},{8,4},{12,0},{16,28},{20,24},{24,20},{28,16},{1,13},{... | collective-permute-start | bytes 245768 | tf_op jit(solution)/shard_map/ppermute | solution.py:699
  28.2 6.3 %collective-permute-start.10 = (bf16[160,256]{1,0:T(8,128)(2,1)S(1)}, bf16[160,256]{1,0:T(8,128)(2,1)S(1)}, u32[]{:S(2)}, u32[]{:S(2)}) collective-permute-start(bf16[160,256]{1,0:T(8,128)(2,1)S(1)} %get-tuple-element.45), channel_id=1, source_target_pairs={{0,16},{4,20},{8,24},{12,28},{16,0},{20,4},{24,8},{28,12},{1,17},{... | collective-permute-start | bytes 245768 | tf_op jit(solution)/shard_map/ppermute | solution.py:699
  30.5 5.8 %collective-permute-start.11 = (bf16[80,256]{1,0:T(8,128)(2,1)S(1)}, bf16[80,256]{1,0:T(8,128)(2,1)S(1)}, u32[]{:S(2)}, u32[]{:S(2)}) collective-permute-start(bf16[80,256]{1,0:T(8,128)(2,1)S(1)} %get-tuple-element.47), channel_id=1, source_target_pairs={{0,12},{4,8},{8,4},{12,0},{16,28},{20,24},{24,20},{28,16},{1,13},{... | collective-permute-start | bytes 122888 | tf_op jit(solution)/shard_map/ppermute | solution.py:699
  34.5 3.1 %collective-permute-start.14 = (f32[3,3,128]{2,1,0:T(4,128)S(1)}, f32[3,3,128]{2,1,0:T(4,128)S(1)}, u32[]{:S(2)}, u32[]{:S(2)}) collective-permute-start(f32[3,3,128]{2,1,0:T(4,128)S(1)} %sums.1), channel_id=1, source_target_pairs={{0,3},{1,2},{2,1},{3,0},{4,7},{5,6},{6,5},{7,4},{8,11},{9,10},{10,... | collective-permute-start | bytes 13832 | tf_op jit(solution)/shard_map/ppermute | solution.py:835
  34.5 3.7 %collective-permute-start.13 = (f32[3,3,128]{2,1,0:T(4,128)S(1)}, f32[3,3,128]{2,1,0:T(4,128)S(1)}, u32[]{:S(2)}, u32[]{:S(2)}) collective-permute-start(f32[3,3,128]{2,1,0:T(4,128)S(1)} %sums.1), channel_id=1, source_target_pairs={{0,2},{1,3},{2,0},{3,1},{4,6},{5,7},{6,4},{7,5},{8,10},{9,11},{10,... | collective-permute-start | bytes 13832 | tf_op jit(solution)/shard_map/ppermute | solution.py:835
  36.0 2.1 %collective-permute-start.12 = (f32[3,3,128]{2,1,0:T(4,128)S(1)}, f32[3,3,128]{2,1,0:T(4,128)S(1)}, u32[]{:S(2)}, u32[]{:S(2)}) collective-permute-start(f32[3,3,128]{2,1,0:T(4,128)S(1)} %sums.1), channel_id=1, source_target_pairs={{0,1},{1,0},{2,3},{3,2},{4,5},{5,4},{6,7},{7,6},{8,9},{9,8},{10,11... | collective-permute-start | bytes 13832 | tf_op jit(solution)/shard_map/ppermute | solution.py:835

commit v7 on v6

--- a/solution.py
+++ b/solution.py
@@ -68,7 +68,7 @@
 
 
 def splits(direct, flip, group):
-    return not direct or flip == group - 1
+    return not direct or flip == 1
 
 
 def partner(me, flip):
@@ -192,7 +192,7 @@
     near_in = Slots((None,) + near_in if direct else near_in, me)
     far_in = Slots((None,) + far_in if direct else far_in, me)
     first_out = Slots((None,) + first_out if direct else first_out, me)
-    late_out = Slots((None,) * (group - 1) + late_out if direct else late_out, me)
+    late_out = Slots((None,) + late_out if direct else late_out, me)
     scale = LANES**-0.5
     log2_scale = scale * 1.4426950408889634
     starts = doc_starts(lengths_ref)
@@ -530,13 +530,13 @@
         owner = partner(me, flip)
         after = (2 if splits(direct, flip, group) else 3) * span
         first_out[flip][after : after + 16] = sums_pair
-        if not direct or flip == group - 1:
+        if not direct:
             first_out[flip][after + 16 :] = rim_for(partner(owner, group))
-        if not direct or flip & (flip + 1) == 0:
-            if splits(direct, flip, group):
-                late_out[flip][span:] = rim_for(owner)
-            else:
-                first_out[flip][after + 16 :] = rim_for(owner)
+        elif flip == group - 1:
+            target = jnp.where(jnp.abs(owner - me) == 1, owner, partner(owner, group))
+            first_out[flip][after + 16 :] = rim_for(target)
+        if splits(direct, flip, group):
+            late_out[flip][span:] = rim_for(owner)
         return carry
 
     loop(group - 1, store_rims, 0, 16 if direct else 1)
@@ -569,7 +569,7 @@
             to_early = low & (source > me)
             near_early = near_early + jnp.where(to_early, third, zero)
             near_late = near_late + jnp.where(to_early, zero, third)
-            if flip & (flip + 1) == 0:
+            if flip == group - 1:
                 rim_scr[source] = joined(message[after + 16 :])
         return near_early, near_late, far_early + early, far_late + jnp.where(low, second, zero)
 
@@ -588,7 +588,7 @@
     pair = jnp.concatenate(split_bits(sums), axis=0)
     half_sums_ref[...] = joined(pair)
     far_ref[rows : rows + 16] = pair
-    far_ref[rows + 16 :] = received[group - 1][rows + 16 :]
+    far_ref[rows + 16 :] = received[group - 1][(rows if not direct else 3 * span) + 16 :]
 
 
 def save_kernel(source_ref, target_hbm, sem):
@@ -614,7 +614,7 @@
     span = dk_ref.shape[1]
     me = lax.axis_index("ctx")
     low = me < group
-    received = Slots((None,) * (group - 1) + received_refs if direct else received_refs, me)
+    received = Slots((None,) + received_refs if direct else received_refs, me)
     starts = doc_starts(lengths_ref)
     blocks = 2 * ctx_count
     neighbours = [jnp.minimum(me + 1, ctx_count - 1), jnp.maximum(me - 1, 0)]
@@ -626,15 +626,14 @@
         source = partner(me, flip)
         message = received[flip]
         terms = message[:span].astype(f32)
-        if not direct or flip & (flip + 1) == 0:
-            rim_scr[source] = joined(message[span:])
+        rim_scr[source] = joined(message[span:])
         to_early = low & (source > me)
         zero = jnp.zeros_like(terms)
         return carry[0] + jnp.where(to_early, terms, zero), carry[1] + jnp.where(to_early, zero, terms)
 
     total = near_ref[...] + far_ref[: 2 * span].astype(f32)
     total = (total[:span], total[span:])
-    total = add(group - 2, total) if direct else loop(group - 1, add, total, 1)
+    total = add(0, total) if direct else loop(group - 1, add, total, 1)
     for half in range(2):
         dk_ref[half] = total[half][:, :LANES]
         dv_ref[half] = total[half][:, LANES:]
@@ -733,7 +732,7 @@
         first_shapes = []
         for flip in flips:
             rows = (2 if splits(direct, flip, group) else 3) * span + 16
-            rows += 16 if flip == group - 1 or flip & (flip + 1) == 0 else 0
+            rows += 16 if flip == group - 1 else 0
             first_shapes.append((rows, 2 * LANES))
         late_shapes = [(span + 16, 2 * LANES)]
     else:
@@ -820,7 +819,7 @@
     )(own_near, own_far, *half_terms)
     from_half = flipped(far, group)
     late_terms = sent[len(first_shapes) :]
-    late_terms = [flipped(late_terms[0], group - 1)] if direct else delivered(late_terms)
+    late_terms = [flipped(late_terms[0], 1)] if direct else delivered(late_terms)
 
     sums = pl.pallas_call(
         functools.partial(sums_kernel, span),

time: 38.5 us -> 37.4 us (0.971); the launches traced: 38.7 us -> 37 us
  waiting for transfers between devices: 7.77 us -> 6.28 us
  Pallas kernels: 8.16 us -> 7.55 us
    ppermute x12, waiting for transfers between devices: 7.23 us -> 5.74 us  [flipped(): return lax.ppermute(array, 'ctx', [(i, i ^ flip) for i in range(ctx_count)])]
    pallas_call x1, Pallas kernels: 3.17 us -> 2.56 us  [shards(): pl.pallas_call(functools.partial(grads_kernel, ctx_count, direct), out_sh...]
  transfers between devices with their start and end apart: 15 -> 15, of which waited for: 6 -> 6; matrix products, arithmetic and copies ran while one was open for 0% -> 0% of each run, Pallas kernels for 10% -> 11%
where the time goes in v7:
time: 37.4 us; the launch traced here: 37 us
  starting transfers between devices  21.8 us (58%)
  Pallas kernels  7.55 us (20%)
  waiting for transfers between devices  6.28 us (17%)
  between operations  0.73 us (2%)
  other arithmetic  0.6 us (2%)
    ppermute x12, starting transfers between devices, flipped(): return lax.ppermute(array, 'ctx', [(i, i ^ flip) for i in range(ctx_count)])  20 us
    ppermute x12, waiting for transfers between devices, flipped(): return lax.ppermute(array, 'ctx', [(i, i ^ flip) for i in range(ctx_count)])  5.74 us
    pallas_call x1, Pallas kernels, shards(): pl.pallas_call(functools.partial(grads_kernel, ctx_count, direct), out_sh...  2.56 us
    pallas_call x1, Pallas kernels, shards(): pl.pallas_call(functools.partial(prep_kernel, ctx_count, direct), out_sha...  1.87 us
    ppermute x3, starting transfers between devices, shards(): lax.ppermute(sums, 'tp', [(i, i ^ flip) for i in range(count)])  1.86 us
    pallas_call x1, Pallas kernels, shards(): pl.pallas_call(functools.partial(finish_kernel, ctx_count, direct), out_s...  1.27 us
    pallas_call x1, Pallas kernels, shards(): pl.pallas_call(pack_kernel, out_shape=jax.ShapeDtypeStruct((msg_rows, 2 *...  0.93 us
    pallas_call x1, Pallas kernels, shards(): pl.pallas_call(save_kernel, out_shape=jax.ShapeDtypeStruct(q_pre.shape, f...  0.8 us
  transfers between devices with their start and end apart: 15, of which 6 were waited for; matrix products, arithmetic and copies ran while one was open for 0% of the time, Pallas kernels for 11%

profile of v7, /device:TPU:0, one launch (start us, length us, event | category | flops | bytes accessed | tf_op | source)
XLA Modules:
  0.0 37.0 jit_solution(5381718368593017900)
XLA Ops:
  0.6 0.0 copy-start.1
  0.6 0.0 copy-start
  0.7 0.9 %pack.1.own_ref.refs_5_ = bf16[144,256]{1,0:T(8,128)(2,1)S(1)} custom-call(bf16[2,64,128]{2,1,0:T(8,128)(2,1)} %k_hbm.1, bf16[2,64,128]{2,1,0:T(8,128)(2,1)} %v_hbm.1, bf16[2,64,1024]{2,1,0:T(8,128)(2,1)} %q_hbm.3), custom_call_target="tpu_custom_call" | custom-call | tf_op jit(solution)/shard_map/pack/pallas_call | solution.py:710
  1.6 4.1 %collective-permute-start.3 = (bf16[144,256]{1,0:T(8,128)(2,1)S(1)}, bf16[144,256]{1,0:T(8,128)(2,1)S(1)}, u32[]{:S(2)}, u32[]{:S(2)}) collective-permute-start(bf16[144,256]{1,0:T(8,128)(2,1)S(1)} %pack.1.own_ref.refs_5_), channel_id=1, source_target_pairs={{0,16},{4,20},{8,24},{12,28},{16,0},{20,4},{24,8},{28,12},{1,17},{... | collective-permute-start | bytes 221192 | tf_op jit(solution)/shard_map/ppermute | solution.py:698
  5.7 2.5 %collective-permute-start.2 = (bf16[144,256]{1,0:T(8,128)(2,1)S(1)}, bf16[144,256]{1,0:T(8,128)(2,1)S(1)}, u32[]{:S(2)}, u32[]{:S(2)}) collective-permute-start(bf16[144,256]{1,0:T(8,128)(2,1)S(1)} %pack.1.own_ref.refs_5_), channel_id=1, source_target_pairs={{0,12},{4,8},{8,4},{12,0},{16,28},{20,24},{24,20},{28,16},{1,13},{... | collective-permute-start | bytes 221192 | tf_op jit(solution)/shard_map/ppermute | solution.py:698
  8.2 0.4 %collective-permute-start.1 = (bf16[144,256]{1,0:T(8,128)(2,1)S(1)}, bf16[144,256]{1,0:T(8,128)(2,1)S(1)}, u32[]{:S(2)}, u32[]{:S(2)}) collective-permute-start(bf16[144,256]{1,0:T(8,128)(2,1)S(1)} %pack.1.own_ref.refs_5_), channel_id=1, source_target_pairs={{0,8},{4,12},{8,0},{12,4},{16,24},{20,28},{24,16},{28,20},{1,9},{5... | collective-permute-start | bytes 221192 | tf_op jit(solution)/shard_map/ppermute | solution.py:698
  8.6 0.5 %collective-permute-start = (bf16[144,256]{1,0:T(8,128)(2,1)S(1)}, bf16[144,256]{1,0:T(8,128)(2,1)S(1)}, u32[]{:S(2)}, u32[]{:S(2)}) collective-permute-start(bf16[144,256]{1,0:T(8,128)(2,1)S(1)} %pack.1.own_ref.refs_5_), channel_id=1, source_target_pairs={{0,4},{4,0},{8,12},{12,8},{16,20},{20,16},{24,28},{28,24},{1,5},{5... | collective-permute-start | bytes 221192 | tf_op jit(solution)/shard_map/ppermute | solution.py:698
  9.2 0.0 collective-permute-done.3.refs_6_
  9.2 2.5 %collective-permute-start.6 = (bf16[144,256]{1,0:T(8,128)(2,1)S(1)}, bf16[144,256]{1,0:T(8,128)(2,1)S(1)}, u32[]{:S(2)}, u32[]{:S(2)}) collective-permute-start(bf16[144,256]{1,0:T(8,128)(2,1)S(1)} %collective-permute-done.3.refs_6_), channel_id=1, source_target_pairs={{0,12},{4,8},{8,4},{12,0},{16,28},{20,24},{24,20},{28,16},{1,13},{... | collective-permute-start | bytes 221192 | tf_op jit(solution)/shard_map/ppermute | solution.py:698
  11.7 0.7 %collective-permute-start.5 = (bf16[144,256]{1,0:T(8,128)(2,1)S(1)}, bf16[144,256]{1,0:T(8,128)(2,1)S(1)}, u32[]{:S(2)}, u32[]{:S(2)}) collective-permute-start(bf16[144,256]{1,0:T(8,128)(2,1)S(1)} %collective-permute-done.3.refs_6_), channel_id=1, source_target_pairs={{0,8},{4,12},{8,0},{12,4},{16,24},{20,28},{24,16},{28,20},{1,9},{5... | collective-permute-start | bytes 221192 | tf_op jit(solution)/shard_map/ppermute | solution.py:698
  12.4 0.0 collective-permute-done.2.refs_2_.refs_9_
  12.4 0.9 %collective-permute-start.4 = (bf16[144,256]{1,0:T(8,128)(2,1)S(1)}, bf16[144,256]{1,0:T(8,128)(2,1)S(1)}, u32[]{:S(2)}, u32[]{:S(2)}) collective-permute-start(bf16[144,256]{1,0:T(8,128)(2,1)S(1)} %collective-permute-done.3.refs_6_), channel_id=1, source_target_pairs={{0,4},{4,0},{8,12},{12,8},{16,20},{20,16},{24,28},{28,24},{1,5},{5... | collective-permute-start | bytes 221192 | tf_op jit(solution)/shard_map/ppermute | solution.py:698
  13.3 0.1 collective-permute-done.1.refs_1_.refs_8_
  13.4 0.9 %collective-permute-done.refs_0_.refs_7_ = bf16[144,256]{1,0:T(8,128)(2,1)S(1)} collective-permute-done((bf16[144,256]{1,0:T(8,128)(2,1)S(1)}, bf16[144,256]{1,0:T(8,128)(2,1)S(1)}, u32[]{:S(2)}, u32[]{:S(2)}) %collective-permute-start) | collective-permute-done | bytes 73760 | tf_op jit(solution)/shard_map/ppermute | solution.py:698
  14.3 0.0 copy-done.1
  14.3 0.0 copy-done
  14.3 1.9 %prep.1 = (f32[1040,128]{1,0:T(8,128)S(1)}, f32[1040,128]{1,0:T(8,128)S(1)}, f32[2,8,72,128]{3,2,1,0:T(8,128)S(1)}, bf16[2,512,128]{2,1,0:T(8,128)(2,1)S(1)}, bf16[2,512,128]{2,1,0:T(8,128)(2,1)S(1)}) custom-call(s32[8]{0:T(128)S(1)} %copy-done.1, f32[3,3,128]{2,1,0:T(4,128)S(1)} %copy-done, bf16[2,64,1024]{2,1,0:T(8,128)(2,1)} %q_hbm.3, ...), custom_call_target="tpu_custom_call" | custom-call | tf_op jit(solution)/shard_map/prep/pallas_call | solution.py:745
  16.2 0.0 collective-permute-done.6.refs_12_
  16.2 0.0 collective-permute-done.5.refs_11_
  16.2 0.5 %collective-permute-done.4.refs_10_ = bf16[144,256]{1,0:T(8,128)(2,1)S(1)} collective-permute-done((bf16[144,256]{1,0:T(8,128)(2,1)S(1)}, bf16[144,256]{1,0:T(8,128)(2,1)S(1)}, u32[]{:S(2)}, u32[]{:S(2)}) %collective-permute-start.4) | collective-permute-done | bytes 73760 | tf_op jit(solution)/shard_map/ppermute | solution.py:698
  16.8 2.6 %grads.1 = (f32[2,64,1024]{2,1,0:T(8,128)S(1)}, f32[2,8,1024]{2,1,0:T(8,128)S(1)}, f32[128,256]{1,0:T(8,128)S(1)}, f32[136,256]{1,0:T(8,128)S(1)}, bf16[144,256]...) custom-call(s32[8]{0:T(128)S(1)} %copy-done.1, ...), custom_call_target="tpu_custom_call" | custom-call | tf_op jit(solution)/shard_map/grads/pallas_call | solution.py:780
  19.3 2.1 %collective-permute-start.9 = (bf16[224,256]{1,0:T(8,128)(2,1)S(1)}, bf16[224,256]{1,0:T(8,128)(2,1)S(1)}, u32[]{:S(2)}, u32[]{:S(2)}) collective-permute-start(bf16[224,256]{1,0:T(8,128)(2,1)S(1)} %get-tuple-element.36), channel_id=1, source_target_pairs={{0,12},{4,8},{8,4},{12,0},{16,28},{20,24},{24,20},{28,16},{1,13},{... | collective-permute-start | bytes 344072 | tf_op jit(solution)/shard_map/ppermute | solution.py:698
  21.4 1.0 %collective-permute-start.8 = (bf16[208,256]{1,0:T(8,128)(2,1)S(1)}, bf16[208,256]{1,0:T(8,128)(2,1)S(1)}, u32[]{:S(2)}, u32[]{:S(2)}) collective-permute-start(bf16[208,256]{1,0:T(8,128)(2,1)S(1)} %get-tuple-element.35), channel_id=1, source_target_pairs={{0,8},{4,12},{8,0},{12,4},{16,24},{20,28},{24,16},{28,20},{1,9},{5... | collective-permute-start | bytes 319496 | tf_op jit(solution)/shard_map/ppermute | solution.py:698
  22.4 0.4 %collective-permute-start.7 = (bf16[144,256]{1,0:T(8,128)(2,1)S(1)}, bf16[144,256]{1,0:T(8,128)(2,1)S(1)}, u32[]{:S(2)}, u32[]{:S(2)}) collective-permute-start(bf16[144,256]{1,0:T(8,128)(2,1)S(1)} %get-tuple-element.34), channel_id=1, source_target_pairs={{0,4},{4,0},{8,12},{12,8},{16,20},{20,16},{24,28},{28,24},{1,5},{5... | collective-permute-start | bytes 221192 | tf_op jit(solution)/shard_map/ppermute | solution.py:698
  22.9 0.8 %save.1.dq_in_hbm = f32[2,64,1024]{2,1,0:T(8,128)} custom-call(f32[2,64,1024]{2,1,0:T(8,128)S(1)} %get-tuple-element.33.source_ref), custom_call_target="tpu_custom_call" | custom-call | tf_op jit(solution)/shard_map/save/pallas_call | solution.py:791
  23.7 3.1 %collective-permute-done.7.refs_0_ = bf16[144,256]{1,0:T(8,128)(2,1)S(1)} collective-permute-done((bf16[144,256]{1,0:T(8,128)(2,1)S(1)}, bf16[144,256]{1,0:T(8,128)(2,1)S(1)}, u32[]{:S(2)}, u32[]{:S(2)}) %collective-permute-start.7) | collective-permute-done | bytes 73760 | tf_op jit(solution)/shard_map/ppermute | solution.py:698
  26.8 0.0 collective-permute-done.8.refs_1_
  26.8 0.0 collective-permute-done.9.refs_2_
  26.8 0.1 merge.1
  26.9 3.3 %collective-permute-start.10 = (bf16[160,256]{1,0:T(8,128)(2,1)S(1)}, bf16[160,256]{1,0:T(8,128)(2,1)S(1)}, u32[]{:S(2)}, u32[]{:S(2)}) collective-permute-start(bf16[160,256]{1,0:T(8,128)(2,1)S(1)} %get-tuple-element.45), channel_id=1, source_target_pairs={{0,16},{4,20},{8,24},{12,28},{16,0},{20,4},{24,8},{28,12},{1,17},{... | collective-permute-start | bytes 245768 | tf_op jit(solution)/shard_map/ppermute | solution.py:698
  30.3 1.3 %collective-permute-start.11 = (bf16[80,256]{1,0:T(8,128)(2,1)S(1)}, bf16[80,256]{1,0:T(8,128)(2,1)S(1)}, u32[]{:S(2)}, u32[]{:S(2)}) collective-permute-start(bf16[80,256]{1,0:T(8,128)(2,1)S(1)} %get-tuple-element.47), channel_id=1, source_target_pairs={{0,4},{4,0},{8,12},{12,8},{16,20},{20,16},{24,28},{28,24},{1,5},{5... | collective-permute-start | bytes 122888 | tf_op jit(solution)/shard_map/ppermute | solution.py:698
  31.6 1.1 %collective-permute-done.10.far_ref = bf16[160,256]{1,0:T(8,128)(2,1)S(1)} collective-permute-done((bf16[160,256]{1,0:T(8,128)(2,1)S(1)}, bf16[160,256]{1,0:T(8,128)(2,1)S(1)}, u32[]{:S(2)}, u32[]{:S(2)}) %collective-permute-start.10) | collective-permute-done | bytes 81952 | tf_op jit(solution)/shard_map/ppermute | solution.py:698
  32.7 0.0 collective-permute-start.14
  32.7 1.6 %collective-permute-start.13 = (f32[3,3,128]{2,1,0:T(4,128)S(1)}, f32[3,3,128]{2,1,0:T(4,128)S(1)}, u32[]{:S(2)}, u32[]{:S(2)}) collective-permute-start(f32[3,3,128]{2,1,0:T(4,128)S(1)} %sums.1), channel_id=1, source_target_pairs={{0,2},{1,3},{2,0},{3,1},{4,6},{5,7},{6,4},{7,5},{8,10},{9,11},{10,... | collective-permute-start | bytes 13832 | tf_op jit(solution)/shard_map/ppermute | solution.py:834
  34.3 0.3 collective-permute-start.12
  34.6 0.0 collective-permute-done.11.refs_0_
  34.6 1.3 %finish.1 = (f32[2,64,1024]{2,1,0:T(8,128)}, f32[2,64,128]{2,1,0:T(8,128)}, f32[2,64,128]{2,1,0:T(8,128)}) custom-call(s32[8]{0:T(128)S(1)} %copy-done.1, f32[3,3,128]{2,1,0:T(4,128)S(1)} %copy-done, f32[2,64,1024]{2,1,0:T(8,128)} %save.1.dq_in_hbm, f32[2,8,1024]{2,1,0:T(8,128)S(1)} %get-tuple-element.38.tail_ref, ...), custom_call_target="tpu_custom_call", output_to_operand_aliasing={{0}: (2, {})} | custom-call | tf_op jit(solution)/shard_map/finish/pallas_call | solution.py:836
  35.8 0.0 collective-permute-done.14
  35.8 0.5 %collective-permute-done.13 = f32[3,3,128]{2,1,0:T(4,128)S(1)} collective-permute-done((f32[3,3,128]{2,1,0:T(4,128)S(1)}, f32[3,3,128]{2,1,0:T(4,128)S(1)}, u32[]{:S(2)}, u32[]{:S(2)}) %collective-permute-start.13) | collective-permute-done | bytes 4640 | tf_op jit(solution)/shard_map/ppermute | solution.py:834
  36.4 0.0 collective-permute-done.12
  36.4 0.6 %add_add_fusion = f32[3,3,128]{2,1,0:T(4,128)} fusion(f32[3,3,128]{2,1,0:T(4,128)S(1)} %collective-permute-done.13, f32[3,3,128]{2,1,0:T(4,128)S(1)} %collective-permute-done.14, f32[3,3,128]{2,1,0:T(4,128)S(1)} %sums.1, f32[3,3,128]{2,1,0:T(4,128)S(1)} %collective-permute-done.12), kind=kLoop, calls=%fused_computation | loop fusion | flops 3456 | bytes 23040 | tf_op jit(solution)/shard_map/add | solution.py:857
  (1 shorter events, 0.0 us)
Async XLA Ops:
  0.6 13.7 %copy-start.1 = (s32[8]{0:T(128)S(1)}, s32[8]{0:T(128)}, u32[]{:S(2)}) copy-start(s32[8]{0:T(128)} %lengths_ref.5) | copy-start | bytes 100
  0.6 13.7 %copy-start = (f32[3,3,128]{2,1,0:T(4,128)S(1)}, f32[3,3,128]{2,1,0:T(4,128)}, u32[]{:S(2)}) copy-start(f32[3,3,128]{2,1,0:T(4,128)} %filters_ref.5) | copy-start | bytes 13828
  1.6 7.6 %collective-permute-start.3 = (bf16[144,256]{1,0:T(8,128)(2,1)S(1)}, bf16[144,256]{1,0:T(8,128)(2,1)S(1)}, u32[]{:S(2)}, u32[]{:S(2)}) collective-permute-start(bf16[144,256]{1,0:T(8,128)(2,1)S(1)} %pack.1.own_ref.refs_5_), channel_id=1, source_target_pairs={{0,16},{4,20},{8,24},{12,28},{16,0},{20,4},{24,8},{28,12},{1,17},{... | collective-permute-start | bytes 221192 | tf_op jit(solution)/shard_map/ppermute | solution.py:698
  5.7 6.7 %collective-permute-start.2 = (bf16[144,256]{1,0:T(8,128)(2,1)S(1)}, bf16[144,256]{1,0:T(8,128)(2,1)S(1)}, u32[]{:S(2)}, u32[]{:S(2)}) collective-permute-start(bf16[144,256]{1,0:T(8,128)(2,1)S(1)} %pack.1.own_ref.refs_5_), channel_id=1, source_target_pairs={{0,12},{4,8},{8,4},{12,0},{16,28},{20,24},{24,20},{28,16},{1,13},{... | collective-permute-start | bytes 221192 | tf_op jit(solution)/shard_map/ppermute | solution.py:698
  8.2 5.2 %collective-permute-start.1 = (bf16[144,256]{1,0:T(8,128)(2,1)S(1)}, bf16[144,256]{1,0:T(8,128)(2,1)S(1)}, u32[]{:S(2)}, u32[]{:S(2)}) collective-permute-start(bf16[144,256]{1,0:T(8,128)(2,1)S(1)} %pack.1.own_ref.refs_5_), channel_id=1, source_target_pairs={{0,8},{4,12},{8,0},{12,4},{16,24},{20,28},{24,16},{28,20},{1,9},{5... | collective-permute-start | bytes 221192 | tf_op jit(solution)/shard_map/ppermute | solution.py:698
  8.6 5.7 %collective-permute-start = (bf16[144,256]{1,0:T(8,128)(2,1)S(1)}, bf16[144,256]{1,0:T(8,128)(2,1)S(1)}, u32[]{:S(2)}, u32[]{:S(2)}) collective-permute-start(bf16[144,256]{1,0:T(8,128)(2,1)S(1)} %pack.1.own_ref.refs_5_), channel_id=1, source_target_pairs={{0,4},{4,0},{8,12},{12,8},{16,20},{20,16},{24,28},{28,24},{1,5},{5... | collective-permute-start | bytes 221192 | tf_op jit(solution)/shard_map/ppermute | solution.py:698
  9.2 7.0 %collective-permute-start.6 = (bf16[144,256]{1,0:T(8,128)(2,1)S(1)}, bf16[144,256]{1,0:T(8,128)(2,1)S(1)}, u32[]{:S(2)}, u32[]{:S(2)}) collective-permute-start(bf16[144,256]{1,0:T(8,128)(2,1)S(1)} %collective-permute-done.3.refs_6_), channel_id=1, source_target_pairs={{0,12},{4,8},{8,4},{12,0},{16,28},{20,24},{24,20},{28,16},{1,13},{... | collective-permute-start | bytes 221192 | tf_op jit(solution)/shard_map/ppermute | solution.py:698
  11.7 4.5 %collective-permute-start.5 = (bf16[144,256]{1,0:T(8,128)(2,1)S(1)}, bf16[144,256]{1,0:T(8,128)(2,1)S(1)}, u32[]{:S(2)}, u32[]{:S(2)}) collective-permute-start(bf16[144,256]{1,0:T(8,128)(2,1)S(1)} %collective-permute-done.3.refs_6_), channel_id=1, source_target_pairs={{0,8},{4,12},{8,0},{12,4},{16,24},{20,28},{24,16},{28,20},{1,9},{5... | collective-permute-start | bytes 221192 | tf_op jit(solution)/shard_map/ppermute | solution.py:698
  12.4 4.4 %collective-permute-start.4 = (bf16[144,256]{1,0:T(8,128)(2,1)S(1)}, bf16[144,256]{1,0:T(8,128)(2,1)S(1)}, u32[]{:S(2)}, u32[]{:S(2)}) collective-permute-start(bf16[144,256]{1,0:T(8,128)(2,1)S(1)} %collective-permute-done.3.refs_6_), channel_id=1, source_target_pairs={{0,4},{4,0},{8,12},{12,8},{16,20},{20,16},{24,28},{28,24},{1,5},{5... | collective-permute-start | bytes 221192 | tf_op jit(solution)/shard_map/ppermute | solution.py:698
  19.3 7.5 %collective-permute-start.9 = (bf16[224,256]{1,0:T(8,128)(2,1)S(1)}, bf16[224,256]{1,0:T(8,128)(2,1)S(1)}, u32[]{:S(2)}, u32[]{:S(2)}) collective-permute-start(bf16[224,256]{1,0:T(8,128)(2,1)S(1)} %get-tuple-element.36), channel_id=1, source_target_pairs={{0,12},{4,8},{8,4},{12,0},{16,28},{20,24},{24,20},{28,16},{1,13},{... | collective-permute-start | bytes 344072 | tf_op jit(solution)/shard_map/ppermute | solution.py:698
  21.4 5.4 %collective-permute-start.8 = (bf16[208,256]{1,0:T(8,128)(2,1)S(1)}, bf16[208,256]{1,0:T(8,128)(2,1)S(1)}, u32[]{:S(2)}, u32[]{:S(2)}) collective-permute-start(bf16[208,256]{1,0:T(8,128)(2,1)S(1)} %get-tuple-element.35), channel_id=1, source_target_pairs={{0,8},{4,12},{8,0},{12,4},{16,24},{20,28},{24,16},{28,20},{1,9},{5... | collective-permute-start | bytes 319496 | tf_op jit(solution)/shard_map/ppermute | solution.py:698
  22.4 4.4 %collective-permute-start.7 = (bf16[144,256]{1,0:T(8,128)(2,1)S(1)}, bf16[144,256]{1,0:T(8,128)(2,1)S(1)}, u32[]{:S(2)}, u32[]{:S(2)}) collective-permute-start(bf16[144,256]{1,0:T(8,128)(2,1)S(1)} %get-tuple-element.34), channel_id=1, source_target_pairs={{0,4},{4,0},{8,12},{12,8},{16,20},{20,16},{24,28},{28,24},{1,5},{5... | collective-permute-start | bytes 221192 | tf_op jit(solution)/shard_map/ppermute | solution.py:698
  26.9 5.8 %collective-permute-start.10 = (bf16[160,256]{1,0:T(8,128)(2,1)S(1)}, bf16[160,256]{1,0:T(8,128)(2,1)S(1)}, u32[]{:S(2)}, u32[]{:S(2)}) collective-permute-start(bf16[160,256]{1,0:T(8,128)(2,1)S(1)} %get-tuple-element.45), channel_id=1, source_target_pairs={{0,16},{4,20},{8,24},{12,28},{16,0},{20,4},{24,8},{28,12},{1,17},{... | collective-permute-start | bytes 245768 | tf_op jit(solution)/shard_map/ppermute | solution.py:698
  30.3 4.3 %collective-permute-start.11 = (bf16[80,256]{1,0:T(8,128)(2,1)S(1)}, bf16[80,256]{1,0:T(8,128)(2,1)S(1)}, u32[]{:S(2)}, u32[]{:S(2)}) collective-permute-start(bf16[80,256]{1,0:T(8,128)(2,1)S(1)} %get-tuple-element.47), channel_id=1, source_target_pairs={{0,4},{4,0},{8,12},{12,8},{16,20},{20,16},{24,28},{28,24},{1,5},{5... | collective-permute-start | bytes 122888 | tf_op jit(solution)/shard_map/ppermute | solution.py:698
  32.7 3.1 %collective-permute-start.14 = (f32[3,3,128]{2,1,0:T(4,128)S(1)}, f32[3,3,128]{2,1,0:T(4,128)S(1)}, u32[]{:S(2)}, u32[]{:S(2)}) collective-permute-start(f32[3,3,128]{2,1,0:T(4,128)S(1)} %sums.1), channel_id=1, source_target_pairs={{0,3},{1,2},{2,1},{3,0},{4,7},{5,6},{6,5},{7,4},{8,11},{9,10},{10,... | collective-permute-start | bytes 13832 | tf_op jit(solution)/shard_map/ppermute | solution.py:834
  32.7 3.7 %collective-permute-start.13 = (f32[3,3,128]{2,1,0:T(4,128)S(1)}, f32[3,3,128]{2,1,0:T(4,128)S(1)}, u32[]{:S(2)}, u32[]{:S(2)}) collective-permute-start(f32[3,3,128]{2,1,0:T(4,128)S(1)} %sums.1), channel_id=1, source_target_pairs={{0,2},{1,3},{2,0},{3,1},{4,6},{5,7},{6,4},{7,5},{8,10},{9,11},{10,... | collective-permute-start | bytes 13832 | tf_op jit(solution)/shard_map/ppermute | solution.py:834
  34.3 2.1 %collective-permute-start.12 = (f32[3,3,128]{2,1,0:T(4,128)S(1)}, f32[3,3,128]{2,1,0:T(4,128)S(1)}, u32[]{:S(2)}, u32[]{:S(2)}) collective-permute-start(f32[3,3,128]{2,1,0:T(4,128)S(1)} %sums.1), channel_id=1, source_target_pairs={{0,1},{1,0},{2,3},{3,2},{4,5},{5,4},{6,7},{7,6},{8,9},{9,8},{10,11... | collective-permute-start | bytes 13832 | tf_op jit(solution)/shard_map/ppermute | solution.py:834
